TPU v7x, 32 devices: a whole 2x2x4 slice. The times are simulated.
32 devices in a mesh: groups: 2 (over y), hid: 4 (over z), dp: 2 (over x), col: 2 (over core).
Axes of the slice: x: 2, y: 2, z: 4, core: 2. Of those that a mesh axis runs over, the one named last changes fastest.
Arguments:
- tokens: bfloat16 [512, 4096], P(('groups', 'hid', 'dp'), 'col'), parts along dimension 0, may hold values from -6 to 6
- target: bfloat16 [512, 4096], P(('groups', 'hid', 'dp'), 'col'), parts along dimension 0, may hold values from -6 to 6
- gate_panel: bfloat16 [8, 2, 64, 40960], P(('groups', 'hid'), 'col'), parts along dimension 0, may hold values from -0.1875 to 0.1875
- up_panel: bfloat16 [8, 2, 64, 40960], P(('groups', 'hid'), 'col'), parts along dimension 0, may hold values from -0.1875 to 0.1875
- down_panel: bfloat16 [8, 2, 64, 40960], P(('groups', 'hid'), 'col'), parts along dimension 0, may hold values from -0.09375 to 0.09375
- gate_list: int32 [8, 2, 640], P(('groups', 'hid'), 'col'), parts along dimension 0, may hold values from 0 to 2048, as said below
- up_list: int32 [8, 2, 640], P(('groups', 'hid'), 'col'), parts along dimension 0, may hold values from 0 to 2048, as said below
- down_list: int32 [8, 2, 640], P(('groups', 'hid'), 'col'), parts along dimension 0, may hold values from 0 to 2048, as said below
Outputs:
- gate_grad: bfloat16 [8, 2, 64, 40960], P(('groups', 'hid'), 'col', None, 'dp'), parts along dimension 0
- up_grad: bfloat16 [8, 2, 64, 40960], P(('groups', 'hid'), 'col', None, 'dp'), parts along dimension 0
- down_grad: bfloat16 [8, 2, 64, 40960], P(('groups', 'hid'), 'col', None, 'dp'), parts along dimension 0
There are 2 independent parts, one for each index of `groups`. A program takes and returns all parts, laid end to end along the dimension named above; each array names one. Nothing has to cross between parts.
Inputs may be any that keep to these rules, and one draw needn't show every extreme that they name: `gate_list`: in each list[h, c] the entries below 2048 are distinct and fill the first slots; the rest equal 2048. Each list[h, c] has between 384 and 640 entries below 2048, and some list[h, c] has exactly 640. `up_list`: as for gate_list. `down_list`: as for gate_list.
All inputs are finite; a program needn't handle non-finite values.
Results may differ from a plain program's by a relative error of at most 0.0069.
Values may be sent and summed in bfloat16 or wider, within the bound.
No kernel may reach another device: no remote copies, remote signals or barrier semaphores. Data moves between devices by JAX's collectives and lax.ppermute only.
A program may use at most 384 MiB of HBM per device.

v0:
```python
import jax
import jax.numpy as jnp
from jax import lax
from jax.sharding import PartitionSpec as P

D = 4096
FF = 16384
BLK = 64


SLOPE_SCALE = 0.0625


def slot_blocks(slot_panel, block_size):
    cap_slots = slot_panel.shape[-1] // block_size
    return slot_panel.reshape(block_size, cap_slots, block_size).transpose(1, 0, 2)


def to_panel(slot_terms):
    cap_slots = slot_terms.shape[0]
    block_size = slot_terms.shape[1]
    return slot_terms.transpose(1, 0, 2).reshape(block_size, cap_slots * block_size)


def densify(slot_panel, block_ids, shape_info, rows_are_hidden):
    block_size, grid_size, row_blocks, slab_blocks = shape_info
    blocks = slot_blocks(slot_panel, block_size).reshape(
        block_ids.shape[0], block_size * block_size
    )
    onehot = (
        lax.broadcasted_iota(jnp.int32, (grid_size, block_ids.shape[0]), 0) == block_ids[None, :]
    ).astype(jnp.bfloat16)
    placed = jnp.dot(onehot, blocks, preferred_element_type=jnp.bfloat16)
    placed = placed.reshape(row_blocks, slab_blocks, block_size, block_size)
    if rows_are_hidden:
        return placed.transpose(1, 2, 0, 3).reshape(
            slab_blocks * block_size, row_blocks * block_size
        )
    return placed.transpose(0, 2, 1, 3).reshape(row_blocks * block_size, slab_blocks * block_size)


def extract(dense_grad, block_ids, shape_info, rows_are_hidden):
    block_size, grid_size, row_blocks, slab_blocks = shape_info
    in_use = block_ids < grid_size
    clipped = jnp.minimum(block_ids, grid_size - 1)
    row_index = clipped // slab_blocks
    slab_index = clipped % slab_blocks
    if rows_are_hidden:
        tiles = dense_grad.reshape(slab_blocks, block_size, row_blocks, block_size)
        picked = tiles[slab_index, :, row_index, :]
    else:
        tiles = dense_grad.reshape(row_blocks, block_size, slab_blocks, block_size)
        picked = tiles[row_index, :, slab_index, :]
    picked = picked * in_use[:, None, None].astype(jnp.float32)
    return to_panel(picked)


def prepare(slot_panel, block_ids, shape_info, rows_are_hidden):
    return (densify(slot_panel, block_ids, shape_info, rows_are_hidden), block_ids)


def project_up(plan, picked):
    return jnp.dot(picked, plan[0], preferred_element_type=jnp.float32)


def project_down(plan, picked):
    return jnp.dot(picked, plan[0], preferred_element_type=jnp.float32)


def project_back(plan, picked):
    return lax.dot_general(
        picked, plan[0], (((1,), (1,)), ((), ())), preferred_element_type=jnp.float32
    )


def grad_inward(plan, picked_in, delta_rows, shape_info):
    dense_grad = lax.dot_general(
        picked_in, delta_rows, (((0,), (0,)), ((), ())), preferred_element_type=jnp.float32
    )
    return extract(dense_grad, plan[1], shape_info, False)


def grad_outward(plan, picked_hidden, picked_slope, shape_info):
    dense_grad = lax.dot_general(
        picked_hidden, picked_slope, (((0,), (0,)), ((), ())), preferred_element_type=jnp.float32
    )
    return extract(dense_grad, plan[1], shape_info, True)


def local(tokens, target, gate_panel, up_panel, down_panel, gate_list, up_list, down_list):
    block_size = BLK
    slab_blocks = FF // block_size // lax.axis_size("hid")
    row_blocks = D // block_size // lax.axis_size("col")
    grid_size = slab_blocks * row_blocks
    shape_info = (block_size, grid_size, row_blocks, slab_blocks)
    gathered = lax.all_gather(tokens, "hid", axis=0, tiled=True)
    gate_plan = prepare(gate_panel[0, 0], gate_list[0, 0], shape_info, False)
    up_plan = prepare(up_panel[0, 0], up_list[0, 0], shape_info, False)
    down_plan = prepare(down_panel[0, 0], down_list[0, 0], shape_info, True)
    gate_sum, up_sum = lax.psum(
        (project_up(gate_plan, gathered), project_up(up_plan, gathered)), "col"
    )
    sigmoid_gate = jax.nn.sigmoid(gate_sum)
    silu_gate = gate_sum * sigmoid_gate
    hidden = (silu_gate * up_sum).astype(jnp.bfloat16)
    out_part = project_down(down_plan, hidden)
    own_output = lax.psum_scatter(out_part, "hid", scatter_dimension=0, tiled=True)
    own_slope = ((own_output - target.astype(jnp.float32)) * SLOPE_SCALE).astype(jnp.bfloat16)
    slope = lax.all_gather(own_slope, "hid", axis=0, tiled=True)
    back_sum = lax.psum(project_back(down_plan, slope), "col")
    gate_slope = (
        back_sum * up_sum * sigmoid_gate * (1.0 + gate_sum * (1.0 - sigmoid_gate))
    ).astype(jnp.bfloat16)
    up_slope = (back_sum * silu_gate).astype(jnp.bfloat16)
    gate_term = grad_inward(gate_plan, gathered, gate_slope, shape_info)
    up_term = grad_inward(up_plan, gathered, up_slope, shape_info)
    down_term = grad_outward(down_plan, hidden, slope, shape_info)
    gate_sum_grad, up_sum_grad, down_sum_grad = (
        lax.psum_scatter(
            gate_term[None, None].astype(jnp.bfloat16), "dp", scatter_dimension=3, tiled=True
        ).astype(jnp.float32),
        lax.psum_scatter(
            up_term[None, None].astype(jnp.bfloat16), "dp", scatter_dimension=3, tiled=True
        ).astype(jnp.float32),
        lax.psum_scatter(
            down_term[None, None].astype(jnp.bfloat16), "dp", scatter_dimension=3, tiled=True
        ).astype(jnp.float32),
    )
    return (
        gate_sum_grad.astype(jnp.bfloat16),
        up_sum_grad.astype(jnp.bfloat16),
        down_sum_grad.astype(jnp.bfloat16),
    )


def solution(mesh):
    return jax.shard_map(
        local,
        mesh=mesh,
        in_specs=(
            P(("groups", "hid", "dp"), "col"),
            P(("groups", "hid", "dp"), "col"),
            P(("groups", "hid"), "col", None, None),
            P(("groups", "hid"), "col", None, None),
            P(("groups", "hid"), "col", None, None),
            P(("groups", "hid"), "col", None),
            P(("groups", "hid"), "col", None),
            P(("groups", "hid"), "col", None),
        ),
        out_specs=(
            P(("groups", "hid"), "col", None, "dp"),
            P(("groups", "hid"), "col", None, "dp"),
            P(("groups", "hid"), "col", None, "dp"),
        ),
        check_vma=False,
    )
```

profile of v0, /device:TPU:1, one launch (start us, length us, event | category | flops | bytes accessed | tf_op | source)
XLA Modules:
  0.0 1108.4 jit_solution(14425879182745804738)
XLA Ops:
  7.2 15.5 %all_gather.6 = bf16[128,2048]{1,0:T(8,128)(2,1)S(1)} all-gather(bf16[32,2048]{1,0:T(8,128)(2,1)} %param.8), channel_id=1, replica_groups=mesh['groups'=2,'hid'=4,'dp'=2,'col'=2] {'hid'}, dimensions={0}, use_global_device_ids=true | all-gather | bytes 655360 | tf_op jit(solution)/shard_map/all_gather | solution.py:96
  22.7 13.3 %reshape_squeeze.9 = bf16[64,640,64]{2,1,0:T(8,128)(2,1)} reshape(bf16[1,1,64,40960]{3,2,1,0:T(8,128)(2,1)} %param.10) | data formatting | bytes 10485760 | tf_op jit(solution)/shard_map/reshape;squeeze | solution.py:16
  46.6 31.2 %convolution_bitcast_fusion.4 = bf16[32,64,64,64]{3,2,1,0:T(8,128)(2,1)} fusion(bf16[640,64,64]{0,2,1:T(8,128)(2,1)} %copy.14, s32[640]{0:T(1024)S(1)} %reduce, s32[32,64]{1,0:T(8,128)S(1)} %multiply_add_fusion), kind=kOutput, calls=%fused_computation.10 | convolution fusion | flops 10738728960 | bytes 22030848 | tf_op jit(solution)/shard_map/dot_general | solution.py:33
  77.8 44.1 %reshape.439 = bf16[2048,4096]{1,0:T(8,128)(2,1)} reshape(bf16[32,64,64,64]{3,2,1,0:T(8,128)(2,1)} %convolution_bitcast_fusion.4) | data formatting | bytes 33554432 | tf_op jit(solution)/shard_map/reshape | solution.py:39
  121.9 13.1 %reshape_squeeze.10 = bf16[64,640,64]{2,1,0:T(8,128)(2,1)} reshape(bf16[1,1,64,40960]{3,2,1,0:T(8,128)(2,1)} %param.11) | data formatting | bytes 10485760 | tf_op jit(solution)/shard_map/reshape;squeeze | solution.py:16
  145.4 31.2 %convolution_bitcast_fusion.3 = bf16[32,64,64,64]{3,2,1,0:T(8,128)(2,1)} fusion(bf16[640,64,64]{0,2,1:T(8,128)(2,1)} %copy.15, s32[640]{0:T(1024)S(1)} %reduce.1, s32[32,64]{1,0:T(8,128)S(1)} %multiply_add_fusion), kind=kOutput, calls=%fused_computation.9 | convolution fusion | flops 10738728960 | bytes 22030848 | tf_op jit(solution)/shard_map/dot_general | solution.py:33
  176.7 44.1 %reshape.441 = bf16[2048,4096]{1,0:T(8,128)(2,1)} reshape(bf16[32,64,64,64]{3,2,1,0:T(8,128)(2,1)} %convolution_bitcast_fusion.3) | data formatting | bytes 33554432 | tf_op jit(solution)/shard_map/reshape | solution.py:39
  238.3 13.4 %reshape_squeeze.11 = bf16[64,640,64]{2,1,0:T(8,128)(2,1)} reshape(bf16[1,1,64,40960]{3,2,1,0:T(8,128)(2,1)} %param.12) | data formatting | bytes 10485760 | tf_op jit(solution)/shard_map/reshape;squeeze | solution.py:16
  262.4 31.4 %convolution_bitcast_fusion.2 = bf16[64,64,32,64]{3,0,1,2:T(8,128)(2,1)} fusion(bf16[640,64,64]{0,2,1:T(8,128)(2,1)} %copy.16, s32[640]{0:T(1024)S(1)} %reduce.2, s32[32,64]{1,0:T(8,128)S(1)} %multiply_add_fusion), kind=kOutput, calls=%fused_computation.8 | convolution fusion | flops 10738728960 | bytes 22030848 | tf_op jit(solution)/shard_map/dot_general | solution.py:33
  293.9 29.5 %copy.17 = bf16[64,64,32,64]{3,2,1,0:T(8,128)(2,1)} copy(bf16[64,64,32,64]{3,0,1,2:T(8,128)(2,1)} %convolution_bitcast_fusion.2) | data formatting | bytes 33554432 | tf_op jit(solution)/shard_map/transpose | solution.py:36
  323.3 45.9 %reshape.443 = bf16[4096,2048]{1,0:T(8,128)(2,1)} reshape(bf16[64,64,32,64]{3,2,1,0:T(8,128)(2,1)} %copy.17) | data formatting | bytes 33554432 | tf_op jit(solution)/shard_map/reshape | solution.py:36
  381.3 30.4 %reduce-scatter.5.cloned.1.call-done = f32[32,2048]{1,0:T(8,128)} async-done(((f32[128,2048]{1,0:T(8,128)}), f32[32,2048]{1,0:T(8,128)}) %reduce-scatter.5.cloned.1.call-update) | async-done | bytes 262160 | tf_op jit(solution)/shard_map/reduce_scatter | solution.py:107
  412.7 12.1 %all_gather.7 = bf16[128,2048]{1,0:T(8,128)(2,1)S(1)} all-gather(bf16[32,2048]{1,0:T(8,128)(2,1)S(1)} %multiply_convert_fusion.8), channel_id=1, replica_groups=mesh['groups'=2,'hid'=4,'dp'=2,'col'=2] {'hid'}, dimensions={0}, use_global_device_ids=true | all-gather | bytes 655360 | tf_op jit(solution)/shard_map/all_gather | solution.py:109
  434.7 14.0 %fusion.43 = f32[4096,2048]{1,0:T(8,128)} fusion(bf16[128,4096]{0,1:T(8,128)(2,1)S(1)} %multiply_convert_fusion.5, bf16[128,2048]{1,0:T(8,128)(2,1)S(1)} %all_gather.7), kind=kOutput, calls=%fused_computation.88 | convolution fusion | flops 2147483648 | bytes 35127296 | tf_op jit(solution)/shard_map/dot_general | solution.py:84
  448.7 54.3 %reshape.446 = f32[64,64,32,64]{3,2,1,0:T(8,128)} reshape(f32[4096,2048]{1,0:T(8,128)} %fusion.43) | data formatting | bytes 67108864 | tf_op jit(solution)/shard_map/reshape | solution.py:49
  503.0 56.3 %copy.23 = f32[64,64,32,64]{3,1,2,0:T(8,128)} copy(f32[64,64,32,64]{3,2,1,0:T(8,128)} %reshape.446) | data formatting | bytes 67108864 | tf_op jit(solution)/shard_map/reshape | solution.py:49
  559.3 27.7 %gather_fusion.2 = f32[640,64,64]{2,1,0:T(8,128)} fusion(f32[64,64,32,64]{3,1,2,0:T(8,128)} %copy.23, s32[640]{0:T(1024)S(1)} %fusion.36), kind=kCustom, calls=%fused_computation.2 | custom fusion | bytes 20976640 | tf_op jit(solution)/shard_map/gather | solution.py:50
  587.0 12.9 %fusion.2 = bf16[64,640,64]{2,0,1:T(8,128)(2,1)} fusion(f32[640,64,64]{2,1,0:T(8,128)} %gather_fusion.2, f32[640]{0:T(1024)S(1)} %compare_convert_fusion), kind=kLoop, calls=%fused_computation.13 | loop fusion | flops 5242880 | bytes 15731200 | tf_op jit(solution)/shard_map/convert_element_type | solution.py:126
  600.0 14.7 %copy.24 = bf16[64,640,64]{2,1,0:T(8,128)(2,1)} copy(bf16[64,640,64]{2,0,1:T(8,128)(2,1)} %fusion.2) | data formatting | bytes 10485760 | tf_op jit(solution)/shard_map/convert_element_type | solution.py:126
  628.4 16.1 %convolution_bitcast_fusion.1 = f32[2048,4096]{0,1:T(8,128)} fusion(bf16[128,2048]{1,0:T(8,128)(2,1)S(1)} %copy-done.3, f32[128,4096]{0,1:T(8,128)S(1)} %copy-done, f32[128,4096]{0,1:T(8,128)} %all-reduce.4.cloned.1.call-done, f32[128,4096]{0,1:T(8,128)} %get-tuple-element.4), kind=kOutput, calls=%fused_computation.7 | convolution fusion | flops 2152726528 | bytes 40370176 | tf_op jit(solution)/shard_map/dot_general | solution.py:77
  644.5 54.4 %reshape.444 = f32[32,64,64,64]{1,0,3,2:T(8,128)} reshape(f32[2048,4096]{0,1:T(8,128)} %convolution_bitcast_fusion.1) | data formatting | bytes 67108864 | tf_op jit(solution)/shard_map/reshape | solution.py:52
  698.9 61.4 %copy.19 = f32[32,64,64,64]{3,1,2,0:T(8,128)} copy(f32[32,64,64,64]{1,0,3,2:T(8,128)} %reshape.444) | data formatting | bytes 67108864 | tf_op jit(solution)/shard_map/reshape | solution.py:52
  760.3 28.0 %gather_fusion = f32[640,64,64]{2,1,0:T(8,128)} fusion(f32[32,64,64,64]{3,1,2,0:T(8,128)} %copy.19, s32[640]{0:T(1024)S(1)} %fusion.38), kind=kCustom, calls=%fused_computation | custom fusion | bytes 20976640 | tf_op jit(solution)/shard_map/gather | solution.py:53
  788.3 13.0 %fusion = bf16[64,640,64]{2,0,1:T(8,128)(2,1)} fusion(f32[640,64,64]{2,1,0:T(8,128)} %gather_fusion, f32[640]{0:T(1024)S(1)} %compare_convert_fusion.2), kind=kLoop, calls=%fused_computation.11 | loop fusion | flops 5242880 | bytes 15731200 | tf_op jit(solution)/shard_map/convert_element_type | solution.py:120
  801.3 14.7 %copy.20 = bf16[64,640,64]{2,1,0:T(8,128)(2,1)} copy(bf16[64,640,64]{2,0,1:T(8,128)(2,1)} %fusion) | data formatting | bytes 10485760 | tf_op jit(solution)/shard_map/convert_element_type | solution.py:120
  828.8 15.8 %convolution_bitcast_fusion = f32[2048,4096]{0,1:T(8,128)} fusion(bf16[128,2048]{1,0:T(8,128)(2,1)S(1)} %copy-done.3, f32[128,4096]{0,1:T(8,128)} %all-reduce.4.cloned.1.call-done, f32[128,4096]{0,1:T(8,128)S(1)} %copy-done), kind=kOutput, calls=%fused_computation.6 | convolution fusion | flops 2150629376 | bytes 38273024 | tf_op jit(solution)/shard_map/dot_general | solution.py:77
  844.6 54.4 %reshape.445 = f32[32,64,64,64]{1,0,3,2:T(8,128)} reshape(f32[2048,4096]{0,1:T(8,128)} %convolution_bitcast_fusion) | data formatting | bytes 67108864 | tf_op jit(solution)/shard_map/reshape | solution.py:52
  899.0 61.5 %copy.21 = f32[32,64,64,64]{3,1,2,0:T(8,128)} copy(f32[32,64,64,64]{1,0,3,2:T(8,128)} %reshape.445) | data formatting | bytes 67108864 | tf_op jit(solution)/shard_map/reshape | solution.py:52
  960.4 27.7 %gather_fusion.1 = f32[640,64,64]{2,1,0:T(8,128)} fusion(f32[32,64,64,64]{3,1,2,0:T(8,128)} %copy.21, s32[640]{0:T(1024)S(1)} %fusion.37), kind=kCustom, calls=%fused_computation.1 | custom fusion | bytes 20976640 | tf_op jit(solution)/shard_map/gather | solution.py:53
  988.1 12.9 %fusion.1 = bf16[64,640,64]{2,0,1:T(8,128)(2,1)} fusion(f32[640,64,64]{2,1,0:T(8,128)} %gather_fusion.1, f32[640]{0:T(1024)S(1)} %compare_convert_fusion.1), kind=kLoop, calls=%fused_computation.12 | loop fusion | flops 5242880 | bytes 15731200 | tf_op jit(solution)/shard_map/convert_element_type | solution.py:123
  1001.1 14.7 %copy.22 = bf16[64,640,64]{2,1,0:T(8,128)(2,1)} copy(bf16[64,640,64]{2,0,1:T(8,128)(2,1)} %fusion.1) | data formatting | bytes 10485760 | tf_op jit(solution)/shard_map/convert_element_type | solution.py:123
  1027.9 73.4 %reduce-scatter.9.cloned.1.call-done = bf16[1,1,64,20480]{3,2,1,0:T(8,128)(2,1)} async-done(((bf16[1,1,64,40960]{3,2,1,0:T(8,128)(2,1)}), bf16[1,1,64,20480]{3,2,1,0:T(8,128)(2,1)}) %reduce-scatter.9.cloned.1.call-update) | async-done | bytes 2621456 | tf_op jit(solution)/shard_map/reduce_scatter | solution.py:122
  (66 shorter events, 110.7 us)
Async XLA Ops:
  7.2 362.1 %all-reduce.6.cloned.1.call-start = ((), (), s32[]{:S(2)}) async-start(), calls=%async_computation.9 | async-start | bytes 8388608 | tf_op jit(solution)/shard_map/psum | solution.py:100
  22.7 207.8 %copy-start.2 = (bf16[128,2048]{1,0:T(8,128)(2,1)}, bf16[128,2048]{1,0:T(8,128)(2,1)S(1)}, u32[]{:S(2)}) copy-start(bf16[128,2048]{1,0:T(8,128)(2,1)S(1)} %all_gather.6) | copy-start | bytes 1572868
  36.0 10.5 copy-start.10
  46.6 31.3 %copy-start.7 = (s32[640]{0:T(1024)}, s32[640]{0:T(1024)S(1)}, u32[]{:S(2)}) copy-start(s32[640]{0:T(1024)S(1)} %reduce) | copy-start | bytes 7684
  135.0 10.4 copy-start.12
  145.4 31.3 %copy-start.5 = (s32[640]{0:T(1024)}, s32[640]{0:T(1024)S(1)}, u32[]{:S(2)}) copy-start(s32[640]{0:T(1024)S(1)} %reduce.1) | copy-start | bytes 7684
  220.7 11.3 %copy-start.1 = (bf16[2048,4096]{1,0:T(8,128)(2,1)S(1)}, bf16[2048,4096]{1,0:T(8,128)(2,1)}, u32[]{:S(2)}) copy-start(bf16[2048,4096]{1,0:T(8,128)(2,1)} %reshape.441) | copy-start | bytes 50331652
  238.2 173.5 %reduce-scatter.5.cloned.1.call-start = ((), (), s32[]{:S(2)}) async-start(), calls=%async_computation.4 | async-start | bytes 1310720 | tf_op jit(solution)/shard_map/reduce_scatter | solution.py:107
  251.7 10.8 copy-start.9
  372.0 39.7 %copy-start.4 = (bf16[32,2048]{1,0:T(8,128)(2,1)S(1)}, bf16[32,2048]{1,0:T(8,128)(2,1)}, u32[]{:S(2)}) copy-start(bf16[32,2048]{1,0:T(8,128)(2,1)} %param.9) | copy-start | bytes 393220
  381.2 246.3 %all-reduce.4.cloned.1.call-start = ((), (), s32[]{:S(2)}) async-start(), calls=%async_computation.5 | async-start | bytes 4194304 | tf_op jit(solution)/shard_map/psum | solution.py:110
  434.7 593.2 %reduce-scatter.11.cloned.1.call-start = ((), (), s32[]{:S(2)}) async-start(), calls=%async_computation.8 | async-start | bytes 7864320 | tf_op jit(solution)/shard_map/reduce_scatter | solution.py:125
  626.7 0.7 copy-start.11
  626.7 0.7 copy-start.8
  626.7 1.6 copy-start
  626.7 1.7 copy-start.3
  626.8 401.1 %reduce-scatter.7.cloned.1.call-start = ((), (), s32[]{:S(2)}) async-start(), calls=%async_computation.6 | async-start | bytes 7864320 | tf_op jit(solution)/shard_map/reduce_scatter | solution.py:119
  828.0 0.7 copy-start.13
  828.0 0.7 copy-start.6
  828.0 273.3 %reduce-scatter.9.cloned.1.call-start = ((), (), s32[]{:S(2)}) async-start(), calls=%async_computation.7 | async-start | bytes 7864320 | tf_op jit(solution)/shard_map/reduce_scatter | solution.py:122
Sparse Core Ops, SparseCore 0:
  238.4 32.1 all-reduce.5
  381.3 30.3 reduce-scatter.4
  434.8 24.0 all-reduce.3
  626.9 70.0 reduce-scatter.10
  828.2 71.9 reduce-scatter.6
  1028.0 73.3 reduce-scatter.8
where the time goes:
time: 1130 us; the launch traced here: 1110 us
  local copies, waits for them, and re-layouts  744 us (66%)
  matrix products  175 us (15%)
  waiting for transfers between devices  104 us (9%)
  other arithmetic  42.8 us (4%)
  blocking collectives  27.6 us (2%)
  between operations  14.5 us (1%)
    reshape x4, local copies, waits for them, and re-layouts, extract(): tiles = dense_grad.reshape(row_blocks, block_size, slab_blocks, block_size)  232 us
    reshape x2, local copies, waits for them, and re-layouts, extract(): tiles = dense_grad.reshape(slab_blocks, block_size, row_blocks, block_size)  111 us
    dot_general x3, matrix products, densify(): placed = jnp.dot(onehot, blocks, preferred_element_type=jnp.bfloat16)  93.9 us
    reshape x2, local copies, waits for them, and re-layouts, densify(): placed.transpose(0, 2, 1, 3)  88.1 us
    reduce_scatter x1, waiting for transfers between devices, local(): lax.psum_scatter(up_term[None, None].astype(jnp.bfloat16), 'dp', scatter_...  73.4 us
    gather x2, local copies, waits for them, and re-layouts, extract(): picked = tiles[row_index, :, slab_index, :]  55.7 us
    reshape x1, local copies, waits for them, and re-layouts, densify(): placed.transpose(1, 2, 0, 3)  45.9 us
    another operation x3, local copies, waits for them, and re-layouts, slot_blocks(): slot_panel.reshape(block_size, cap_slots, block_size).transpose(1, 0, 2)  39.8 us
  transfers between devices with their start and end apart: 6, of which 2 were waited for; matrix products, arithmetic and copies ran while one was open for 65% of the time, Pallas kernels for 0%

commit v1 on v0

v1 whole, which is shorter than its diff:
```python
import functools

import jax
import jax.numpy as jnp
from jax import lax
from jax.experimental import pallas as pl
from jax.experimental.pallas import tpu as pltpu
from jax.sharding import PartitionSpec as P

D = 4096
FF = 16384
BLK = 64
PAIR = 2 * BLK
SLOPE_SCALE = 0.0625
VMEM_BYTES = 52 * 2**20


def left_half():
    return lax.broadcasted_iota(jnp.int32, (BLK, PAIR), 1) < BLK


def swap_halves(tile):
    return jnp.concatenate([tile[:, BLK:], tile[:, :BLK]], axis=1)


def densify_kernel(half_cap, rows_per_step, n_cols, table, panel, out, tiles):
    step = pl.program_id(0)

    @pl.when(step == 0)
    def _():
        tiles[2 * half_cap] = jnp.zeros((BLK, PAIR), tiles.dtype)

        def stage(t, carry):
            tile = panel[:, pl.ds(pl.multiple_of(t * PAIR, PAIR), PAIR)]
            tiles[t] = tile
            tiles[half_cap + t] = swap_halves(tile)
            return carry

        lax.fori_loop(0, half_cap, stage, 0, unroll=4)

    mask = left_half()

    def row(i, carry):
        base = (step * rows_per_step + i) * n_cols
        for p in range(n_cols // 2):
            left = tiles[table[base + 2 * p]]
            right = tiles[table[base + 2 * p + 1]]
            out[pl.ds(pl.multiple_of(i * BLK, BLK), BLK), p * PAIR : (p + 1) * PAIR] = jnp.where(
                mask, left, right
            )
        return carry

    lax.fori_loop(0, rows_per_step, row, 0)


def densify(panel, table):
    n_rows, n_cols = table.shape
    half_cap = panel.shape[1] // PAIR
    rows_per_step = 4
    return pl.pallas_call(
        functools.partial(densify_kernel, half_cap, rows_per_step, n_cols),
        grid_spec=pltpu.PrefetchScalarGridSpec(
            num_scalar_prefetch=1,
            grid=(n_rows // rows_per_step,),
            in_specs=[pl.BlockSpec(panel.shape, lambda s, *_: (0, 0))],
            out_specs=pl.BlockSpec((rows_per_step * BLK, n_cols * BLK), lambda s, *_: (s, 0)),
            scratch_shapes=[pltpu.VMEM((2 * half_cap + 1, BLK, PAIR), panel.dtype)],
        ),
        out_shape=jax.ShapeDtypeStruct((n_rows * BLK, n_cols * BLK), panel.dtype),
        compiler_params=pltpu.CompilerParams(vmem_limit_bytes=VMEM_BYTES),
        cost_estimate=pl.CostEstimate(
            flops=0, bytes_accessed=2 * panel.size + 2 * n_rows * n_cols * BLK * BLK, transcendentals=0
        ),
        name="densify",
    )(table.reshape(-1), panel)


def gradient_kernel(n_steps, rows_per_step, n_cols, picks, lhs, rhs, out, tiles):
    step = pl.program_id(0)
    col_pairs = n_cols // 2
    width = min(4, col_pairs)
    for c in range(0, col_pairs, width):
        part = jnp.dot(
            lhs[...], rhs[:, c * PAIR : (c + width) * PAIR], preferred_element_type=jnp.float32
        ).astype(tiles.dtype)
        for i in range(rows_per_step):
            for p in range(width):
                tiles[(step * rows_per_step + i) * col_pairs + c + p] = part[
                    i * BLK : (i + 1) * BLK, p * PAIR : (p + 1) * PAIR
                ]

    @pl.when(step == n_steps - 1)
    def _():
        tiles[n_steps * rows_per_step * col_pairs] = jnp.zeros((BLK, PAIR), tiles.dtype)
        mask = left_half()

        def fetch(code):
            tile = tiles[code // 2]
            return jnp.where(code % 2 == 1, swap_halves(tile), tile)

        def pick(k, carry):
            out[:, pl.ds(pl.multiple_of(k * PAIR, PAIR), PAIR)] = jnp.where(
                mask, fetch(picks[2 * k]), fetch(picks[2 * k + 1])
            )
            return carry

        lax.fori_loop(0, out.shape[1] // PAIR, pick, 0, unroll=2)


def gradient(lhs, rhs, picks):
    n_rows, n_cols = lhs.shape[0] // BLK, rhs.shape[1] // BLK
    rows_per_step = 4
    n_steps = n_rows // rows_per_step
    return pl.pallas_call(
        functools.partial(gradient_kernel, n_steps, rows_per_step, n_cols),
        grid_spec=pltpu.PrefetchScalarGridSpec(
            num_scalar_prefetch=1,
            grid=(n_steps,),
            in_specs=[
                pl.BlockSpec((rows_per_step * BLK, lhs.shape[1]), lambda s, *_: (s, 0)),
                pl.BlockSpec(rhs.shape, lambda s, *_: (0, 0)),
            ],
            out_specs=pl.BlockSpec((BLK, picks.shape[0] * BLK), lambda s, *_: (0, 0)),
            scratch_shapes=[pltpu.VMEM((n_rows * n_cols // 2 + 1, BLK, PAIR), jnp.bfloat16)],
        ),
        out_shape=jax.ShapeDtypeStruct((BLK, picks.shape[0] * BLK), jnp.bfloat16),
        compiler_params=pltpu.CompilerParams(vmem_limit_bytes=VMEM_BYTES),
        cost_estimate=pl.CostEstimate(
            flops=2 * lhs.shape[0] * lhs.shape[1] * rhs.shape[1],
            bytes_accessed=2 * (lhs.size + rhs.size + picks.shape[0] * BLK * BLK),
            transcendentals=0,
        ),
        name="gradient",
    )(picks, lhs, rhs)


def tile_table(block_ids, row_blocks, slab_blocks, rows_are_hidden):
    cap = block_ids.shape[0]
    grid = row_blocks * slab_blocks
    slot = jnp.arange(1, cap + 1, dtype=jnp.int32)
    held = jnp.sum(
        jnp.where(block_ids[None, :] == jnp.arange(grid, dtype=jnp.int32)[:, None], slot[None, :], 0), axis=1
    )
    held = held.reshape(row_blocks, slab_blocks)
    if rows_are_hidden:
        held = held.T
    half = jnp.arange(held.shape[1], dtype=jnp.int32)[None, :] % 2
    index = held - 1
    tile = index // 2 + jnp.where(index % 2 != half, cap // 2, 0)
    return jnp.where(held > 0, tile, cap)


def pick_codes(block_ids, row_blocks, slab_blocks, rows_are_hidden):
    grid = row_blocks * slab_blocks
    row, col = block_ids // slab_blocks, block_ids % slab_blocks
    cols = slab_blocks
    if rows_are_hidden:
        row, col, cols = col, row, row_blocks
    half = jnp.arange(block_ids.shape[0], dtype=jnp.int32) % 2
    code = 2 * (row * (cols // 2) + col // 2) + jnp.where(col % 2 != half, 1, 0)
    return jnp.where(block_ids < grid, code, grid)


def shift(values, axis, k):
    n = lax.axis_size(axis)
    return values if k == 0 else lax.ppermute(values, axis, [(i, i ^ k) for i in range(n)])


def gather_rows(values):
    near = [shift(values, "hid", k) for k in range(lax.axis_size("hid"))]
    return [[shift(v, "dp", j) for v in near] for j in range(lax.axis_size("dp"))]


def swap_cores(values):
    return lax.ppermute(values, "col", [(0, 1), (1, 0)])


def f32(values):
    return values.astype(jnp.float32)


def local(tokens, target, gate_panel, up_panel, down_panel, gate_list, up_list, down_list):
    n_hid, n_dp = lax.axis_size("hid"), lax.axis_size("dp")
    slab_blocks = FF // BLK // n_hid
    row_blocks = D // BLK // lax.axis_size("col")
    rows = tokens.shape[0]
    own = rows * n_hid

    shards = gather_rows(tokens)
    inputs = jnp.concatenate([v for part in shards for v in part])

    gate_w = densify(gate_panel[0, 0], tile_table(gate_list[0, 0], row_blocks, slab_blocks, False))
    up_w = densify(up_panel[0, 0], tile_table(up_list[0, 0], row_blocks, slab_blocks, False))
    down_w = densify(down_panel[0, 0], tile_table(down_list[0, 0], row_blocks, slab_blocks, True))

    def mine(block_list):
        share = block_list.shape[-1] // n_dp
        return lax.dynamic_slice_in_dim(block_list[0, 0], lax.axis_index("dp") * share, share)

    gate_codes = pick_codes(mine(gate_list), row_blocks, slab_blocks, False)
    up_codes = pick_codes(mine(up_list), row_blocks, slab_blocks, False)
    down_codes = pick_codes(mine(down_list), row_blocks, slab_blocks, True)

    gate_part = jnp.dot(inputs, gate_w, preferred_element_type=jnp.float32).astype(jnp.bfloat16)
    gate_other = swap_cores(gate_part)
    up_part = jnp.dot(inputs, up_w, preferred_element_type=jnp.float32).astype(jnp.bfloat16)
    up_other = swap_cores(up_part)
    gate = f32(gate_part) + f32(gate_other)
    up = f32(up_part) + f32(up_other)
    sigmoid_gate = jax.nn.sigmoid(gate)
    hidden = (gate * sigmoid_gate * up).astype(jnp.bfloat16)

    out_part = jnp.dot(hidden[:own], down_w, preferred_element_type=jnp.float32).astype(jnp.bfloat16)
    output = f32(out_part[:rows])
    for k in range(1, n_hid):
        output = output + f32(shift(out_part[k * rows : (k + 1) * rows], "hid", k))
    own_slope = ((output - f32(target)) * SLOPE_SCALE).astype(jnp.bfloat16)
    slope_shards = gather_rows(own_slope)
    slope = jnp.concatenate([v for part in slope_shards for v in part])

    back_part = lax.dot_general(
        slope, down_w, (((1,), (1,)), ((), ())), preferred_element_type=jnp.float32
    ).astype(jnp.bfloat16)
    back = f32(back_part) + f32(swap_cores(back_part))
    gate_slope = (back * up * sigmoid_gate * (1.0 + gate * (1.0 - sigmoid_gate))).astype(jnp.bfloat16)
    up_slope = (back * (gate * sigmoid_gate)).astype(jnp.bfloat16)

    inputs_t = inputs.T
    down_grad = gradient(hidden.T, slope, down_codes)
    gate_grad = gradient(inputs_t, gate_slope, gate_codes)
    up_grad = gradient(inputs_t, up_slope, up_codes)
    return gate_grad[None, None], up_grad[None, None], down_grad[None, None]


def solution(mesh):
    return jax.shard_map(
        local,
        mesh=mesh,
        in_specs=(
            P(("groups", "hid", "dp"), "col"),
            P(("groups", "hid", "dp"), "col"),
            P(("groups", "hid"), "col", None, None),
            P(("groups", "hid"), "col", None, None),
            P(("groups", "hid"), "col", None, None),
            P(("groups", "hid"), "col", None),
            P(("groups", "hid"), "col", None),
            P(("groups", "hid"), "col", None),
        ),
        out_specs=(
            P(("groups", "hid"), "col", None, "dp"),
            P(("groups", "hid"), "col", None, "dp"),
            P(("groups", "hid"), "col", None, "dp"),
        ),
        check_vma=False,
    )
```

time: 1130 us -> 268 us (0.24); the launches traced: 1110 us -> 268 us
  local copies, waits for them, and re-layouts: 744 us -> 17.6 us
  matrix products: 175 us -> 36.8 us
  Pallas kernels: 0 us -> 114 us
  waiting for transfers between devices: 104 us -> 48.1 us
  starting transfers between devices: 0.25 us -> 34.9 us
  other arithmetic: 42.8 us -> 15.1 us
  blocking collectives: 27.6 us -> 0 us
  between operations: 14.5 us -> 0.99 us
    reshape x9 -> x1, local copies, waits for them, and re-layouts: 476 us -> 0.07 us  [densify(): table.reshape(-1)]
    dot_general x10 -> x4, matrix products: 175 us -> 36.8 us  [the longest x1 11.6 us: local(): jnp.dot(inputs, up_w, preferred_element_type=jnp.float32)]
    pallas_call x0 -> x6, Pallas kernels: none -> 114 us  [the longest x3 59.6 us: densify(): pl.pallas_call(functools.partial(densify_kernel, half_cap, rows_per_step,...]
    reduce_scatter x4 -> x0, waiting for transfers between devices: 104 us -> none  [the longest x1 73.4 us: local(): lax.psum_scatter(up_term[None, None].astype(jnp.bfloat16), 'dp', scatter_...]
    gather x3 -> x0, local copies, waits for them, and re-layouts: 83.4 us -> none  [the longest x2 55.7 us: extract(): picked = tiles[row_index, :, slab_index, :]]
    convert_element_type x6 -> x2, local copies, waits for them, and re-layouts: 80.1 us -> 8.21 us  [the longest x1 4.12 us: local(): (back * up * sigmoid_gate * (1.0 + gate * (1.0 - sigmoid_gate))).astype(j...]
    transpose x4 -> x0, local copies, waits for them, and re-layouts: 61.1 us -> none  [the longest x3 31.7 us: slot_blocks(): slot_panel.reshape(block_size, cap_slots, block_size).transpose(1, 0, 2)]
    ppermute x0 -> x20, waiting for transfers between devices: none -> 48.1 us  [the longest x17 48.1 us: shift(): lax.ppermute(values, axis, [(i, i ^ k) for i in range(n)])]
  transfers between devices with their start and end apart: 6 -> 20, of which waited for: 2 -> 8; matrix products, arithmetic and copies ran while one was open for 65% -> 6% of each run, Pallas kernels for 0% -> 30%
where the time goes in v1:
time: 268 us
  Pallas kernels  114 us (43%)
  waiting for transfers between devices  48.1 us (18%)
  matrix products  36.8 us (14%)
  starting transfers between devices  34.9 us (13%)
  local copies, waits for them, and re-layouts  17.6 us (7%)
  other arithmetic  15.1 us (6%)
    pallas_call x3, Pallas kernels, densify(): pl.pallas_call(functools.partial(densify_kernel, half_cap, rows_per_step,...  59.6 us
    pallas_call x3, Pallas kernels, gradient(): pl.pallas_call(functools.partial(gradient_kernel, n_steps, rows_per_step,...  54.5 us
    ppermute x17, waiting for transfers between devices, shift(): lax.ppermute(values, axis, [(i, i ^ k) for i in range(n)])  48.1 us
    ppermute x17, starting transfers between devices, shift(): lax.ppermute(values, axis, [(i, i ^ k) for i in range(n)])  27 us
    dot_general x1, matrix products, local(): jnp.dot(inputs, up_w, preferred_element_type=jnp.float32)  11.6 us
    dot_general x1, matrix products, local(): jnp.dot(inputs, gate_w, preferred_element_type=jnp.float32)  10.3 us
    dot_general x1, matrix products, local(): jnp.dot(hidden[:own], down_w, preferred_element_type=jnp.float32)  8.93 us
    ppermute x3, starting transfers between devices, swap_cores(): return lax.ppermute(values, 'col', [(0, 1), (1, 0)])  7.9 us
  transfers between devices with their start and end apart: 20, of which 8 were waited for; matrix products, arithmetic and copies ran while one was open for 6% of the time, Pallas kernels for 30%

profile of v1, /device:TPU:1, one launch (start us, length us, event | category | flops | bytes accessed | tf_op | source)
XLA Modules:
  0.0 267.6 jit_solution(13077275356621212075)
XLA Ops:
  1.8 2.2 collective-permute-start
  4.0 2.3 collective-permute-start.1
  6.3 1.2 collective-permute-start.3
  9.6 2.0 select_reduce_fusion
  11.7 14.4 %collective-permute-done = bf16[32,2048]{0,1:T(8,128)(2,1)S(1)} collective-permute-done((bf16[32,2048]{0,1:T(8,128)(2,1)S(1)}, bf16[32,2048]{0,1:T(8,128)(2,1)S(1)}, u32[]{:S(2)}, u32[]{:S(2)}) %collective-permute-start) | collective-permute-done | bytes 131104 | tf_op jit(solution)/shard_map/ppermute | solution.py:166
  27.6 12.5 %collective-permute-done.2 = bf16[32,2048]{0,1:T(8,128)(2,1)S(1)} collective-permute-done((bf16[32,2048]{0,1:T(8,128)(2,1)S(1)}, bf16[32,2048]{0,1:T(8,128)(2,1)S(1)}, u32[]{:S(2)}, u32[]{:S(2)}) %collective-permute-start.2) | collective-permute-done | bytes 131104 | tf_op jit(solution)/shard_map/ppermute | solution.py:166
  40.0 1.2 collective-permute-start.6
  41.3 19.1 %densify.3 = bf16[2048,4096]{1,0:T(8,128)(2,1)} custom-call(s32[2048]{0:T(1024)S(1)} %get-tuple-element.14.table, bf16[64,40960]{1,0:T(8,128)(2,1)} %bitcast.38), custom_call_target="tpu_custom_call" | custom-call | bytes 22020096 | tf_op jit(solution)/shard_map/densify/pallas_call | solution.py:60
  60.4 19.1 %densify.4 = bf16[2048,4096]{1,0:T(8,128)(2,1)} custom-call(s32[2048]{0:T(1024)S(1)} %get-tuple-element.13.table, bf16[64,40960]{1,0:T(8,128)(2,1)} %bitcast.39), custom_call_target="tpu_custom_call" | custom-call | bytes 22020096 | tf_op jit(solution)/shard_map/densify/pallas_call | solution.py:60
  81.3 5.7 %concatenate.6 = bf16[256,2048]{0,1:T(8,128)(2,1)S(1)} concatenate(bf16[32,2048]{0,1:T(8,128)(2,1)S(1)} %copy.46, bf16[32,2048]{0,1:T(8,128)(2,1)S(1)} %collective-permute-done, bf16[32,2048]{0,1:T(8,128)(2,1)S(1)} %collective-permute-done.1, bf16[32,2048]{0,1:T(8,128)(2,1)S(1)} %collective-permute-done.2, bf16[32,2048]{0,1:T(8,128)(2,1)} %copy-done.5, ...), dimensions={0} | concatenate | bytes 2097152 | tf_op jit(solution)/shard_map/concatenate | solution.py:190
  87.1 10.3 %convolution_convert_fusion.2 = bf16[256,4096]{0,1:T(8,128)(2,1)S(1)} fusion(bf16[256,2048]{0,1:T(8,128)(2,1)S(1)} %concatenate.6, bf16[2048,4096]{1,0:T(8,128)(2,1)} %densify.3), kind=kOutput, calls=%fused_computation.8 | convolution fusion | flops 4296015872 | bytes 19922944 | tf_op jit(solution)/shard_map/dot_general | solution.py:204
  97.4 4.0 %collective-permute-start.7 = (bf16[256,4096]{0,1:T(8,128)(2,1)S(1)}, bf16[256,4096]{0,1:T(8,128)(2,1)}, u32[]{:S(2)}, u32[]{:S(2)}) collective-permute-start(bf16[256,4096]{0,1:T(8,128)(2,1)S(1)} %convolution_convert_fusion.2), channel_id=1, source_target_pairs={{0,1},{1,0},{2,3},{3,2},{4,5},{5,4},{6,7},{7,6},{8,9},{9,8},{10,11... | collective-permute-start | bytes 6291464 | tf_op jit(solution)/shard_map/ppermute | solution.py:175
  101.4 11.6 %convolution_convert_fusion.1 = bf16[256,4096]{0,1:T(8,128)(2,1)} fusion(bf16[256,2048]{0,1:T(8,128)(2,1)S(1)} %concatenate.6, bf16[2048,4096]{1,0:T(8,128)(2,1)} %densify.4), kind=kOutput, calls=%fused_computation.7 | convolution fusion | flops 4296015872 | bytes 19922944 | tf_op jit(solution)/shard_map/dot_general | solution.py:206
  114.2 21.4 %densify.5 = bf16[4096,2048]{1,0:T(8,128)(2,1)} custom-call(s32[2048]{0:T(1024)S(1)} %reshape.60.table, bf16[64,40960]{1,0:T(8,128)(2,1)} %bitcast.40), custom_call_target="tpu_custom_call" | custom-call | bytes 22020096 | tf_op jit(solution)/shard_map/densify/pallas_call | solution.py:60
  135.6 4.1 %multiply_convert_fusion.2 = bf16[256,4096]{0,1:T(8,128)(2,1)S(1)} fusion(bf16[256,4096]{0,1:T(8,128)(2,1)} %collective-permute-done.8, bf16[256,4096]{0,1:T(8,128)(2,1)S(1)} %copy-done.2, bf16[256,4096]{0,1:T(8,128)(2,1)} %collective-permute-done.7, bf16[256,4096]{0,1:T(8,128)(2,1)S(1)} %convolution_convert_fusion.2), kind=kLoop, calls=%fused_computation.12 | loop fusion | flops 12582912 | bytes 10485760 | tf_op jit(solution)/shard_map/convert_element_type | solution.py:211
  139.7 8.9 %convolution_convert_fusion.3 = bf16[128,2048]{1,0:T(8,128)(2,1)S(1)} fusion(bf16[4096,2048]{1,0:T(8,128)(2,1)} %densify.5, bf16[256,4096]{0,1:T(8,128)(2,1)S(1)} %multiply_convert_fusion.2), kind=kOutput, calls=%fused_computation.17 | convolution fusion | flops 2147745792 | bytes 18350080 | tf_op jit(solution)/shard_map/dot_general | solution.py:213
  148.7 10.6 %collective-permute-start.10 = (bf16[32,2048]{1,0:T(8,128)(2,1)S(1)}, bf16[32,2048]{1,0:T(8,128)(2,1)S(1)}, u32[]{:S(2)}, u32[]{:S(2)}) collective-permute-start(bf16[32,2048]{1,0:T(8,128)(2,1)S(1)} %get-tuple-element.12), channel_id=1, source_target_pairs={{0,8},{4,12},{8,0},{12,4},{1,9},{5,13},{9,1},{13,5},{2,10},{6,14},... | collective-permute-start | bytes 393224 | tf_op jit(solution)/shard_map/ppermute | solution.py:166
  160.4 8.5 %collective-permute-done.10 = bf16[32,2048]{1,0:T(8,128)(2,1)S(1)} collective-permute-done((bf16[32,2048]{1,0:T(8,128)(2,1)S(1)}, bf16[32,2048]{1,0:T(8,128)(2,1)S(1)}, u32[]{:S(2)}, u32[]{:S(2)}) %collective-permute-start.10) | collective-permute-done | bytes 131104 | tf_op jit(solution)/shard_map/ppermute | solution.py:166
  169.5 2.7 %collective-permute-start.12 = (bf16[32,2048]{1,0:T(8,128)(2,1)S(1)}, bf16[32,2048]{1,0:T(8,128)(2,1)S(1)}, u32[]{:S(2)}, u32[]{:S(2)}) collective-permute-start(bf16[32,2048]{1,0:T(8,128)(2,1)S(1)} %get-tuple-element.7), channel_id=1, source_target_pairs={{0,4},{4,0},{8,12},{12,8},{1,5},{5,1},{9,13},{13,9},{2,6},{6,2},{1... | collective-permute-start | bytes 393224 | tf_op jit(solution)/shard_map/ppermute | solution.py:166
  172.2 2.2 collective-permute-start.14
  175.8 7.5 %collective-permute-done.13 = bf16[32,2048]{1,0:T(8,128)(2,1)S(1)} collective-permute-done((bf16[32,2048]{1,0:T(8,128)(2,1)S(1)}, bf16[32,2048]{1,0:T(8,128)(2,1)S(1)}, u32[]{:S(2)}, u32[]{:S(2)}) %collective-permute-start.13) | collective-permute-done | bytes 131104 | tf_op jit(solution)/shard_map/ppermute | solution.py:166
  183.5 1.3 collective-permute-start.18
  184.9 2.2 collective-permute-done.17
  187.1 1.7 collective-permute-done.18
  188.9 5.9 %convolution_convert_fusion = bf16[256,4096]{0,1:T(8,128)(2,1)} fusion(bf16[256,2048]{1,0:T(8,128)(2,1)S(1)} %constant_dynamic-update-slice_fusion.rhs, bf16[4096,2048]{1,0:T(8,128)(2,1)S(1)} %bitcast.36), kind=kOutput, calls=%fused_computation.6 | convolution fusion | flops 4296015872 | bytes 19922944 | tf_op jit(solution)/shard_map/dot_general | solution.py:221
  194.8 3.2 %collective-permute-start.19 = (bf16[256,4096]{0,1:T(8,128)(2,1)}, bf16[256,4096]{0,1:T(8,128)(2,1)}, u32[]{:S(2)}, u32[]{:S(2)}) collective-permute-start(bf16[256,4096]{0,1:T(8,128)(2,1)} %convolution_convert_fusion), channel_id=1, source_target_pairs={{0,1},{1,0},{2,3},{3,2},{4,5},{5,4},{6,7},{7,6},{8,9},{9,8},{10,11... | collective-permute-start | bytes 6291464 | tf_op jit(solution)/shard_map/ppermute | solution.py:175
  198.3 21.0 %gradient.5 = bf16[64,20480]{1,0:T(8,128)(2,1)} custom-call(s32[320]{0:T(512)S(1)} %fusion.34.picks, bf16[4096,256]{1,0:T(8,128)(2,1)} %bitcast.37, bf16[256,2048]{1,0:T(8,128)(2,1)S(1)} %constant_dynamic-update-slice_fusion.rhs), custom_call_target="tpu_custom_call" | custom-call | flops 4294967296 | bytes 5767168 | tf_op jit(solution)/shard_map/gradient/pallas_call | solution.py:114
  219.3 6.6 %multiply_convert_fusion = (bf16[256,4096]{0,1:T(8,128)(2,1)}, bf16[256,4096]{0,1:T(8,128)(2,1)}) fusion(bf16[256,4096]{0,1:T(8,128)(2,1)} %collective-permute-done.19, bf16[256,4096]{0,1:T(8,128)(2,1)} %convolution_convert_fusion, bf16[256,4096]{0,1:T(8,128)(2,1)} %collective-permute-done.7, bf16[256,4096]{0,1:T(8,128)(2,1)S(1)} %copy-done.1, ...), kind=kLoop, calls=%fused_computation.9 | loop fusion | flops 23068672 | bytes 16777216 | tf_op jit(solution)/shard_map/convert_element_type | solution.py:226
  225.9 4.1 %copy.52.rhs = bf16[256,4096]{1,0:T(8,128)(2,1)} copy(bf16[256,4096]{0,1:T(8,128)(2,1)} %get-tuple-element.8) | data formatting | bytes 4194304 | tf_op jit(solution)/shard_map/convert_element_type | solution.py:226
  230.0 4.1 %copy.51.rhs = bf16[256,4096]{1,0:T(8,128)(2,1)} copy(bf16[256,4096]{0,1:T(8,128)(2,1)} %get-tuple-element.9) | data formatting | bytes 4194304 | tf_op jit(solution)/shard_map/convert_element_type | solution.py:225
  234.1 16.7 %gradient.4 = bf16[64,20480]{1,0:T(8,128)(2,1)} custom-call(s32[320]{0:T(512)S(1)} %fusion.28.picks, bf16[2048,256]{1,0:T(8,128)(2,1)S(1)} %bitcast.33, bf16[256,4096]{1,0:T(8,128)(2,1)} %copy.52.rhs), custom_call_target="tpu_custom_call" | custom-call | flops 4294967296 | bytes 5767168 | tf_op jit(solution)/shard_map/gradient/pallas_call | solution.py:114
  250.9 16.7 %gradient.3 = bf16[64,20480]{1,0:T(8,128)(2,1)} custom-call(s32[320]{0:T(512)S(1)} %fusion.22.picks, bf16[2048,256]{1,0:T(8,128)(2,1)S(1)} %bitcast.34, bf16[256,4096]{1,0:T(8,128)(2,1)} %copy.51.rhs), custom_call_target="tpu_custom_call" | custom-call | flops 4294967296 | bytes 5767168 | tf_op jit(solution)/shard_map/gradient/pallas_call | solution.py:114
  (87 shorter events, 11.5 us)
Async XLA Ops:
  1.8 24.3 %collective-permute-start = (bf16[32,2048]{0,1:T(8,128)(2,1)S(1)}, bf16[32,2048]{0,1:T(8,128)(2,1)S(1)}, u32[]{:S(2)}, u32[]{:S(2)}) collective-permute-start(bf16[32,2048]{0,1:T(8,128)(2,1)S(1)} %copy.46), channel_id=1, source_target_pairs={{0,4},{4,0},{8,12},{12,8},{1,5},{5,1},{9,13},{13,9},{2,6},{6,2},{1... | collective-permute-start | bytes 393224 | tf_op jit(solution)/shard_map/ppermute | solution.py:166
  4.0 23.2 %collective-permute-start.1 = (bf16[32,2048]{0,1:T(8,128)(2,1)S(1)}, bf16[32,2048]{0,1:T(8,128)(2,1)S(1)}, u32[]{:S(2)}, u32[]{:S(2)}) collective-permute-start(bf16[32,2048]{0,1:T(8,128)(2,1)S(1)} %copy.46), channel_id=1, source_target_pairs={{0,8},{4,12},{8,0},{12,4},{1,9},{5,13},{9,1},{13,5},{2,10},{6,14},... | collective-permute-start | bytes 393224 | tf_op jit(solution)/shard_map/ppermute | solution.py:166
  6.3 33.7 %collective-permute-start.2 = (bf16[32,2048]{0,1:T(8,128)(2,1)S(1)}, bf16[32,2048]{0,1:T(8,128)(2,1)S(1)}, u32[]{:S(2)}, u32[]{:S(2)}) collective-permute-start(bf16[32,2048]{0,1:T(8,128)(2,1)S(1)} %copy.46), channel_id=1, source_target_pairs={{0,12},{4,8},{8,4},{12,0},{1,13},{5,9},{9,5},{13,1},{2,14},{6,10},... | collective-permute-start | bytes 393224 | tf_op jit(solution)/shard_map/ppermute | solution.py:166
  6.3 73.2 %collective-permute-start.3 = (bf16[32,2048]{0,1:T(8,128)(2,1)S(1)}, bf16[32,2048]{0,1:T(8,128)(2,1)S(1)}, u32[]{:S(2)}, u32[]{:S(2)}) collective-permute-start(bf16[32,2048]{0,1:T(8,128)(2,1)S(1)} %copy.46), channel_id=1, source_target_pairs={{0,2},{2,0},{1,3},{3,1},{4,6},{6,4},{5,7},{7,5},{8,10},{10,8},{9,1... | collective-permute-start | bytes 393224 | tf_op jit(solution)/shard_map/ppermute | solution.py:166
  26.1 53.4 %collective-permute-start.4 = (bf16[32,2048]{0,1:T(8,128)(2,1)S(1)}, bf16[32,2048]{0,1:T(8,128)(2,1)S(1)}, u32[]{:S(2)}, u32[]{:S(2)}) collective-permute-start(bf16[32,2048]{0,1:T(8,128)(2,1)S(1)} %collective-permute-done), channel_id=1, source_target_pairs={{0,2},{2,0},{1,3},{3,1},{4,6},{6,4},{5,7},{7,5},{8,10},{10,8},{9,1... | collective-permute-start | bytes 393224 | tf_op jit(solution)/shard_map/ppermute | solution.py:166
  27.2 52.4 %collective-permute-start.5 = (bf16[32,2048]{0,1:T(8,128)(2,1)S(1)}, bf16[32,2048]{0,1:T(8,128)(2,1)S(1)}, u32[]{:S(2)}, u32[]{:S(2)}) collective-permute-start(bf16[32,2048]{0,1:T(8,128)(2,1)S(1)} %collective-permute-done.1), channel_id=1, source_target_pairs={{0,2},{2,0},{1,3},{3,1},{4,6},{6,4},{5,7},{7,5},{8,10},{10,8},{9,1... | collective-permute-start | bytes 393224 | tf_op jit(solution)/shard_map/ppermute | solution.py:166
  40.0 41.3 %collective-permute-start.6 = (bf16[32,2048]{0,1:T(8,128)(2,1)S(1)}, bf16[32,2048]{0,1:T(8,128)(2,1)}, u32[]{:S(2)}, u32[]{:S(2)}) collective-permute-start(bf16[32,2048]{0,1:T(8,128)(2,1)S(1)} %collective-permute-done.2), channel_id=1, source_target_pairs={{0,2},{2,0},{1,3},{3,1},{4,6},{6,4},{5,7},{7,5},{8,10},{10,8},{9,1... | collective-permute-start | bytes 393224 | tf_op jit(solution)/shard_map/ppermute | solution.py:166
  97.4 38.2 %copy-start = (bf16[256,4096]{0,1:T(8,128)(2,1)}, bf16[256,4096]{0,1:T(8,128)(2,1)S(1)}, u32[]{:S(2)}) copy-start(bf16[256,4096]{0,1:T(8,128)(2,1)S(1)} %convolution_convert_fusion.2) | copy-start | bytes 6291460
  97.4 38.1 %collective-permute-start.7 = (bf16[256,4096]{0,1:T(8,128)(2,1)S(1)}, bf16[256,4096]{0,1:T(8,128)(2,1)}, u32[]{:S(2)}, u32[]{:S(2)}) collective-permute-start(bf16[256,4096]{0,1:T(8,128)(2,1)S(1)} %convolution_convert_fusion.2), channel_id=1, source_target_pairs={{0,1},{1,0},{2,3},{3,2},{4,5},{5,4},{6,7},{7,6},{8,9},{9,8},{10,11... | collective-permute-start | bytes 6291464 | tf_op jit(solution)/shard_map/ppermute | solution.py:175
  113.1 22.5 %collective-permute-start.8 = (bf16[256,4096]{0,1:T(8,128)(2,1)}, bf16[256,4096]{0,1:T(8,128)(2,1)}, u32[]{:S(2)}, u32[]{:S(2)}) collective-permute-start(bf16[256,4096]{0,1:T(8,128)(2,1)} %convolution_convert_fusion.1), channel_id=1, source_target_pairs={{0,1},{1,0},{2,3},{3,2},{4,5},{5,4},{6,7},{7,6},{8,9},{9,8},{10,11... | collective-permute-start | bytes 6291464 | tf_op jit(solution)/shard_map/ppermute | solution.py:175
  114.2 21.4 %copy-start.2 = (bf16[256,4096]{0,1:T(8,128)(2,1)S(1)}, bf16[256,4096]{0,1:T(8,128)(2,1)}, u32[]{:S(2)}) copy-start(bf16[256,4096]{0,1:T(8,128)(2,1)} %convolution_convert_fusion.1) | copy-start | bytes 6291460
  135.6 53.2 %slice-start = ((s8[16777216]{0:T(1024)(128)(4,1)}), s8[4194304]{0:T(1024)(128)(4,1)S(1)}, s32[]{:S(2)}) async-start(s8[16777216]{0:T(1024)(128)(4,1)} %bitcast.35), calls=%async_computation | async-start | bytes 8388608
  135.6 53.2 %slice-start.1 = ((s8[16777216]{0:T(1024)(128)(4,1)}), s8[4194304]{0:T(1024)(128)(4,1)S(1)}, s32[]{:S(2)}) async-start(s8[16777216]{0:T(1024)(128)(4,1)} %bitcast.35), calls=%async_computation.1 | async-start | bytes 8388608
  139.7 29.7 %copy-start.8 = (bf16[32,2048]{1,0:T(8,128)(2,1)S(1)}, bf16[32,2048]{1,0:T(8,128)(2,1)}, u32[]{:S(2)}) copy-start(bf16[32,2048]{1,0:T(8,128)(2,1)} %param.9) | copy-start | bytes 393220
  139.7 49.1 %slice-start.2 = ((s8[16777216]{0:T(1024)(128)(4,1)}), s8[4194304]{0:T(1024)(128)(4,1)S(1)}, s32[]{:S(2)}) async-start(s8[16777216]{0:T(1024)(128)(4,1)} %bitcast.35), calls=%async_computation.2 | async-start | bytes 8388608
  139.7 49.1 %slice-start.3 = ((s8[16777216]{0:T(1024)(128)(4,1)}), s8[4194304]{0:T(1024)(128)(4,1)S(1)}, s32[]{:S(2)}) async-start(s8[16777216]{0:T(1024)(128)(4,1)} %bitcast.35), calls=%async_computation.3 | async-start | bytes 8388608
  148.7 20.2 %collective-permute-start.10 = (bf16[32,2048]{1,0:T(8,128)(2,1)S(1)}, bf16[32,2048]{1,0:T(8,128)(2,1)S(1)}, u32[]{:S(2)}, u32[]{:S(2)}) collective-permute-start(bf16[32,2048]{1,0:T(8,128)(2,1)S(1)} %get-tuple-element.12), channel_id=1, source_target_pairs={{0,8},{4,12},{8,0},{12,4},{1,9},{5,13},{9,1},{13,5},{2,10},{6,14},... | collective-permute-start | bytes 393224 | tf_op jit(solution)/shard_map/ppermute | solution.py:166
  159.4 9.5 %collective-permute-start.11 = (bf16[32,2048]{1,0:T(8,128)(2,1)S(1)}, bf16[32,2048]{1,0:T(8,128)(2,1)S(1)}, u32[]{:S(2)}, u32[]{:S(2)}) collective-permute-start(bf16[32,2048]{1,0:T(8,128)(2,1)S(1)} %get-tuple-element.11), channel_id=1, source_target_pairs={{0,12},{4,8},{8,4},{12,0},{1,13},{5,9},{9,5},{13,1},{2,14},{6,10},... | collective-permute-start | bytes 393224 | tf_op jit(solution)/shard_map/ppermute | solution.py:166
  160.4 8.9 %collective-permute-start.9 = (bf16[32,2048]{1,0:T(8,128)(2,1)S(1)}, bf16[32,2048]{1,0:T(8,128)(2,1)S(1)}, u32[]{:S(2)}, u32[]{:S(2)}) collective-permute-start(bf16[32,2048]{1,0:T(8,128)(2,1)S(1)} %get-tuple-element.10), channel_id=1, source_target_pairs={{0,4},{4,0},{8,12},{12,8},{1,5},{5,1},{9,13},{13,9},{2,6},{6,2},{1... | collective-permute-start | bytes 393224 | tf_op jit(solution)/shard_map/ppermute | solution.py:166
  169.5 6.0 %collective-permute-start.12 = (bf16[32,2048]{1,0:T(8,128)(2,1)S(1)}, bf16[32,2048]{1,0:T(8,128)(2,1)S(1)}, u32[]{:S(2)}, u32[]{:S(2)}) collective-permute-start(bf16[32,2048]{1,0:T(8,128)(2,1)S(1)} %get-tuple-element.7), channel_id=1, source_target_pairs={{0,4},{4,0},{8,12},{12,8},{1,5},{5,1},{9,13},{13,9},{2,6},{6,2},{1... | collective-permute-start | bytes 393224 | tf_op jit(solution)/shard_map/ppermute | solution.py:166
  172.2 11.1 %collective-permute-start.13 = (bf16[32,2048]{1,0:T(8,128)(2,1)S(1)}, bf16[32,2048]{1,0:T(8,128)(2,1)S(1)}, u32[]{:S(2)}, u32[]{:S(2)}) collective-permute-start(bf16[32,2048]{1,0:T(8,128)(2,1)S(1)} %get-tuple-element.7), channel_id=1, source_target_pairs={{0,8},{4,12},{8,0},{12,4},{1,9},{5,13},{9,1},{13,5},{2,10},{6,14},... | collective-permute-start | bytes 393224 | tf_op jit(solution)/shard_map/ppermute | solution.py:166
  172.2 11.4 %collective-permute-start.14 = (bf16[32,2048]{1,0:T(8,128)(2,1)S(1)}, bf16[32,2048]{1,0:T(8,128)(2,1)S(1)}, u32[]{:S(2)}, u32[]{:S(2)}) collective-permute-start(bf16[32,2048]{1,0:T(8,128)(2,1)S(1)} %get-tuple-element.7), channel_id=1, source_target_pairs={{0,12},{4,8},{8,4},{12,0},{1,13},{5,9},{9,5},{13,1},{2,14},{6,10},... | collective-permute-start | bytes 393224 | tf_op jit(solution)/shard_map/ppermute | solution.py:166
  174.3 10.5 %collective-permute-start.15 = (bf16[32,2048]{1,0:T(8,128)(2,1)S(1)}, bf16[32,2048]{1,0:T(8,128)(2,1)S(1)}, u32[]{:S(2)}, u32[]{:S(2)}) collective-permute-start(bf16[32,2048]{1,0:T(8,128)(2,1)S(1)} %get-tuple-element.7), channel_id=1, source_target_pairs={{0,2},{2,0},{1,3},{3,1},{4,6},{6,4},{5,7},{7,5},{8,10},{10,8},{9,1... | collective-permute-start | bytes 393224 | tf_op jit(solution)/shard_map/ppermute | solution.py:166
  175.5 9.4 %collective-permute-start.16 = (bf16[32,2048]{1,0:T(8,128)(2,1)S(1)}, bf16[32,2048]{1,0:T(8,128)(2,1)S(1)}, u32[]{:S(2)}, u32[]{:S(2)}) collective-permute-start(bf16[32,2048]{1,0:T(8,128)(2,1)S(1)} %collective-permute-done.12), channel_id=1, source_target_pairs={{0,2},{2,0},{1,3},{3,1},{4,6},{6,4},{5,7},{7,5},{8,10},{10,8},{9,1... | collective-permute-start | bytes 393224 | tf_op jit(solution)/shard_map/ppermute | solution.py:166
  183.3 3.8 %collective-permute-start.17 = (bf16[32,2048]{1,0:T(8,128)(2,1)S(1)}, bf16[32,2048]{1,0:T(8,128)(2,1)S(1)}, u32[]{:S(2)}, u32[]{:S(2)}) collective-permute-start(bf16[32,2048]{1,0:T(8,128)(2,1)S(1)} %collective-permute-done.13), channel_id=1, source_target_pairs={{0,2},{2,0},{1,3},{3,1},{4,6},{6,4},{5,7},{7,5},{8,10},{10,8},{9,1... | collective-permute-start | bytes 393224 | tf_op jit(solution)/shard_map/ppermute | solution.py:166
  183.5 5.3 %collective-permute-start.18 = (bf16[32,2048]{1,0:T(8,128)(2,1)S(1)}, bf16[32,2048]{1,0:T(8,128)(2,1)S(1)}, u32[]{:S(2)}, u32[]{:S(2)}) collective-permute-start(bf16[32,2048]{1,0:T(8,128)(2,1)S(1)} %collective-permute-done.14), channel_id=1, source_target_pairs={{0,2},{2,0},{1,3},{3,1},{4,6},{6,4},{5,7},{7,5},{8,10},{10,8},{9,1... | collective-permute-start | bytes 393224 | tf_op jit(solution)/shard_map/ppermute | solution.py:166
  188.8 9.1 %copy-start.9 = (s32[1,1,640]{2,1,0:T(1,128)S(1)}, s32[1,1,640]{2,1,0:T(1,128)}, u32[]{:S(2)}) copy-start(s32[1,1,640]{2,1,0:T(1,128)} %param.15) | copy-start | bytes 7684
  188.9 9.2 %copy-start.10 = (s32[1,1,640]{2,1,0:T(1,128)S(1)}, s32[1,1,640]{2,1,0:T(1,128)}, u32[]{:S(2)}) copy-start(s32[1,1,640]{2,1,0:T(1,128)} %param.14) | copy-start | bytes 7684
  188.9 9.2 %copy-start.11 = (s32[1,1,640]{2,1,0:T(1,128)S(1)}, s32[1,1,640]{2,1,0:T(1,128)}, u32[]{:S(2)}) copy-start(s32[1,1,640]{2,1,0:T(1,128)} %param.13) | copy-start | bytes 7684
  194.8 24.5 %collective-permute-start.19 = (bf16[256,4096]{0,1:T(8,128)(2,1)}, bf16[256,4096]{0,1:T(8,128)(2,1)}, u32[]{:S(2)}, u32[]{:S(2)}) collective-permute-start(bf16[256,4096]{0,1:T(8,128)(2,1)} %convolution_convert_fusion), channel_id=1, source_target_pairs={{0,1},{1,0},{2,3},{3,2},{4,5},{5,4},{6,7},{7,6},{8,9},{9,8},{10,11... | collective-permute-start | bytes 6291464 | tf_op jit(solution)/shard_map/ppermute | solution.py:175
  198.3 21.0 %copy-start.1 = (bf16[256,4096]{0,1:T(8,128)(2,1)S(1)}, bf16[256,4096]{0,1:T(8,128)(2,1)}, u32[]{:S(2)}) copy-start(bf16[256,4096]{0,1:T(8,128)(2,1)} %copy-done) | copy-start | bytes 6291460
  198.3 21.0 %copy-start.3 = (bf16[256,4096]{0,1:T(8,128)(2,1)S(1)}, bf16[256,4096]{0,1:T(8,128)(2,1)}, u32[]{:S(2)}) copy-start(bf16[256,4096]{0,1:T(8,128)(2,1)} %convolution_convert_fusion.1) | copy-start | bytes 6291460
  (4 other events, 11.5 us)

commit v2 on v1

v2 whole, which is shorter than its diff:
```python
import functools

import jax
import jax.numpy as jnp
from jax import lax
from jax.experimental import pallas as pl
from jax.experimental.pallas import tpu as pltpu
from jax.sharding import PartitionSpec as P

D = 4096
FF = 16384
BLK = 64
PAIR = 2 * BLK
SLOPE_SCALE = 0.0625
DENSIFY_VMEM = 20 * 2**20
GRADIENT_VMEM = 44 * 2**20


def swap_halves(tile):
    return jnp.concatenate([tile[:, BLK:], tile[:, :BLK]], axis=1)


def join(left, right):
    return jnp.concatenate([left[:, :BLK], right[:, BLK:]], axis=1)


def lanes(t):
    return pl.ds(pl.multiple_of(t * PAIR, PAIR), PAIR)


def largest(options, total):
    return max(n for n in options if total % n == 0)


def densify_kernel(half_cap, rows_per_step, n_cols, chunks, table, panel, out, tiles, sems):
    step = pl.program_id(0)
    share = half_cap // chunks

    @pl.when(step == 0)
    def _():
        copies = []
        for c in range(chunks):
            span = pl.ds(c * share * PAIR, share * PAIR)
            copies.append(pltpu.make_async_copy(panel.at[:, span], tiles.at[:, span], sems.at[c]))
            copies[c].start()
        tiles[:, 2 * half_cap * PAIR :] = jnp.zeros((BLK, PAIR), tiles.dtype)
        batch = largest((1, 2, 4, 5, 8), share)
        for c in range(chunks):
            copies[c].wait()

            def stage(b, carry):
                t = c * share + b * batch
                swapped = [swap_halves(tiles[:, lanes(t + u)]) for u in range(batch)]
                for u in range(batch):
                    tiles[:, lanes(half_cap + t + u)] = swapped[u]
                return carry

            lax.fori_loop(0, share // batch, stage, 0)

    def row(i, carry):
        base = (step * rows_per_step + i) * n_cols
        for p in range(n_cols // 2):
            out[pl.ds(pl.multiple_of(i * BLK, BLK), BLK), p * PAIR : (p + 1) * PAIR] = join(
                tiles[:, lanes(table[base + 2 * p])], tiles[:, lanes(table[base + 2 * p + 1])]
            )
        return carry

    lax.fori_loop(0, rows_per_step, row, 0)


def densify(panel, table):
    n_rows, n_cols = table.shape
    half_cap = panel.shape[1] // PAIR
    rows_per_step = 4
    chunks = largest((1, 2, 4), half_cap)
    return pl.pallas_call(
        functools.partial(densify_kernel, half_cap, rows_per_step, n_cols, chunks),
        grid_spec=pltpu.PrefetchScalarGridSpec(
            num_scalar_prefetch=1,
            grid=(n_rows // rows_per_step,),
            in_specs=[pl.BlockSpec(memory_space=pl.ANY)],
            out_specs=pl.BlockSpec((rows_per_step * BLK, n_cols * BLK), lambda s, *_: (s, 0)),
            scratch_shapes=[
                pltpu.VMEM((BLK, (2 * half_cap + 1) * PAIR), panel.dtype),
                pltpu.SemaphoreType.DMA((chunks,)),
            ],
        ),
        out_shape=jax.ShapeDtypeStruct((n_rows * BLK, n_cols * BLK), panel.dtype),
        compiler_params=pltpu.CompilerParams(vmem_limit_bytes=DENSIFY_VMEM),
        cost_estimate=pl.CostEstimate(
            flops=0, bytes_accessed=4 * panel.size + 4 * n_rows * n_cols * BLK * BLK, transcendentals=0
        ),
        name="densify",
    )(table.reshape(-1), panel)


def gradient_kernel(n_steps, rows_per_step, n_cols, n_rhs, picks, lhs, *refs):
    terms, (out, tiles, rows) = refs[:n_rhs], refs[n_rhs : n_rhs + 3]
    step = pl.program_id(0)
    col_pairs = n_cols // 2
    width = 2
    rhs = terms[0]
    if n_rhs == 3:
        rhs = refs[n_rhs + 3]

        @pl.when(step == 0)
        def _():
            mine, theirs, factor = terms

            def scale(j, carry):
                span = pl.ds(pl.multiple_of(j * 2 * PAIR, 2 * PAIR), 2 * PAIR)
                rhs[:, span] = ((f32(mine[:, span]) + f32(theirs[:, span])) * factor[:, span]).astype(rhs.dtype)
                return carry

            lax.fori_loop(0, col_pairs // 2, scale, 0)

    rows[...] = lhs[...].T
    for c in range(0, col_pairs, width):
        part = jnp.dot(
            rows[...], rhs[:, c * PAIR : (c + width) * PAIR], preferred_element_type=jnp.float32
        ).astype(tiles.dtype)
        for i in range(rows_per_step):
            for p in range(width):
                tiles[(step * rows_per_step + i) * col_pairs + c + p] = part[
                    i * BLK : (i + 1) * BLK, p * PAIR : (p + 1) * PAIR
                ]

    @pl.when(step == n_steps - 1)
    def _():
        tiles[n_steps * rows_per_step * col_pairs] = jnp.zeros((BLK, PAIR), tiles.dtype)

        def fetch(code):
            tile = tiles[code // 2]
            return jnp.where(code % 2 == 1, swap_halves(tile), tile)

        def pick(k, carry):
            out[:, lanes(k)] = join(fetch(picks[2 * k]), fetch(picks[2 * k + 1]))
            return carry

        pairs = out.shape[1] // PAIR
        lax.fori_loop(0, pairs, pick, 0, unroll=largest((1, 2, 5, 8), pairs))


def gradient(lhs, terms, picks):
    n_rows, n_cols = lhs.shape[1] // BLK, terms[0].shape[1] // BLK
    rows_per_step = min(16, n_rows)
    n_steps = n_rows // rows_per_step
    scratch = [
        pltpu.VMEM((n_rows * n_cols // 2 + 1, BLK, PAIR), jnp.bfloat16),
        pltpu.VMEM((rows_per_step * BLK, lhs.shape[0]), jnp.bfloat16),
    ]
    if len(terms) == 3:
        scratch.append(pltpu.VMEM(terms[0].shape, jnp.bfloat16))
    return pl.pallas_call(
        functools.partial(gradient_kernel, n_steps, rows_per_step, n_cols, len(terms)),
        grid_spec=pltpu.PrefetchScalarGridSpec(
            num_scalar_prefetch=1,
            grid=(n_steps,),
            in_specs=[pl.BlockSpec((lhs.shape[0], rows_per_step * BLK), lambda s, *_: (0, s))]
            + [pl.BlockSpec(t.shape, lambda s, *_: (0, 0)) for t in terms],
            out_specs=pl.BlockSpec((BLK, picks.shape[0] * BLK), lambda s, *_: (0, 0)),
            scratch_shapes=scratch,
        ),
        out_shape=jax.ShapeDtypeStruct((BLK, picks.shape[0] * BLK), jnp.bfloat16),
        compiler_params=pltpu.CompilerParams(vmem_limit_bytes=GRADIENT_VMEM),
        cost_estimate=pl.CostEstimate(
            flops=2 * lhs.size * terms[0].shape[1],
            bytes_accessed=2 * lhs.size + 4 * len(terms) * terms[0].size + 2 * picks.shape[0] * BLK * BLK,
            transcendentals=0,
        ),
        name="gradient",
    )(picks, lhs, *terms)


def tile_table(block_ids, row_blocks, slab_blocks, rows_are_hidden):
    cap = block_ids.shape[0]
    grid = row_blocks * slab_blocks
    slot = jnp.arange(1, cap + 1, dtype=jnp.int32)
    held = jnp.sum(
        jnp.where(block_ids[None, :] == jnp.arange(grid, dtype=jnp.int32)[:, None], slot[None, :], 0), axis=1
    )
    held = held.reshape(row_blocks, slab_blocks)
    if rows_are_hidden:
        held = held.T
    half = jnp.arange(held.shape[1], dtype=jnp.int32)[None, :] % 2
    index = held - 1
    tile = index // 2 + jnp.where(index % 2 != half, cap // 2, 0)
    return jnp.where(held > 0, tile, cap)


def pick_codes(block_ids, row_blocks, slab_blocks, rows_are_hidden):
    grid = row_blocks * slab_blocks
    row, col = block_ids // slab_blocks, block_ids % slab_blocks
    cols = slab_blocks
    if rows_are_hidden:
        row, col, cols = col, row, row_blocks
    half = jnp.arange(block_ids.shape[0], dtype=jnp.int32) % 2
    code = 2 * (row * (cols // 2) + col // 2) + jnp.where(col % 2 != half, 1, 0)
    return jnp.where(block_ids < grid, code, grid)


def shift(values, axis, k):
    n = lax.axis_size(axis)
    return values if k == 0 else lax.ppermute(values, axis, [(i, i ^ k) for i in range(n)])


def gather_near(values):
    return [shift(values, "hid", k) for k in range(lax.axis_size("hid"))]


def gather_far(near):
    far = [shift(v, "dp", j) for j in range(1, lax.axis_size("dp")) for v in near]
    return near + far


def swap_cores(values):
    return lax.ppermute(values, "col", [(0, 1), (1, 0)])


def f32(values):
    return values.astype(jnp.float32)


def whole(mine, theirs):
    return f32(mine) + f32(theirs)


def activation(gate, up):
    return (gate * jax.nn.sigmoid(gate) * up).astype(jnp.bfloat16)


def local(tokens, target, gate_panel, up_panel, down_panel, gate_list, up_list, down_list):
    n_hid, n_dp = lax.axis_size("hid"), lax.axis_size("dp")
    slab_blocks = FF // BLK // n_hid
    row_blocks = D // BLK // lax.axis_size("col")
    rows = tokens.shape[0]
    own = rows * n_hid

    gate_table = tile_table(gate_list[0, 0], row_blocks, slab_blocks, False)
    up_table = tile_table(up_list[0, 0], row_blocks, slab_blocks, False)
    down_table = tile_table(down_list[0, 0], row_blocks, slab_blocks, True)

    near = gather_near(tokens)
    gate_w = densify(gate_panel[0, 0], gate_table)
    near, gate_w = lax.optimization_barrier((near, gate_w))
    shards = gather_far(near)
    up_w = densify(up_panel[0, 0], up_table)
    shards, up_w = lax.optimization_barrier((shards, up_w))
    inputs = jnp.concatenate(shards)

    def mine(block_list):
        share = block_list.shape[-1] // n_dp
        return lax.dynamic_slice_in_dim(block_list[0, 0], lax.axis_index("dp") * share, share)

    gate_part = jnp.dot(inputs, gate_w, preferred_element_type=jnp.float32).astype(jnp.bfloat16)
    gate_other = swap_cores(gate_part)
    up_part = jnp.dot(inputs, up_w, preferred_element_type=jnp.float32).astype(jnp.bfloat16)
    up_other = swap_cores(up_part)
    down_w = densify(down_panel[0, 0], down_table)

    own_hidden = activation(whole(gate_part[:own], gate_other[:own]), whole(up_part[:own], up_other[:own]))
    out_part = jnp.dot(own_hidden, down_w, preferred_element_type=jnp.float32).astype(jnp.bfloat16)
    output = f32(out_part[:rows])
    for k in range(1, n_hid):
        output = output + f32(shift(out_part[k * rows : (k + 1) * rows], "hid", k))
    own_slope = ((output - f32(target)) * SLOPE_SCALE).astype(jnp.bfloat16)
    slope = jnp.concatenate(gather_far(gather_near(own_slope)))

    gate_part, gate_other, up_part, up_other, out_part = lax.optimization_barrier(
        (gate_part, gate_other, up_part, up_other, out_part)
    )
    gate = whole(gate_part, gate_other)
    up = whole(up_part, up_other)
    sigmoid_gate = jax.nn.sigmoid(gate)
    silu_gate = gate * sigmoid_gate
    hidden = jnp.concatenate([own_hidden, activation(gate[own:], up[own:])])
    gate_factor = up * sigmoid_gate * (1.0 + gate * (1.0 - sigmoid_gate))
    gate_codes = pick_codes(mine(gate_list), row_blocks, slab_blocks, False)
    up_codes = pick_codes(mine(up_list), row_blocks, slab_blocks, False)
    down_codes = pick_codes(mine(down_list), row_blocks, slab_blocks, True)

    back_part = lax.dot_general(
        slope, down_w, (((1,), (1,)), ((), ())), preferred_element_type=jnp.float32
    ).astype(jnp.bfloat16)
    back_other = swap_cores(back_part)
    down_grad = gradient(hidden, (slope,), down_codes)
    gate_grad = gradient(inputs, (back_part, back_other, gate_factor), gate_codes)
    up_grad = gradient(inputs, (back_part, back_other, silu_gate), up_codes)
    return gate_grad[None, None], up_grad[None, None], down_grad[None, None]


def solution(mesh):
    return jax.shard_map(
        local,
        mesh=mesh,
        in_specs=(
            P(("groups", "hid", "dp"), "col"),
            P(("groups", "hid", "dp"), "col"),
            P(("groups", "hid"), "col", None, None),
            P(("groups", "hid"), "col", None, None),
            P(("groups", "hid"), "col", None, None),
            P(("groups", "hid"), "col", None),
            P(("groups", "hid"), "col", None),
            P(("groups", "hid"), "col", None),
        ),
        out_specs=(
            P(("groups", "hid"), "col", None, "dp"),
            P(("groups", "hid"), "col", None, "dp"),
            P(("groups", "hid"), "col", None, "dp"),
        ),
        check_vma=False,
    )
```

time: 268 us -> 176 us (0.66)
  Pallas kernels: 114 us -> 64.6 us
  waiting for transfers between devices: 48.1 us -> 16.3 us
  starting transfers between devices: 34.9 us -> 27.8 us
  local copies, waits for them, and re-layouts: 17.6 us -> 12.2 us
    ppermute x17, waiting for transfers between devices: 48.1 us -> 16.3 us  [shift(): lax.ppermute(values, axis, [(i, i ^ k) for i in range(n)])]
    pallas_call x3, Pallas kernels: 59.6 us -> 31.7 us  [densify(): pl.pallas_call(functools.partial(densify_kernel, half_cap, rows_per_step,...]
    pallas_call x3, Pallas kernels: 54.5 us -> 32.9 us  [gradient(): pl.pallas_call(functools.partial(gradient_kernel, n_steps, rows_per_step,...]
    dot_general x1, matrix products: 5.92 us -> 18.3 us  [local(): lax.dot_general(slope, down_w, (((1,), (1,)), ((), ())), preferred_elemen...]
    unnamed x39, local copies, waits for them, and re-layouts: 3.04 us -> 11.5 us
    convert_element_type x2 -> x0, local copies, waits for them, and re-layouts: 8.21 us -> none  [the longest x1 4.12 us: local(): (back * up * sigmoid_gate * (1.0 + gate * (1.0 - sigmoid_gate))).astype(j...]
    ppermute x17, starting transfers between devices: 27 us -> 19 us  [shift(): lax.ppermute(values, axis, [(i, i ^ k) for i in range(n)])]
    dot_general x1, matrix products: 8.93 us -> 2.49 us  [local(): jnp.dot(own_hidden, down_w, preferred_element_type=jnp.float32)]
  transfers between devices with their start and end apart: 20 -> 20, of which waited for: 8 -> 6; matrix products, arithmetic and copies ran while one was open for 6% -> 9% of each run, Pallas kernels for 30% -> 24%
where the time goes in v2:
time: 176 us
  Pallas kernels  64.6 us (37%)
  matrix products  38 us (22%)
  starting transfers between devices  27.8 us (16%)
  waiting for transfers between devices  16.3 us (9%)
  other arithmetic  15.8 us (9%)
  local copies, waits for them, and re-layouts  12.2 us (7%)
    pallas_call x3, Pallas kernels, gradient(): pl.pallas_call(functools.partial(gradient_kernel, n_steps, rows_per_step,...  32.9 us
    pallas_call x3, Pallas kernels, densify(): pl.pallas_call(functools.partial(densify_kernel, half_cap, rows_per_step,...  31.7 us
    ppermute x17, starting transfers between devices, shift(): lax.ppermute(values, axis, [(i, i ^ k) for i in range(n)])  19 us
    dot_general x1, matrix products, local(): lax.dot_general(slope, down_w, (((1,), (1,)), ((), ())), preferred_elemen...  18.3 us
    ppermute x17, waiting for transfers between devices, shift(): lax.ppermute(values, axis, [(i, i ^ k) for i in range(n)])  16.3 us
    unnamed x39, local copies, waits for them, and re-layouts  11.5 us
    dot_general x1, matrix products, local(): jnp.dot(inputs, up_w, preferred_element_type=jnp.float32)  11.5 us
    ppermute x3, starting transfers between devices, swap_cores(): return lax.ppermute(values, 'col', [(0, 1), (1, 0)])  8.75 us
  transfers between devices with their start and end apart: 20, of which 6 were waited for; matrix products, arithmetic and copies ran while one was open for 9% of the time, Pallas kernels for 24%

profile of v2, /device:TPU:1, one launch (start us, length us, event | category | flops | bytes accessed | tf_op | source)
XLA Modules:
  0.0 175.8 jit_solution(5712012309748519132)
XLA Ops:
  0.6 2.2 %collective-permute-start = (bf16[32,2048]{1,0:T(8,128)(2,1)}, bf16[32,2048]{1,0:T(8,128)(2,1)S(1)}, u32[]{:S(2)}, u32[]{:S(2)}) collective-permute-start(bf16[32,2048]{1,0:T(8,128)(2,1)} %param.8), channel_id=1, source_target_pairs={{0,4},{4,0},{8,12},{12,8},{1,5},{5,1},{9,13},{13,9},{2,6},{6,2},{1... | collective-permute-start | bytes 393224 | tf_op jit(solution)/shard_map/ppermute | solution.py:204
  2.8 2.3 %collective-permute-start.1 = (bf16[32,2048]{1,0:T(8,128)(2,1)}, bf16[32,2048]{1,0:T(8,128)(2,1)S(1)}, u32[]{:S(2)}, u32[]{:S(2)}) collective-permute-start(bf16[32,2048]{1,0:T(8,128)(2,1)} %param.8), channel_id=1, source_target_pairs={{0,8},{4,12},{8,0},{12,4},{1,9},{5,13},{9,1},{13,5},{2,10},{6,14},... | collective-permute-start | bytes 393224 | tf_op jit(solution)/shard_map/ppermute | solution.py:204
  7.3 2.0 %select_reduce_fusion = (s32[2048]{0:T(1024)S(1)}, s32[2048]{0:T(1024)S(1)}, s32[2048]{0:T(1024)S(1)}) fusion(s32[640]{0:T(1024)S(1)} %reduce.3, s32[640]{0:T(1024)S(1)} %iota_add_fusion, s32[640]{0:T(1024)S(1)} %reduce.2, s32[640]{0:T(1024)S(1)} %reduce.1), kind=kLoop, calls=%fused_computation | loop fusion | flops 11790336 | bytes 34816 | tf_op jit(solution)/shard_map/reduce_sum | solution.py:179
  9.3 2.5 %copy-done.2 = bf16[1,1,64,40960]{3,2,1,0:T(8,128)(2,1)S(1)} copy-done((bf16[1,1,64,40960]{3,2,1,0:T(8,128)(2,1)S(1)}, bf16[1,1,64,40960]{3,2,1,0:T(8,128)(2,1)}, u32[]{:S(2)}) %copy-start.2) | copy-done | bytes 5242904
  11.8 10.6 %densify.3 = bf16[2048,4096]{1,0:T(8,128)(2,1)S(1)} custom-call(s32[2048]{0:T(1024)S(1)} %get-tuple-element.52.table, bf16[64,40960]{1,0:T(8,128)(2,1)S(1)} %bitcast.32), custom_call_target="tpu_custom_call" | custom-call | bytes 44040192 | tf_op jit(solution)/shard_map/densify/pallas_call | solution.py:76
  22.5 1.3 collective-permute-start.3
  24.0 1.2 collective-permute-start.5
  25.5 10.4 %densify.4 = bf16[2048,4096]{1,0:T(8,128)(2,1)S(1)} custom-call(s32[2048]{0:T(1024)S(1)} %get-tuple-element.51.table, bf16[64,40960]{1,0:T(8,128)(2,1)S(1)} %bitcast.33), custom_call_target="tpu_custom_call" | custom-call | bytes 44040192 | tf_op jit(solution)/shard_map/densify/pallas_call | solution.py:76
  35.9 5.7 %copy-done.1 = bf16[2048,4096]{1,0:T(8,128)(2,1)} copy-done((bf16[2048,4096]{1,0:T(8,128)(2,1)}, bf16[2048,4096]{1,0:T(8,128)(2,1)S(1)}, u32[]{:S(2)}) %copy-start.1) | copy-done | bytes 16777240
  41.8 11.5 %convolution_convert_fusion.1 = bf16[256,4096]{1,0:T(8,128)(2,1)} fusion(bf16[256,2048]{1,0:T(8,128)(2,1)S(1)} %constant_dynamic-update-slice_fusion.lhs, bf16[2048,4096]{1,0:T(8,128)(2,1)} %copy-done.1), kind=kOutput, calls=%fused_computation.7 | convolution fusion | flops 4296015872 | bytes 19922944 | tf_op jit(solution)/shard_map/dot_general | solution.py:257
  53.3 2.4 %collective-permute-start.8 = (bf16[256,4096]{1,0:T(8,128)(2,1)}, bf16[256,4096]{1,0:T(8,128)(2,1)}, u32[]{:S(2)}, u32[]{:S(2)}) collective-permute-start(bf16[256,4096]{1,0:T(8,128)(2,1)} %convolution_convert_fusion.1), channel_id=1, source_target_pairs={{0,1},{1,0},{2,3},{3,2},{4,5},{5,4},{6,7},{7,6},{8,9},{9,8},{10,11... | collective-permute-start | bytes 6291464 | tf_op jit(solution)/shard_map/ppermute | solution.py:217
  55.7 5.7 %convolution_convert_fusion.2 = bf16[256,4096]{1,0:T(8,128)(2,1)} fusion(bf16[256,2048]{1,0:T(8,128)(2,1)S(1)} %constant_dynamic-update-slice_fusion.lhs, bf16[2048,4096]{1,0:T(8,128)(2,1)S(1)} %densify.3), kind=kOutput, calls=%fused_computation.8 | convolution fusion | flops 4296015872 | bytes 19922944 | tf_op jit(solution)/shard_map/dot_general | solution.py:255
  61.8 2.5 %copy-done.4 = bf16[1,1,64,40960]{3,2,1,0:T(8,128)(2,1)S(1)} copy-done((bf16[1,1,64,40960]{3,2,1,0:T(8,128)(2,1)S(1)}, bf16[1,1,64,40960]{3,2,1,0:T(8,128)(2,1)}, u32[]{:S(2)}) %copy-start.4) | copy-done | bytes 5242904
  64.3 10.6 %densify.5 = bf16[4096,2048]{1,0:T(8,128)(2,1)S(1)} custom-call(s32[2048]{0:T(1024)S(1)} %reshape.60.table, bf16[64,40960]{1,0:T(8,128)(2,1)S(1)} %bitcast.34), custom_call_target="tpu_custom_call" | custom-call | bytes 44040192 | tf_op jit(solution)/shard_map/densify/pallas_call | solution.py:76
  75.2 6.2 %multiply_convert_fusion = bf16[128,4096]{1,0:T(8,128)(2,1)S(1)} fusion(bf16[256,4096]{1,0:T(8,128)(2,1)} %collective-permute-done.8, bf16[256,4096]{1,0:T(8,128)(2,1)} %convolution_convert_fusion.1, bf16[256,4096]{1,0:T(8,128)(2,1)} %collective-permute-done.7, bf16[256,4096]{1,0:T(8,128)(2,1)} %convolution_convert_fusion.2), kind=kLoop, calls=%fused_computation.18 | loop fusion | flops 6291456 | bytes 5242880 | tf_op jit(solution)/shard_map/convert_element_type | solution.py:229
  81.4 2.5 %convolution_convert_fusion.3 = bf16[128,2048]{1,0:T(8,128)(2,1)S(1)} fusion(bf16[128,4096]{1,0:T(8,128)(2,1)S(1)} %multiply_convert_fusion, bf16[4096,2048]{1,0:T(8,128)(2,1)S(1)} %densify.5), kind=kOutput, calls=%fused_computation.14 | convolution fusion | flops 2147745792 | bytes 18350080 | tf_op jit(solution)/shard_map/dot_general | solution.py:262
  84.0 3.6 %collective-permute-start.11 = (bf16[32,2048]{1,0:T(8,128)(2,1)S(1)}, bf16[32,2048]{1,0:T(8,128)(2,1)S(1)}, u32[]{:S(2)}, u32[]{:S(2)}) collective-permute-start(bf16[32,2048]{1,0:T(8,128)(2,1)S(1)} %get-tuple-element.49), channel_id=1, source_target_pairs={{0,12},{4,8},{8,4},{12,0},{1,13},{5,9},{9,5},{13,1},{2,14},{6,10},... | collective-permute-start | bytes 393224 | tf_op jit(solution)/shard_map/ppermute | solution.py:204
  88.0 3.1 %collective-permute-done.11 = bf16[32,2048]{1,0:T(8,128)(2,1)S(1)} collective-permute-done((bf16[32,2048]{1,0:T(8,128)(2,1)S(1)}, bf16[32,2048]{1,0:T(8,128)(2,1)S(1)}, u32[]{:S(2)}, u32[]{:S(2)}) %collective-permute-start.11) | collective-permute-done | bytes 131104 | tf_op jit(solution)/shard_map/ppermute | solution.py:204
  91.1 6.4 %collective-permute-done.10 = bf16[32,2048]{1,0:T(8,128)(2,1)S(1)} collective-permute-done((bf16[32,2048]{1,0:T(8,128)(2,1)S(1)}, bf16[32,2048]{1,0:T(8,128)(2,1)S(1)}, u32[]{:S(2)}, u32[]{:S(2)}) %collective-permute-start.10) | collective-permute-done | bytes 131104 | tf_op jit(solution)/shard_map/ppermute | solution.py:204
  98.0 2.2 %collective-permute-start.13 = (bf16[32,2048]{1,0:T(8,128)(2,1)S(1)}, bf16[32,2048]{1,0:T(8,128)(2,1)S(1)}, u32[]{:S(2)}, u32[]{:S(2)}) collective-permute-start(bf16[32,2048]{1,0:T(8,128)(2,1)S(1)} %get-tuple-element.43), channel_id=1, source_target_pairs={{0,8},{4,12},{8,0},{12,4},{1,9},{5,13},{9,1},{13,5},{2,10},{6,14},... | collective-permute-start | bytes 393224 | tf_op jit(solution)/shard_map/ppermute | solution.py:204
  100.3 1.0 collective-permute-start.14
  101.2 1.2 collective-permute-start.15
  103.5 1.2 collective-permute-start.17
  104.7 3.1 %collective-permute-done.14 = bf16[32,2048]{1,0:T(8,128)(2,1)S(1)} collective-permute-done((bf16[32,2048]{1,0:T(8,128)(2,1)S(1)}, bf16[32,2048]{1,0:T(8,128)(2,1)S(1)}, u32[]{:S(2)}, u32[]{:S(2)}) %collective-permute-start.14) | collective-permute-done | bytes 131104 | tf_op jit(solution)/shard_map/ppermute | solution.py:204
  107.8 1.2 collective-permute-start.18
  109.7 2.4 %collective-permute-done.18 = bf16[32,2048]{1,0:T(8,128)(2,1)S(1)} collective-permute-done((bf16[32,2048]{1,0:T(8,128)(2,1)S(1)}, bf16[32,2048]{1,0:T(8,128)(2,1)S(1)}, u32[]{:S(2)}, u32[]{:S(2)}) %collective-permute-start.18) | collective-permute-done | bytes 131104 | tf_op jit(solution)/shard_map/ppermute | solution.py:204
  112.1 18.3 %convolution_convert_fusion.refs_0_ = bf16[256,4096]{1,0:T(8,128)(2,1)} fusion(bf16[256,2048]{1,0:T(8,128)(2,1)S(1)} %constant_dynamic-update-slice_fusion.8.refs_0_, bf16[4096,2048]{1,0:T(8,128)(2,1)} %copy-done), kind=kOutput, calls=%fused_computation.6 | convolution fusion | flops 4296015872 | bytes 19922944 | tf_op jit(solution)/shard_map/dot_general | solution.py:282
  130.4 6.4 %collective-permute-start.19 = (bf16[256,4096]{1,0:T(8,128)(2,1)}, bf16[256,4096]{1,0:T(8,128)(2,1)S(1)}, u32[]{:S(2)}, u32[]{:S(2)}) collective-permute-start(bf16[256,4096]{1,0:T(8,128)(2,1)} %convolution_convert_fusion.refs_0_), channel_id=1, source_target_pairs={{0,1},{1,0},{2,3},{3,2},{4,5},{5,4},{6,7},{7,6},{8,9},{9,8},{10,11... | collective-permute-start | bytes 6291464 | tf_op jit(solution)/shard_map/ppermute | solution.py:217
  136.8 4.5 %convert_add_fusion = (f32[256,4096]{1,0:T(8,128)S(1)}, f32[256,4096]{1,0:T(8,128)S(1)}, f32[256,4096]{1,0:T(8,128)S(1)}, f32[256,4096]{1,0:T(8,128)S(1)}) fusion(bf16[256,4096]{1,0:T(8,128)(2,1)} %collective-permute-done.7, bf16[256,4096]{1,0:T(8,128)(2,1)} %convolution_convert_fusion.2, bf16[256,4096]{1,0:T(8,128)(2,1)} %collective-permute-done.8, ...), kind=kLoop, calls=%fused_computation.12 | loop fusion | flops 15728640 | bytes 25165824 | tf_op jit(solution)/shard_map/add | solution.py:225
  142.8 10.6 %gradient.5 = bf16[64,20480]{1,0:T(8,128)(2,1)} custom-call(s32[320]{0:T(512)S(1)} %fusion.34.picks, bf16[256,4096]{1,0:T(8,128)(2,1)S(1)} %pad_maximum_fusion.lhs, bf16[256,2048]{1,0:T(8,128)(2,1)S(1)} %constant_dynamic-update-slice_fusion.8.refs_0_), custom_call_target="tpu_custom_call" | custom-call | flops 4294967296 | bytes 6815744 | tf_op jit(solution)/shard_map/gradient/pallas_call | solution.py:154
  153.5 11.0 %gradient.3 = bf16[64,20480]{1,0:T(8,128)(2,1)} custom-call(s32[320]{0:T(512)S(1)} %fusion.22.picks, bf16[256,2048]{1,0:T(8,128)(2,1)S(1)} %constant_dynamic-update-slice_fusion.lhs, bf16[256,4096]{1,0:T(8,128)(2,1)S(1)} %copy-done.5, bf16[256,4096]{1,0:T(8,128)(2,1)S(1)} %collective-permute-done.19.refs_1_, f32[256,4096]{1,0:T(8,128)S(1)} %get-tuple-element.45.refs_2_), custom_call_target="tpu_custom_call" | custom-call | flops 4294967296 | bytes 16252928 | tf_op jit(solution)/shard_map/gradient/pallas_call | solution.py:154
  164.5 11.3 %gradient.4 = bf16[64,20480]{1,0:T(8,128)(2,1)} custom-call(s32[320]{0:T(512)S(1)} %fusion.28.picks, bf16[256,2048]{1,0:T(8,128)(2,1)S(1)} %constant_dynamic-update-slice_fusion.lhs, bf16[256,4096]{1,0:T(8,128)(2,1)S(1)} %copy-done.5, bf16[256,4096]{1,0:T(8,128)(2,1)S(1)} %collective-permute-done.19.refs_1_, f32[256,4096]{1,0:T(8,128)S(1)} %get-tuple-element.47.refs_2_), custom_call_target="tpu_custom_call" | custom-call | flops 4294967296 | bytes 16252928 | tf_op jit(solution)/shard_map/gradient/pallas_call | solution.py:154
  (86 shorter events, 7.6 us)
Async XLA Ops:
  0.6 21.8 %collective-permute-start = (bf16[32,2048]{1,0:T(8,128)(2,1)}, bf16[32,2048]{1,0:T(8,128)(2,1)S(1)}, u32[]{:S(2)}, u32[]{:S(2)}) collective-permute-start(bf16[32,2048]{1,0:T(8,128)(2,1)} %param.8), channel_id=1, source_target_pairs={{0,4},{4,0},{8,12},{12,8},{1,5},{5,1},{9,13},{13,9},{2,6},{6,2},{1... | collective-permute-start | bytes 393224 | tf_op jit(solution)/shard_map/ppermute | solution.py:204
  2.8 19.6 %collective-permute-start.1 = (bf16[32,2048]{1,0:T(8,128)(2,1)}, bf16[32,2048]{1,0:T(8,128)(2,1)S(1)}, u32[]{:S(2)}, u32[]{:S(2)}) collective-permute-start(bf16[32,2048]{1,0:T(8,128)(2,1)} %param.8), channel_id=1, source_target_pairs={{0,8},{4,12},{8,0},{12,4},{1,9},{5,13},{9,1},{13,5},{2,10},{6,14},... | collective-permute-start | bytes 393224 | tf_op jit(solution)/shard_map/ppermute | solution.py:204
  5.1 17.3 %collective-permute-start.2 = (bf16[32,2048]{1,0:T(8,128)(2,1)}, bf16[32,2048]{1,0:T(8,128)(2,1)S(1)}, u32[]{:S(2)}, u32[]{:S(2)}) collective-permute-start(bf16[32,2048]{1,0:T(8,128)(2,1)} %param.8), channel_id=1, source_target_pairs={{0,12},{4,8},{8,4},{12,0},{1,13},{5,9},{9,5},{13,1},{2,14},{6,10},... | collective-permute-start | bytes 393224 | tf_op jit(solution)/shard_map/ppermute | solution.py:204
  9.3 2.5 %copy-start.2 = (bf16[1,1,64,40960]{3,2,1,0:T(8,128)(2,1)S(1)}, bf16[1,1,64,40960]{3,2,1,0:T(8,128)(2,1)}, u32[]{:S(2)}) copy-start(bf16[1,1,64,40960]{3,2,1,0:T(8,128)(2,1)} %param.10) | copy-start | bytes 15728644
  11.8 10.7 %copy-start.9 = (bf16[32,2048]{1,0:T(8,128)(2,1)S(1)}, bf16[32,2048]{1,0:T(8,128)(2,1)}, u32[]{:S(2)}) copy-start(bf16[32,2048]{1,0:T(8,128)(2,1)} %param.8) | copy-start | bytes 393220
  11.8 13.7 %copy-start.3 = (bf16[1,1,64,40960]{3,2,1,0:T(8,128)(2,1)S(1)}, bf16[1,1,64,40960]{3,2,1,0:T(8,128)(2,1)}, u32[]{:S(2)}) copy-start(bf16[1,1,64,40960]{3,2,1,0:T(8,128)(2,1)} %param.11) | copy-start | bytes 15728644
  22.5 19.2 %collective-permute-start.3 = (bf16[32,2048]{1,0:T(8,128)(2,1)S(1)}, bf16[32,2048]{1,0:T(8,128)(2,1)S(1)}, u32[]{:S(2)}, u32[]{:S(2)}) collective-permute-start(bf16[32,2048]{1,0:T(8,128)(2,1)S(1)} %copy-done.9), channel_id=1, source_target_pairs={{0,2},{2,0},{1,3},{3,1},{4,6},{6,4},{5,7},{7,5},{8,10},{10,8},{9,1... | collective-permute-start | bytes 393224 | tf_op jit(solution)/shard_map/ppermute | solution.py:204
  23.8 17.9 %collective-permute-start.4 = (bf16[32,2048]{1,0:T(8,128)(2,1)S(1)}, bf16[32,2048]{1,0:T(8,128)(2,1)S(1)}, u32[]{:S(2)}, u32[]{:S(2)}) collective-permute-start(bf16[32,2048]{1,0:T(8,128)(2,1)S(1)} %collective-permute-done), channel_id=1, source_target_pairs={{0,2},{2,0},{1,3},{3,1},{4,6},{6,4},{5,7},{7,5},{8,10},{10,8},{9,1... | collective-permute-start | bytes 393224 | tf_op jit(solution)/shard_map/ppermute | solution.py:204
  24.0 17.7 %collective-permute-start.5 = (bf16[32,2048]{1,0:T(8,128)(2,1)S(1)}, bf16[32,2048]{1,0:T(8,128)(2,1)S(1)}, u32[]{:S(2)}, u32[]{:S(2)}) collective-permute-start(bf16[32,2048]{1,0:T(8,128)(2,1)S(1)} %collective-permute-done.1), channel_id=1, source_target_pairs={{0,2},{2,0},{1,3},{3,1},{4,6},{6,4},{5,7},{7,5},{8,10},{10,8},{9,1... | collective-permute-start | bytes 393224 | tf_op jit(solution)/shard_map/ppermute | solution.py:204
  25.2 16.5 %collective-permute-start.6 = (bf16[32,2048]{1,0:T(8,128)(2,1)S(1)}, bf16[32,2048]{1,0:T(8,128)(2,1)S(1)}, u32[]{:S(2)}, u32[]{:S(2)}) collective-permute-start(bf16[32,2048]{1,0:T(8,128)(2,1)S(1)} %collective-permute-done.2), channel_id=1, source_target_pairs={{0,2},{2,0},{1,3},{3,1},{4,6},{6,4},{5,7},{7,5},{8,10},{10,8},{9,1... | collective-permute-start | bytes 393224 | tf_op jit(solution)/shard_map/ppermute | solution.py:204
  35.9 5.7 %copy-start.1 = (bf16[2048,4096]{1,0:T(8,128)(2,1)}, bf16[2048,4096]{1,0:T(8,128)(2,1)S(1)}, u32[]{:S(2)}) copy-start(bf16[2048,4096]{1,0:T(8,128)(2,1)S(1)} %densify.4) | copy-start | bytes 50331652
  53.3 21.9 %collective-permute-start.8 = (bf16[256,4096]{1,0:T(8,128)(2,1)}, bf16[256,4096]{1,0:T(8,128)(2,1)}, u32[]{:S(2)}, u32[]{:S(2)}) collective-permute-start(bf16[256,4096]{1,0:T(8,128)(2,1)} %convolution_convert_fusion.1), channel_id=1, source_target_pairs={{0,1},{1,0},{2,3},{3,2},{4,5},{5,4},{6,7},{7,6},{8,9},{9,8},{10,11... | collective-permute-start | bytes 6291464 | tf_op jit(solution)/shard_map/ppermute | solution.py:217
  61.4 13.8 %collective-permute-start.7 = (bf16[256,4096]{1,0:T(8,128)(2,1)}, bf16[256,4096]{1,0:T(8,128)(2,1)}, u32[]{:S(2)}, u32[]{:S(2)}) collective-permute-start(bf16[256,4096]{1,0:T(8,128)(2,1)} %convolution_convert_fusion.2), channel_id=1, source_target_pairs={{0,1},{1,0},{2,3},{3,2},{4,5},{5,4},{6,7},{7,6},{8,9},{9,8},{10,11... | collective-permute-start | bytes 6291464 | tf_op jit(solution)/shard_map/ppermute | solution.py:217
  61.8 2.5 %copy-start.4 = (bf16[1,1,64,40960]{3,2,1,0:T(8,128)(2,1)S(1)}, bf16[1,1,64,40960]{3,2,1,0:T(8,128)(2,1)}, u32[]{:S(2)}) copy-start(bf16[1,1,64,40960]{3,2,1,0:T(8,128)(2,1)} %param.12) | copy-start | bytes 15728644
  64.3 10.6 %copy-start.10 = (s32[1,1,640]{2,1,0:T(1,128)S(1)}, s32[1,1,640]{2,1,0:T(1,128)}, u32[]{:S(2)}) copy-start(s32[1,1,640]{2,1,0:T(1,128)} %param.15) | copy-start | bytes 7684
  64.3 10.8 %copy-start.11 = (s32[1,1,640]{2,1,0:T(1,128)S(1)}, s32[1,1,640]{2,1,0:T(1,128)}, u32[]{:S(2)}) copy-start(s32[1,1,640]{2,1,0:T(1,128)} %param.14) | copy-start | bytes 7684
  64.3 10.8 %copy-start.12 = (s32[1,1,640]{2,1,0:T(1,128)S(1)}, s32[1,1,640]{2,1,0:T(1,128)}, u32[]{:S(2)}) copy-start(s32[1,1,640]{2,1,0:T(1,128)} %param.13) | copy-start | bytes 7684
  75.0 9.0 %copy-start = (bf16[4096,2048]{1,0:T(8,128)(2,1)}, bf16[4096,2048]{1,0:T(8,128)(2,1)S(1)}, u32[]{:S(2)}) copy-start(bf16[4096,2048]{1,0:T(8,128)(2,1)S(1)} %densify.5) | copy-start | bytes 50331652
  81.4 2.5 %copy-start.6 = (bf16[128,4096]{1,0:T(8,128)(2,1)}, bf16[128,4096]{1,0:T(8,128)(2,1)S(1)}, u32[]{:S(2)}) copy-start(bf16[128,4096]{1,0:T(8,128)(2,1)S(1)} %multiply_convert_fusion) | copy-start | bytes 3145732
  81.4 16.0 %copy-start.8 = (bf16[32,2048]{1,0:T(8,128)(2,1)S(1)}, bf16[32,2048]{1,0:T(8,128)(2,1)}, u32[]{:S(2)}) copy-start(bf16[32,2048]{1,0:T(8,128)(2,1)} %param.9) | copy-start | bytes 393220
  84.0 7.1 %collective-permute-start.11 = (bf16[32,2048]{1,0:T(8,128)(2,1)S(1)}, bf16[32,2048]{1,0:T(8,128)(2,1)S(1)}, u32[]{:S(2)}, u32[]{:S(2)}) collective-permute-start(bf16[32,2048]{1,0:T(8,128)(2,1)S(1)} %get-tuple-element.49), channel_id=1, source_target_pairs={{0,12},{4,8},{8,4},{12,0},{1,13},{5,9},{9,5},{13,1},{2,14},{6,10},... | collective-permute-start | bytes 393224 | tf_op jit(solution)/shard_map/ppermute | solution.py:204
  87.6 9.8 %collective-permute-start.10 = (bf16[32,2048]{1,0:T(8,128)(2,1)S(1)}, bf16[32,2048]{1,0:T(8,128)(2,1)S(1)}, u32[]{:S(2)}, u32[]{:S(2)}) collective-permute-start(bf16[32,2048]{1,0:T(8,128)(2,1)S(1)} %get-tuple-element.50), channel_id=1, source_target_pairs={{0,8},{4,12},{8,0},{12,4},{1,9},{5,13},{9,1},{13,5},{2,10},{6,14},... | collective-permute-start | bytes 393224 | tf_op jit(solution)/shard_map/ppermute | solution.py:204
  87.6 9.8 %collective-permute-start.9 = (bf16[32,2048]{1,0:T(8,128)(2,1)S(1)}, bf16[32,2048]{1,0:T(8,128)(2,1)S(1)}, u32[]{:S(2)}, u32[]{:S(2)}) collective-permute-start(bf16[32,2048]{1,0:T(8,128)(2,1)S(1)} %get-tuple-element.48), channel_id=1, source_target_pairs={{0,4},{4,0},{8,12},{12,8},{1,5},{5,1},{9,13},{13,9},{2,6},{6,2},{1... | collective-permute-start | bytes 393224 | tf_op jit(solution)/shard_map/ppermute | solution.py:204
  97.5 4.9 %collective-permute-start.12 = (bf16[32,2048]{1,0:T(8,128)(2,1)S(1)}, bf16[32,2048]{1,0:T(8,128)(2,1)S(1)}, u32[]{:S(2)}, u32[]{:S(2)}) collective-permute-start(bf16[32,2048]{1,0:T(8,128)(2,1)S(1)} %get-tuple-element.43), channel_id=1, source_target_pairs={{0,4},{4,0},{8,12},{12,8},{1,5},{5,1},{9,13},{13,9},{2,6},{6,2},{1... | collective-permute-start | bytes 393224 | tf_op jit(solution)/shard_map/ppermute | solution.py:204
  98.0 5.5 %collective-permute-start.13 = (bf16[32,2048]{1,0:T(8,128)(2,1)S(1)}, bf16[32,2048]{1,0:T(8,128)(2,1)S(1)}, u32[]{:S(2)}, u32[]{:S(2)}) collective-permute-start(bf16[32,2048]{1,0:T(8,128)(2,1)S(1)} %get-tuple-element.43), channel_id=1, source_target_pairs={{0,8},{4,12},{8,0},{12,4},{1,9},{5,13},{9,1},{13,5},{2,10},{6,14},... | collective-permute-start | bytes 393224 | tf_op jit(solution)/shard_map/ppermute | solution.py:204
  100.3 7.6 %collective-permute-start.14 = (bf16[32,2048]{1,0:T(8,128)(2,1)S(1)}, bf16[32,2048]{1,0:T(8,128)(2,1)S(1)}, u32[]{:S(2)}, u32[]{:S(2)}) collective-permute-start(bf16[32,2048]{1,0:T(8,128)(2,1)S(1)} %get-tuple-element.43), channel_id=1, source_target_pairs={{0,12},{4,8},{8,4},{12,0},{1,13},{5,9},{9,5},{13,1},{2,14},{6,10},... | collective-permute-start | bytes 393224 | tf_op jit(solution)/shard_map/ppermute | solution.py:204
  101.2 7.8 %collective-permute-start.15 = (bf16[32,2048]{1,0:T(8,128)(2,1)S(1)}, bf16[32,2048]{1,0:T(8,128)(2,1)S(1)}, u32[]{:S(2)}, u32[]{:S(2)}) collective-permute-start(bf16[32,2048]{1,0:T(8,128)(2,1)S(1)} %get-tuple-element.43), channel_id=1, source_target_pairs={{0,2},{2,0},{1,3},{3,1},{4,6},{6,4},{5,7},{7,5},{8,10},{10,8},{9,1... | collective-permute-start | bytes 393224 | tf_op jit(solution)/shard_map/ppermute | solution.py:204
  102.5 6.6 %collective-permute-start.16 = (bf16[32,2048]{1,0:T(8,128)(2,1)S(1)}, bf16[32,2048]{1,0:T(8,128)(2,1)S(1)}, u32[]{:S(2)}, u32[]{:S(2)}) collective-permute-start(bf16[32,2048]{1,0:T(8,128)(2,1)S(1)} %collective-permute-done.12), channel_id=1, source_target_pairs={{0,2},{2,0},{1,3},{3,1},{4,6},{6,4},{5,7},{7,5},{8,10},{10,8},{9,1... | collective-permute-start | bytes 393224 | tf_op jit(solution)/shard_map/ppermute | solution.py:204
  103.5 6.2 %collective-permute-start.17 = (bf16[32,2048]{1,0:T(8,128)(2,1)S(1)}, bf16[32,2048]{1,0:T(8,128)(2,1)S(1)}, u32[]{:S(2)}, u32[]{:S(2)}) collective-permute-start(bf16[32,2048]{1,0:T(8,128)(2,1)S(1)} %collective-permute-done.13), channel_id=1, source_target_pairs={{0,2},{2,0},{1,3},{3,1},{4,6},{6,4},{5,7},{7,5},{8,10},{10,8},{9,1... | collective-permute-start | bytes 393224 | tf_op jit(solution)/shard_map/ppermute | solution.py:204
  107.8 4.2 %collective-permute-start.18 = (bf16[32,2048]{1,0:T(8,128)(2,1)S(1)}, bf16[32,2048]{1,0:T(8,128)(2,1)S(1)}, u32[]{:S(2)}, u32[]{:S(2)}) collective-permute-start(bf16[32,2048]{1,0:T(8,128)(2,1)S(1)} %collective-permute-done.14), channel_id=1, source_target_pairs={{0,2},{2,0},{1,3},{3,1},{4,6},{6,4},{5,7},{7,5},{8,10},{10,8},{9,1... | collective-permute-start | bytes 393224 | tf_op jit(solution)/shard_map/ppermute | solution.py:204
  130.4 23.0 %collective-permute-start.19 = (bf16[256,4096]{1,0:T(8,128)(2,1)}, bf16[256,4096]{1,0:T(8,128)(2,1)S(1)}, u32[]{:S(2)}, u32[]{:S(2)}) collective-permute-start(bf16[256,4096]{1,0:T(8,128)(2,1)} %convolution_convert_fusion.refs_0_), channel_id=1, source_target_pairs={{0,1},{1,0},{2,3},{3,2},{4,5},{5,4},{6,7},{7,6},{8,9},{9,8},{10,11... | collective-permute-start | bytes 6291464 | tf_op jit(solution)/shard_map/ppermute | solution.py:217
  142.8 10.7 %copy-start.5 = (bf16[256,4096]{1,0:T(8,128)(2,1)S(1)}, bf16[256,4096]{1,0:T(8,128)(2,1)}, u32[]{:S(2)}) copy-start(bf16[256,4096]{1,0:T(8,128)(2,1)} %convolution_convert_fusion.refs_0_) | copy-start | bytes 6291460
  (1 other events, 1.2 us)

commit v3 on v2

--- a/solution.py
+++ b/solution.py
@@ -12,7 +12,8 @@
 BLK = 64
 PAIR = 2 * BLK
 SLOPE_SCALE = 0.0625
-DENSIFY_VMEM = 20 * 2**20
+DENSIFY_VMEM = 14 * 2**20
+PRODUCT_VMEM = 14 * 2**20
 GRADIENT_VMEM = 44 * 2**20
 
 
@@ -68,17 +69,16 @@
     lax.fori_loop(0, rows_per_step, row, 0)
 
 
-def densify(panel, table):
-    n_rows, n_cols = table.shape
+def densify(panel, table, n_rows, n_cols):
     half_cap = panel.shape[1] // PAIR
-    rows_per_step = 4
+    rows_per_step = max(1, 128 // n_cols)
     chunks = largest((1, 2, 4), half_cap)
     return pl.pallas_call(
         functools.partial(densify_kernel, half_cap, rows_per_step, n_cols, chunks),
         grid_spec=pltpu.PrefetchScalarGridSpec(
             num_scalar_prefetch=1,
             grid=(n_rows // rows_per_step,),
-            in_specs=[pl.BlockSpec(memory_space=pl.ANY)],
+            in_specs=[pl.BlockSpec(memory_space=pltpu.HBM)],
             out_specs=pl.BlockSpec((rows_per_step * BLK, n_cols * BLK), lambda s, *_: (s, 0)),
             scratch_shapes=[
                 pltpu.VMEM((BLK, (2 * half_cap + 1) * PAIR), panel.dtype),
@@ -91,7 +91,7 @@
             flops=0, bytes_accessed=4 * panel.size + 4 * n_rows * n_cols * BLK * BLK, transcendentals=0
         ),
         name="densify",
-    )(table.reshape(-1), panel)
+    )(table, panel)
 
 
 def gradient_kernel(n_steps, rows_per_step, n_cols, n_rhs, picks, lhs, *refs):
@@ -172,6 +172,76 @@
     )(picks, lhs, *terms)
 
 
+def output_kernel(gate_mine, gate_theirs, up_mine, up_theirs, weights, hidden, out):
+    @pl.when(pl.program_id(0) == 0)
+    def _():
+        def act(j, carry):
+            span = pl.ds(pl.multiple_of(j * PAIR, PAIR), PAIR)
+            hidden[:, span] = activation(
+                whole(gate_mine[:, span], gate_theirs[:, span]), whole(up_mine[:, span], up_theirs[:, span])
+            )
+            return carry
+
+        lax.fori_loop(0, hidden.shape[1] // PAIR, act, 0)
+
+    out[...] = jnp.dot(hidden[...], weights[...], preferred_element_type=jnp.float32).astype(out.dtype)
+
+
+def hidden_and_output(own, partials, weights):
+    depth, width = weights.shape
+    part = min(256, width)
+    return pl.pallas_call(
+        output_kernel,
+        grid=(width // part,),
+        in_specs=[pl.BlockSpec((own, depth), lambda s: (0, 0), pipeline_mode=pl.Buffered(1))] * 4
+        + [pl.BlockSpec((depth, part), lambda s: (0, s))],
+        out_specs=[
+            pl.BlockSpec((own, depth), lambda s: (0, 0)),
+            pl.BlockSpec((own, part), lambda s: (0, s)),
+        ],
+        out_shape=[
+            jax.ShapeDtypeStruct((own, depth), jnp.bfloat16),
+            jax.ShapeDtypeStruct((own, width), jnp.bfloat16),
+        ],
+        compiler_params=pltpu.CompilerParams(vmem_limit_bytes=PRODUCT_VMEM),
+        cost_estimate=pl.CostEstimate(
+            flops=2 * own * depth * width,
+            bytes_accessed=2 * (5 * own * depth + depth * width + own * width),
+            transcendentals=own * depth,
+        ),
+        name="output",
+    )(*partials, weights)
+
+
+def back_kernel(slope, weights, out):
+    out[...] = lax.dot_general(
+        slope[...], weights[...], (((1,), (1,)), ((), ())), preferred_element_type=jnp.float32
+    ).astype(out.dtype)
+
+
+def back_product(slope, weights):
+    width, depth = weights.shape
+    rows = slope.shape[0]
+    part = min(512, width)
+    return pl.pallas_call(
+        back_kernel,
+        grid=(width // part,),
+        in_specs=[
+            pl.BlockSpec((rows, depth), lambda s: (0, 0)),
+            pl.BlockSpec((part, depth), lambda s: (s, 0)),
+        ],
+        out_specs=pl.BlockSpec((rows, part), lambda s: (0, s)),
+        out_shape=jax.ShapeDtypeStruct((rows, width), jnp.bfloat16),
+        compiler_params=pltpu.CompilerParams(vmem_limit_bytes=PRODUCT_VMEM),
+        cost_estimate=pl.CostEstimate(
+            flops=2 * rows * depth * width,
+            bytes_accessed=2 * (rows * depth + depth * width + rows * width),
+            transcendentals=0,
+        ),
+        name="back",
+    )(slope, weights)
+
+
 def tile_table(block_ids, row_blocks, slab_blocks, rows_are_hidden):
     cap = block_ids.shape[0]
     grid = row_blocks * slab_blocks
@@ -185,7 +255,7 @@
     half = jnp.arange(held.shape[1], dtype=jnp.int32)[None, :] % 2
     index = held - 1
     tile = index // 2 + jnp.where(index % 2 != half, cap // 2, 0)
-    return jnp.where(held > 0, tile, cap)
+    return jnp.where(held > 0, tile, cap).reshape(-1)
 
 
 def pick_codes(block_ids, row_blocks, slab_blocks, rows_are_hidden):
@@ -236,52 +306,59 @@
     rows = tokens.shape[0]
     own = rows * n_hid
 
-    gate_table = tile_table(gate_list[0, 0], row_blocks, slab_blocks, False)
-    up_table = tile_table(up_list[0, 0], row_blocks, slab_blocks, False)
-    down_table = tile_table(down_list[0, 0], row_blocks, slab_blocks, True)
-
-    near = gather_near(tokens)
-    gate_w = densify(gate_panel[0, 0], gate_table)
-    near, gate_w = lax.optimization_barrier((near, gate_w))
-    shards = gather_far(near)
-    up_w = densify(up_panel[0, 0], up_table)
-    shards, up_w = lax.optimization_barrier((shards, up_w))
-    inputs = jnp.concatenate(shards)
-
     def mine(block_list):
         share = block_list.shape[-1] // n_dp
         return lax.dynamic_slice_in_dim(block_list[0, 0], lax.axis_index("dp") * share, share)
 
+    tables = (
+        tile_table(gate_list[0, 0], row_blocks, slab_blocks, False),
+        tile_table(up_list[0, 0], row_blocks, slab_blocks, False),
+        tile_table(down_list[0, 0], row_blocks, slab_blocks, True),
+        pick_codes(mine(gate_list), row_blocks, slab_blocks, False),
+        pick_codes(mine(up_list), row_blocks, slab_blocks, False),
+        pick_codes(mine(down_list), row_blocks, slab_blocks, True),
+    )
+    tables, gate_panel = lax.optimization_barrier((tables, gate_panel))
+    gate_table, up_table, down_table, gate_codes, up_codes, down_codes = tables
+
+    near = gather_near(tokens)
+    gate_w = densify(gate_panel[0, 0], gate_table, row_blocks, slab_blocks)
+    near, gate_w = lax.optimization_barrier((near, gate_w))
+    inputs = jnp.concatenate(gather_far(near))
+
     gate_part = jnp.dot(inputs, gate_w, preferred_element_type=jnp.float32).astype(jnp.bfloat16)
     gate_other = swap_cores(gate_part)
+    up_table, gate_part = lax.optimization_barrier((up_table, gate_part))
+    up_w = densify(up_panel[0, 0], up_table, row_blocks, slab_blocks)
     up_part = jnp.dot(inputs, up_w, preferred_element_type=jnp.float32).astype(jnp.bfloat16)
     up_other = swap_cores(up_part)
-    down_w = densify(down_panel[0, 0], down_table)
-
-    own_hidden = activation(whole(gate_part[:own], gate_other[:own]), whole(up_part[:own], up_other[:own]))
-    out_part = jnp.dot(own_hidden, down_w, preferred_element_type=jnp.float32).astype(jnp.bfloat16)
-    output = f32(out_part[:rows])
-    for k in range(1, n_hid):
-        output = output + f32(shift(out_part[k * rows : (k + 1) * rows], "hid", k))
-    own_slope = ((output - f32(target)) * SLOPE_SCALE).astype(jnp.bfloat16)
-    slope = jnp.concatenate(gather_far(gather_near(own_slope)))
-
-    gate_part, gate_other, up_part, up_other, out_part = lax.optimization_barrier(
-        (gate_part, gate_other, up_part, up_other, out_part)
-    )
-    gate = whole(gate_part, gate_other)
-    up = whole(up_part, up_other)
+    down_w = densify(down_panel[0, 0], down_table, slab_blocks, row_blocks)
+
+    partials = (gate_part, gate_other, up_part, up_other)
+    own_hidden, out_part = hidden_and_output(own, partials, down_w)
+    sent = [out_part[k * rows : (k + 1) * rows] for k in range(n_hid)]
+    moved = [shift(sent[k], "hid", k) for k in range(n_hid)]
+
+    partials, own_hidden, out_part, down_table = lax.optimization_barrier(
+        (partials, own_hidden, out_part, down_table)
+    )
+    down_w = densify(down_panel[0, 0], down_table, slab_blocks, row_blocks)
+    gate = whole(*partials[:2])
+    up = whole(*partials[2:])
     sigmoid_gate = jax.nn.sigmoid(gate)
     silu_gate = gate * sigmoid_gate
     hidden = jnp.concatenate([own_hidden, activation(gate[own:], up[own:])])
     gate_factor = up * sigmoid_gate * (1.0 + gate * (1.0 - sigmoid_gate))
-    gate_codes = pick_codes(mine(gate_list), row_blocks, slab_blocks, False)
-    up_codes = pick_codes(mine(up_list), row_blocks, slab_blocks, False)
-    down_codes = pick_codes(mine(down_list), row_blocks, slab_blocks, True)
-
-    back_part = lax.dot_general(
-        slope, down_w, (((1,), (1,)), ((), ())), preferred_element_type=jnp.float32
-    ).astype(jnp.bfloat16)
+    moved, down_w, silu_gate, hidden, gate_factor = lax.optimization_barrier(
+        (moved, down_w, silu_gate, hidden, gate_factor)
+    )
+
+    output = f32(moved[0])
+    for k in range(1, n_hid):
+        output = output + f32(moved[k])
+    own_slope = ((output - f32(target)) * SLOPE_SCALE).astype(jnp.bfloat16)
+    slope = jnp.concatenate(gather_far(gather_near(own_slope)))
+    back_part = back_product(slope, down_w)
     back_other = swap_cores(back_part)
     down_grad = gradient(hidden, (slope,), down_codes)
     gate_grad = gradient(inputs, (back_part, back_other, gate_factor), gate_codes)

time: 176 us -> 162 us (0.920)
  matrix products: 38 us -> 10.4 us
  Pallas kernels: 64.6 us -> 89 us
  local copies, waits for them, and re-layouts: 12.2 us -> 7.13 us
  other arithmetic: 15.8 us -> 10.9 us
  starting transfers between devices: 27.8 us -> 23.2 us
  waiting for transfers between devices: 16.3 us -> 20.4 us
    dot_general x2 -> x0, matrix products: 20.8 us -> none  [the longest x1 18.3 us: local(): lax.dot_general(slope, down_w, (((1,), (1,)), ((), ())), preferred_elemen...]
    pallas_call x0 -> x2, Pallas kernels: none -> 13.7 us  [the longest x1 7.56 us: hidden_and_output(): pl.pallas_call(output_kernel, grid=(width // part,), in_specs=[pl.BlockSp...]
    pallas_call x3 -> x4, Pallas kernels: 31.7 us -> 42.5 us  [densify(): pl.pallas_call(functools.partial(densify_kernel, half_cap, rows_per_step,...]
    unnamed x39 -> x31, local copies, waits for them, and re-layouts: 11.5 us -> 5.13 us
    convert_element_type x2 -> x1, other arithmetic: 6.74 us -> 0.55 us  [activation(): return (gate * jax.nn.sigmoid(gate) * up).astype(jnp.bfloat16)]
    dot_general x1, matrix products: 11.5 us -> 5.67 us  [local(): jnp.dot(inputs, up_w, preferred_element_type=jnp.float32)]
    mul x0 -> x1, other arithmetic: none -> 4.84 us  [local(): gate_factor = up * sigmoid_gate * (1.0 + gate * (1.0 - sigmoid_gate))]
    add x1 -> x0, other arithmetic: 4.54 us -> none  [whole(): return f32(mine) + f32(theirs)]
  transfers between devices with their start and end apart: 20 -> 20, of which waited for: 6 -> 7; matrix products, arithmetic and copies ran while one was open for 9% -> 7% of each run, Pallas kernels for 24% -> 26%
where the time goes in v3:
time: 162 us
  Pallas kernels  89 us (55%)
  starting transfers between devices  23.2 us (14%)
  waiting for transfers between devices  20.4 us (13%)
  other arithmetic  10.9 us (7%)
  matrix products  10.4 us (6%)
  local copies, waits for them, and re-layouts  7.13 us (4%)
    pallas_call x4, Pallas kernels, densify(): pl.pallas_call(functools.partial(densify_kernel, half_cap, rows_per_step,...  42.5 us
    pallas_call x3, Pallas kernels, gradient(): pl.pallas_call(functools.partial(gradient_kernel, n_steps, rows_per_step,...  32.8 us
    ppermute x17, waiting for transfers between devices, shift(): lax.ppermute(values, axis, [(i, i ^ k) for i in range(n)])  20.4 us
    ppermute x17, starting transfers between devices, shift(): lax.ppermute(values, axis, [(i, i ^ k) for i in range(n)])  17.8 us
    pallas_call x1, Pallas kernels, hidden_and_output(): pl.pallas_call(output_kernel, grid=(width // part,), in_specs=[pl.BlockSp...  7.56 us
    pallas_call x1, Pallas kernels, back_product(): pl.pallas_call(back_kernel, grid=(width // part,), in_specs=[pl.BlockSpec...  6.1 us
    dot_general x1, matrix products, local(): jnp.dot(inputs, up_w, preferred_element_type=jnp.float32)  5.67 us
    ppermute x3, starting transfers between devices, swap_cores(): return lax.ppermute(values, 'col', [(0, 1), (1, 0)])  5.31 us
  transfers between devices with their start and end apart: 20, of which 7 were waited for; matrix products, arithmetic and copies ran while one was open for 7% of the time, Pallas kernels for 26%

profile of v3, /device:TPU:1, one launch (start us, length us, event | category | flops | bytes accessed | tf_op | source)
XLA Modules:
  0.0 162.0 jit_solution(12075811928467442313)
XLA Ops:
  0.6 2.2 %collective-permute-start = (bf16[32,2048]{1,0:T(8,128)(2,1)}, bf16[32,2048]{1,0:T(8,128)(2,1)S(1)}, u32[]{:S(2)}, u32[]{:S(2)}) collective-permute-start(bf16[32,2048]{1,0:T(8,128)(2,1)} %param.8), channel_id=1, source_target_pairs={{0,4},{4,0},{8,12},{12,8},{1,5},{5,1},{9,13},{13,9},{2,6},{6,2},{1... | collective-permute-start | bytes 393224 | tf_op jit(solution)/shard_map/ppermute | solution.py:274
  2.8 2.3 %collective-permute-start.1 = (bf16[32,2048]{1,0:T(8,128)(2,1)}, bf16[32,2048]{1,0:T(8,128)(2,1)S(1)}, u32[]{:S(2)}, u32[]{:S(2)}) collective-permute-start(bf16[32,2048]{1,0:T(8,128)(2,1)} %param.8), channel_id=1, source_target_pairs={{0,8},{4,12},{8,0},{12,4},{1,9},{5,13},{9,1},{13,5},{2,10},{6,14},... | collective-permute-start | bytes 393224 | tf_op jit(solution)/shard_map/ppermute | solution.py:274
  8.9 2.0 %select_reduce_fusion = (s32[2048]{0:T(1024)S(1)}, s32[2048]{0:T(1024)S(1)}, s32[2048]{0:T(1024)S(1)}) fusion(s32[640]{0:T(1024)S(1)} %reduce.2, s32[640]{0:T(1024)S(1)} %iota_add_fusion, s32[640]{0:T(1024)S(1)} %reduce.1, s32[640]{0:T(1024)S(1)} %reduce), kind=kLoop, calls=%fused_computation | loop fusion | flops 11790336 | bytes 34816 | tf_op jit(solution)/shard_map/reduce_sum | solution.py:249
  11.4 2.5 %copy-done.2 = bf16[1,1,64,40960]{3,2,1,0:T(8,128)(2,1)S(1)} copy-done((bf16[1,1,64,40960]{3,2,1,0:T(8,128)(2,1)S(1)}, bf16[1,1,64,40960]{3,2,1,0:T(8,128)(2,1)}, u32[]{:S(2)}) %copy-start.2) | copy-done | bytes 5242904
  13.9 10.7 %densify.4 = bf16[2048,4096]{1,0:T(8,128)(2,1)S(1)} custom-call(s32[2048]{0:T(1024)S(1)} %get-tuple-element.34.table, bf16[64,40960]{1,0:T(8,128)(2,1)S(1)} %bitcast.32), custom_call_target="tpu_custom_call" | custom-call | bytes 44040192 | tf_op jit(solution)/shard_map/densify/pallas_call | solution.py:76
  24.7 1.3 collective-permute-start.3
  26.2 1.3 collective-permute-start.5
  28.6 2.7 %collective-permute-done.4 = bf16[32,2048]{1,0:T(8,128)(2,1)S(1)} collective-permute-done((bf16[32,2048]{1,0:T(8,128)(2,1)S(1)}, bf16[32,2048]{1,0:T(8,128)(2,1)S(1)}, u32[]{:S(2)}, u32[]{:S(2)}) %collective-permute-start.4) | collective-permute-done | bytes 131104 | tf_op jit(solution)/shard_map/ppermute | solution.py:274
  31.3 2.8 %collective-permute-done.5 = bf16[32,2048]{1,0:T(8,128)(2,1)S(1)} collective-permute-done((bf16[32,2048]{1,0:T(8,128)(2,1)S(1)}, bf16[32,2048]{1,0:T(8,128)(2,1)S(1)}, u32[]{:S(2)}, u32[]{:S(2)}) %collective-permute-start.5) | collective-permute-done | bytes 131104 | tf_op jit(solution)/shard_map/ppermute | solution.py:274
  34.1 2.8 %collective-permute-done.6 = bf16[32,2048]{1,0:T(8,128)(2,1)S(1)} collective-permute-done((bf16[32,2048]{1,0:T(8,128)(2,1)S(1)}, bf16[32,2048]{1,0:T(8,128)(2,1)S(1)}, u32[]{:S(2)}, u32[]{:S(2)}) %collective-permute-start.6) | collective-permute-done | bytes 131104 | tf_op jit(solution)/shard_map/ppermute | solution.py:274
  36.9 4.7 %convolution_convert_fusion.1.gate_mine = bf16[256,4096]{1,0:T(8,128)(2,1)S(1)} fusion(bf16[256,2048]{1,0:T(8,128)(2,1)S(1)} %constant_dynamic-update-slice_fusion.lhs, bf16[2048,4096]{1,0:T(8,128)(2,1)S(1)} %densify.4), kind=kOutput, calls=%fused_computation.7 | convolution fusion | flops 4296015872 | bytes 19922944 | tf_op jit(solution)/shard_map/dot_general | solution.py:329
  41.7 2.5 %copy-done.3 = bf16[1,1,64,40960]{3,2,1,0:T(8,128)(2,1)S(1)} copy-done((bf16[1,1,64,40960]{3,2,1,0:T(8,128)(2,1)S(1)}, bf16[1,1,64,40960]{3,2,1,0:T(8,128)(2,1)}, u32[]{:S(2)}) %copy-start.3) | copy-done | bytes 5242904
  44.1 10.5 %densify.5 = bf16[2048,4096]{1,0:T(8,128)(2,1)S(1)} custom-call(s32[2048]{0:T(1024)S(1)} %get-tuple-element.43.table, bf16[64,40960]{1,0:T(8,128)(2,1)S(1)} %bitcast.33), custom_call_target="tpu_custom_call" | custom-call | bytes 44040192 | tf_op jit(solution)/shard_map/densify/pallas_call | solution.py:76
  54.7 5.7 %convolution_convert_fusion.up_mine = bf16[256,4096]{1,0:T(8,128)(2,1)} fusion(bf16[256,2048]{1,0:T(8,128)(2,1)S(1)} %constant_dynamic-update-slice_fusion.lhs, bf16[2048,4096]{1,0:T(8,128)(2,1)S(1)} %densify.5), kind=kOutput, calls=%fused_computation.6 | convolution fusion | flops 4296015872 | bytes 19922944 | tf_op jit(solution)/shard_map/dot_general | solution.py:333
  60.4 2.2 %collective-permute-start.8 = (bf16[256,4096]{1,0:T(8,128)(2,1)}, bf16[256,4096]{1,0:T(8,128)(2,1)S(1)}, u32[]{:S(2)}, u32[]{:S(2)}) collective-permute-start(bf16[256,4096]{1,0:T(8,128)(2,1)} %convolution_convert_fusion.up_mine), channel_id=1, source_target_pairs={{0,1},{1,0},{2,3},{3,2},{4,5},{5,4},{6,7},{7,6},{8,9},{9,8},{10,11... | collective-permute-start | bytes 6291464 | tf_op jit(solution)/shard_map/ppermute | solution.py:287
  62.5 10.6 %densify.6.weights = bf16[4096,2048]{1,0:T(8,128)(2,1)S(1)} custom-call(s32[2048]{0:T(1024)S(1)} %reshape.60.table, bf16[64,40960]{1,0:T(8,128)(2,1)S(1)} %bitcast.30), custom_call_target="tpu_custom_call" | custom-call | bytes 44040192 | tf_op jit(solution)/shard_map/densify/pallas_call | solution.py:76
  73.2 7.6 %output.1 = (bf16[128,4096]{1,0:T(8,128)(2,1)S(1)}, bf16[128,2048]{1,0:T(8,128)(2,1)S(1)}) custom-call(bf16[256,4096]{1,0:T(8,128)(2,1)S(1)} %convolution_convert_fusion.1.gate_mine, bf16[256,4096]{1,0:T(8,128)(2,1)S(1)} %collective-permute-done.7.gate_theirs, bf16[256,4096]{1,0:T(8,128)(2,1)S(1)} %copy-done, ...), custom_call_target="tpu_custom_call" | custom-call | flops 2147483648 | bytes 22544384 | tf_op jit(solution)/shard_map/output/pallas_call | solution.py:193
  80.9 1.4 collective-permute-start.10
  82.3 2.0 %collective-permute-start.11 = (bf16[32,2048]{1,0:T(8,128)(2,1)S(1)}, bf16[32,2048]{1,0:T(8,128)(2,1)S(1)}, u32[]{:S(2)}, u32[]{:S(2)}) collective-permute-start(bf16[32,2048]{1,0:T(8,128)(2,1)S(1)} %get-tuple-element.72), channel_id=1, source_target_pairs={{0,12},{4,8},{8,4},{12,0},{1,13},{5,9},{9,5},{13,1},{2,14},{6,10},... | collective-permute-start | bytes 393224 | tf_op jit(solution)/shard_map/ppermute | solution.py:274
  84.5 4.8 %add_multiply_fusion = (f32[256,4096]{1,0:T(8,128)}, f32[256,4096]{1,0:T(8,128)S(1)}, f32[256,4096]{1,0:T(8,128)S(1)}, f32[256,4096]{1,0:T(8,128)S(1)}) fusion(bf16[256,4096]{1,0:T(8,128)(2,1)} %copy-done.1, bf16[256,4096]{1,0:T(8,128)(2,1)S(1)} %copy-done, bf16[256,4096]{1,0:T(8,128)(2,1)S(1)} %collective-permute-done.7.gate_theirs, ...), kind=kLoop, calls=%fused_computation.8 | loop fusion | flops 15728640 | bytes 25165824 | tf_op jit(solution)/shard_map/mul | solution.py:351
  90.1 10.6 %densify.7.weights = bf16[4096,2048]{1,0:T(8,128)(2,1)S(1)} custom-call(s32[2048]{0:T(1024)S(1)} %reshape.60.table, bf16[64,40960]{1,0:T(8,128)(2,1)S(1)} %bitcast.31), custom_call_target="tpu_custom_call" | custom-call | bytes 44040192 | tf_op jit(solution)/shard_map/densify/pallas_call | solution.py:76
  101.8 1.3 collective-permute-start.12
  103.1 1.4 collective-permute-start.13
  105.4 1.2 collective-permute-start.15
  106.9 7.4 %collective-permute-done.13 = bf16[32,2048]{1,0:T(8,128)(2,1)S(1)} collective-permute-done((bf16[32,2048]{1,0:T(8,128)(2,1)S(1)}, bf16[32,2048]{1,0:T(8,128)(2,1)S(1)}, u32[]{:S(2)}, u32[]{:S(2)}) %collective-permute-start.13) | collective-permute-done | bytes 131104 | tf_op jit(solution)/shard_map/ppermute | solution.py:274
  115.9 2.2 %collective-permute-done.17 = bf16[32,2048]{1,0:T(8,128)(2,1)S(1)} collective-permute-done((bf16[32,2048]{1,0:T(8,128)(2,1)S(1)}, bf16[32,2048]{1,0:T(8,128)(2,1)S(1)}, u32[]{:S(2)}, u32[]{:S(2)}) %collective-permute-start.17) | collective-permute-done | bytes 131104 | tf_op jit(solution)/shard_map/ppermute | solution.py:274
  118.1 1.8 %collective-permute-done.18 = bf16[32,2048]{1,0:T(8,128)(2,1)S(1)} collective-permute-done((bf16[32,2048]{1,0:T(8,128)(2,1)S(1)}, bf16[32,2048]{1,0:T(8,128)(2,1)S(1)}, u32[]{:S(2)}, u32[]{:S(2)}) %collective-permute-start.18) | collective-permute-done | bytes 131104 | tf_op jit(solution)/shard_map/ppermute | solution.py:274
  119.9 6.1 %back.1.refs_0_ = bf16[256,4096]{1,0:T(8,128)(2,1)S(1)} custom-call(bf16[256,2048]{1,0:T(8,128)(2,1)S(1)} %constant_dynamic-update-slice_fusion.8.slope.refs_0_, bf16[4096,2048]{1,0:T(8,128)(2,1)S(1)} %densify.7.weights), custom_call_target="tpu_custom_call" | custom-call | flops 4294967296 | bytes 19922944 | tf_op jit(solution)/shard_map/back/pallas_call | solution.py:226
  126.0 3.1 %collective-permute-start.19 = (bf16[256,4096]{1,0:T(8,128)(2,1)S(1)}, bf16[256,4096]{1,0:T(8,128)(2,1)S(1)}, u32[]{:S(2)}, u32[]{:S(2)}) collective-permute-start(bf16[256,4096]{1,0:T(8,128)(2,1)S(1)} %back.1.refs_0_), channel_id=1, source_target_pairs={{0,1},{1,0},{2,3},{3,2},{4,5},{5,4},{6,7},{7,6},{8,9},{9,8},{10,11... | collective-permute-start | bytes 6291464 | tf_op jit(solution)/shard_map/ppermute | solution.py:287
  129.1 10.6 %gradient.5 = bf16[64,20480]{1,0:T(8,128)(2,1)} custom-call(s32[320]{0:T(512)S(1)} %fusion.34.picks, bf16[256,4096]{1,0:T(8,128)(2,1)S(1)} %pad_maximum_fusion.lhs, bf16[256,2048]{1,0:T(8,128)(2,1)S(1)} %constant_dynamic-update-slice_fusion.8.slope.refs_0_), custom_call_target="tpu_custom_call" | custom-call | flops 4294967296 | bytes 6815744 | tf_op jit(solution)/shard_map/gradient/pallas_call | solution.py:154
  139.8 11.2 %gradient.4 = bf16[64,20480]{1,0:T(8,128)(2,1)} custom-call(s32[320]{0:T(512)S(1)} %fusion.28.picks, bf16[256,2048]{1,0:T(8,128)(2,1)S(1)} %constant_dynamic-update-slice_fusion.lhs, bf16[256,4096]{1,0:T(8,128)(2,1)S(1)} %back.1.refs_0_, bf16[256,4096]{1,0:T(8,128)(2,1)S(1)} %collective-permute-done.19.refs_1_, f32[256,4096]{1,0:T(8,128)S(1)} %get-tuple-element.60.refs_2_), custom_call_target="tpu_custom_call" | custom-call | flops 4294967296 | bytes 16252928 | tf_op jit(solution)/shard_map/gradient/pallas_call | solution.py:154
  151.0 11.0 %gradient.3 = bf16[64,20480]{1,0:T(8,128)(2,1)} custom-call(s32[320]{0:T(512)S(1)} %fusion.22.picks, bf16[256,2048]{1,0:T(8,128)(2,1)S(1)} %constant_dynamic-update-slice_fusion.lhs, bf16[256,4096]{1,0:T(8,128)(2,1)S(1)} %back.1.refs_0_, bf16[256,4096]{1,0:T(8,128)(2,1)S(1)} %collective-permute-done.19.refs_1_, f32[256,4096]{1,0:T(8,128)S(1)} %copy-done.4), custom_call_target="tpu_custom_call" | custom-call | flops 4294967296 | bytes 16252928 | tf_op jit(solution)/shard_map/gradient/pallas_call | solution.py:154
  (79 shorter events, 10.5 us)
Async XLA Ops:
  0.6 24.0 %collective-permute-start = (bf16[32,2048]{1,0:T(8,128)(2,1)}, bf16[32,2048]{1,0:T(8,128)(2,1)S(1)}, u32[]{:S(2)}, u32[]{:S(2)}) collective-permute-start(bf16[32,2048]{1,0:T(8,128)(2,1)} %param.8), channel_id=1, source_target_pairs={{0,4},{4,0},{8,12},{12,8},{1,5},{5,1},{9,13},{13,9},{2,6},{6,2},{1... | collective-permute-start | bytes 393224 | tf_op jit(solution)/shard_map/ppermute | solution.py:274
  2.8 21.8 %collective-permute-start.1 = (bf16[32,2048]{1,0:T(8,128)(2,1)}, bf16[32,2048]{1,0:T(8,128)(2,1)S(1)}, u32[]{:S(2)}, u32[]{:S(2)}) collective-permute-start(bf16[32,2048]{1,0:T(8,128)(2,1)} %param.8), channel_id=1, source_target_pairs={{0,8},{4,12},{8,0},{12,4},{1,9},{5,13},{9,1},{13,5},{2,10},{6,14},... | collective-permute-start | bytes 393224 | tf_op jit(solution)/shard_map/ppermute | solution.py:274
  5.1 19.5 %collective-permute-start.2 = (bf16[32,2048]{1,0:T(8,128)(2,1)}, bf16[32,2048]{1,0:T(8,128)(2,1)S(1)}, u32[]{:S(2)}, u32[]{:S(2)}) collective-permute-start(bf16[32,2048]{1,0:T(8,128)(2,1)} %param.8), channel_id=1, source_target_pairs={{0,12},{4,8},{8,4},{12,0},{1,13},{5,9},{9,5},{13,1},{2,14},{6,10},... | collective-permute-start | bytes 393224 | tf_op jit(solution)/shard_map/ppermute | solution.py:274
  11.4 2.5 %copy-start.2 = (bf16[1,1,64,40960]{3,2,1,0:T(8,128)(2,1)S(1)}, bf16[1,1,64,40960]{3,2,1,0:T(8,128)(2,1)}, u32[]{:S(2)}) copy-start(bf16[1,1,64,40960]{3,2,1,0:T(8,128)(2,1)} %param.10) | copy-start | bytes 15728644
  13.9 10.8 %copy-start.6 = (bf16[32,2048]{1,0:T(8,128)(2,1)S(1)}, bf16[32,2048]{1,0:T(8,128)(2,1)}, u32[]{:S(2)}) copy-start(bf16[32,2048]{1,0:T(8,128)(2,1)} %param.8) | copy-start | bytes 393220
  24.7 3.9 %collective-permute-start.3 = (bf16[32,2048]{1,0:T(8,128)(2,1)S(1)}, bf16[32,2048]{1,0:T(8,128)(2,1)S(1)}, u32[]{:S(2)}, u32[]{:S(2)}) collective-permute-start(bf16[32,2048]{1,0:T(8,128)(2,1)S(1)} %copy-done.6), channel_id=1, source_target_pairs={{0,2},{2,0},{1,3},{3,1},{4,6},{6,4},{5,7},{7,5},{8,10},{10,8},{9,1... | collective-permute-start | bytes 393224 | tf_op jit(solution)/shard_map/ppermute | solution.py:274
  25.9 5.4 %collective-permute-start.4 = (bf16[32,2048]{1,0:T(8,128)(2,1)S(1)}, bf16[32,2048]{1,0:T(8,128)(2,1)S(1)}, u32[]{:S(2)}, u32[]{:S(2)}) collective-permute-start(bf16[32,2048]{1,0:T(8,128)(2,1)S(1)} %collective-permute-done), channel_id=1, source_target_pairs={{0,2},{2,0},{1,3},{3,1},{4,6},{6,4},{5,7},{7,5},{8,10},{10,8},{9,1... | collective-permute-start | bytes 393224 | tf_op jit(solution)/shard_map/ppermute | solution.py:274
  26.2 7.9 %collective-permute-start.5 = (bf16[32,2048]{1,0:T(8,128)(2,1)S(1)}, bf16[32,2048]{1,0:T(8,128)(2,1)S(1)}, u32[]{:S(2)}, u32[]{:S(2)}) collective-permute-start(bf16[32,2048]{1,0:T(8,128)(2,1)S(1)} %collective-permute-done.1), channel_id=1, source_target_pairs={{0,2},{2,0},{1,3},{3,1},{4,6},{6,4},{5,7},{7,5},{8,10},{10,8},{9,1... | collective-permute-start | bytes 393224 | tf_op jit(solution)/shard_map/ppermute | solution.py:274
  27.5 9.4 %collective-permute-start.6 = (bf16[32,2048]{1,0:T(8,128)(2,1)S(1)}, bf16[32,2048]{1,0:T(8,128)(2,1)S(1)}, u32[]{:S(2)}, u32[]{:S(2)}) collective-permute-start(bf16[32,2048]{1,0:T(8,128)(2,1)S(1)} %collective-permute-done.2), channel_id=1, source_target_pairs={{0,2},{2,0},{1,3},{3,1},{4,6},{6,4},{5,7},{7,5},{8,10},{10,8},{9,1... | collective-permute-start | bytes 393224 | tf_op jit(solution)/shard_map/ppermute | solution.py:274
  41.6 2.5 %copy-start.3 = (bf16[1,1,64,40960]{3,2,1,0:T(8,128)(2,1)S(1)}, bf16[1,1,64,40960]{3,2,1,0:T(8,128)(2,1)}, u32[]{:S(2)}) copy-start(bf16[1,1,64,40960]{3,2,1,0:T(8,128)(2,1)} %param.11) | copy-start | bytes 15728644
  44.1 18.4 %slice-start = ((s8[5242880]{0:T(1024)(128)(4,1)}), s8[4194304]{0:T(1024)(128)(4,1)S(1)}, s32[]{:S(2)}) async-start(s8[5242880]{0:T(1024)(128)(4,1)} %bitcast.28), calls=%async_computation | async-start | bytes 8388608
  54.7 7.9 %slice-start.1 = ((s8[5242880]{0:T(1024)(128)(4,1)}), s8[1048576]{0:T(1024)(128)(4,1)S(1)}, s32[]{:S(2)}) async-start(s8[5242880]{0:T(1024)(128)(4,1)} %bitcast.28), calls=%async_computation.1 | async-start | bytes 2097152
  60.4 12.8 %collective-permute-start.8 = (bf16[256,4096]{1,0:T(8,128)(2,1)}, bf16[256,4096]{1,0:T(8,128)(2,1)S(1)}, u32[]{:S(2)}, u32[]{:S(2)}) collective-permute-start(bf16[256,4096]{1,0:T(8,128)(2,1)} %convolution_convert_fusion.up_mine), channel_id=1, source_target_pairs={{0,1},{1,0},{2,3},{3,2},{4,5},{5,4},{6,7},{7,6},{8,9},{9,8},{10,11... | collective-permute-start | bytes 6291464 | tf_op jit(solution)/shard_map/ppermute | solution.py:287
  62.5 10.7 %collective-permute-start.7 = (bf16[256,4096]{1,0:T(8,128)(2,1)S(1)}, bf16[256,4096]{1,0:T(8,128)(2,1)S(1)}, u32[]{:S(2)}, u32[]{:S(2)}) collective-permute-start(bf16[256,4096]{1,0:T(8,128)(2,1)S(1)} %convolution_convert_fusion.1.gate_mine), channel_id=1, source_target_pairs={{0,1},{1,0},{2,3},{3,2},{4,5},{5,4},{6,7},{7,6},{8,9},{9,8},{10,11... | collective-permute-start | bytes 6291464 | tf_op jit(solution)/shard_map/ppermute | solution.py:287
  62.5 10.7 %copy-start = (bf16[256,4096]{1,0:T(8,128)(2,1)S(1)}, bf16[256,4096]{1,0:T(8,128)(2,1)}, u32[]{:S(2)}) copy-start(bf16[256,4096]{1,0:T(8,128)(2,1)} %convolution_convert_fusion.up_mine) | copy-start | bytes 6291460
  73.2 7.6 %copy-start.1 = (bf16[256,4096]{1,0:T(8,128)(2,1)}, bf16[256,4096]{1,0:T(8,128)(2,1)S(1)}, u32[]{:S(2)}) copy-start(bf16[256,4096]{1,0:T(8,128)(2,1)S(1)} %collective-permute-done.8.up_theirs) | copy-start | bytes 6291460
  80.9 19.9 %collective-permute-start.10 = (bf16[32,2048]{1,0:T(8,128)(2,1)S(1)}, bf16[32,2048]{1,0:T(8,128)(2,1)S(1)}, u32[]{:S(2)}, u32[]{:S(2)}) collective-permute-start(bf16[32,2048]{1,0:T(8,128)(2,1)S(1)} %get-tuple-element.73), channel_id=1, source_target_pairs={{0,8},{4,12},{8,0},{12,4},{1,9},{5,13},{9,1},{13,5},{2,10},{6,14},... | collective-permute-start | bytes 393224 | tf_op jit(solution)/shard_map/ppermute | solution.py:274
  82.3 18.5 %collective-permute-start.11 = (bf16[32,2048]{1,0:T(8,128)(2,1)S(1)}, bf16[32,2048]{1,0:T(8,128)(2,1)S(1)}, u32[]{:S(2)}, u32[]{:S(2)}) collective-permute-start(bf16[32,2048]{1,0:T(8,128)(2,1)S(1)} %get-tuple-element.72), channel_id=1, source_target_pairs={{0,12},{4,8},{8,4},{12,0},{1,13},{5,9},{9,5},{13,1},{2,14},{6,10},... | collective-permute-start | bytes 393224 | tf_op jit(solution)/shard_map/ppermute | solution.py:274
  84.2 16.5 %collective-permute-start.9 = (bf16[32,2048]{1,0:T(8,128)(2,1)S(1)}, bf16[32,2048]{1,0:T(8,128)(2,1)}, u32[]{:S(2)}, u32[]{:S(2)}) collective-permute-start(bf16[32,2048]{1,0:T(8,128)(2,1)S(1)} %get-tuple-element.74), channel_id=1, source_target_pairs={{0,4},{4,0},{8,12},{12,8},{1,5},{5,1},{9,13},{13,9},{2,6},{6,2},{1... | collective-permute-start | bytes 393224 | tf_op jit(solution)/shard_map/ppermute | solution.py:274
  90.1 10.7 %copy-start.5 = (bf16[32,2048]{1,0:T(8,128)(2,1)S(1)}, bf16[32,2048]{1,0:T(8,128)(2,1)}, u32[]{:S(2)}) copy-start(bf16[32,2048]{1,0:T(8,128)(2,1)} %param.9) | copy-start | bytes 393220
  101.8 4.8 %collective-permute-start.12 = (bf16[32,2048]{1,0:T(8,128)(2,1)S(1)}, bf16[32,2048]{1,0:T(8,128)(2,1)S(1)}, u32[]{:S(2)}, u32[]{:S(2)}) collective-permute-start(bf16[32,2048]{1,0:T(8,128)(2,1)S(1)} %get-tuple-element.67), channel_id=1, source_target_pairs={{0,4},{4,0},{8,12},{12,8},{1,5},{5,1},{9,13},{13,9},{2,6},{6,2},{1... | collective-permute-start | bytes 393224 | tf_op jit(solution)/shard_map/ppermute | solution.py:274
  103.1 11.1 %collective-permute-start.13 = (bf16[32,2048]{1,0:T(8,128)(2,1)S(1)}, bf16[32,2048]{1,0:T(8,128)(2,1)S(1)}, u32[]{:S(2)}, u32[]{:S(2)}) collective-permute-start(bf16[32,2048]{1,0:T(8,128)(2,1)S(1)} %get-tuple-element.67), channel_id=1, source_target_pairs={{0,8},{4,12},{8,0},{12,4},{1,9},{5,13},{9,1},{13,5},{2,10},{6,14},... | collective-permute-start | bytes 393224 | tf_op jit(solution)/shard_map/ppermute | solution.py:274
  104.5 11.0 %collective-permute-start.14 = (bf16[32,2048]{1,0:T(8,128)(2,1)S(1)}, bf16[32,2048]{1,0:T(8,128)(2,1)S(1)}, u32[]{:S(2)}, u32[]{:S(2)}) collective-permute-start(bf16[32,2048]{1,0:T(8,128)(2,1)S(1)} %get-tuple-element.67), channel_id=1, source_target_pairs={{0,12},{4,8},{8,4},{12,0},{1,13},{5,9},{9,5},{13,1},{2,14},{6,10},... | collective-permute-start | bytes 393224 | tf_op jit(solution)/shard_map/ppermute | solution.py:274
  105.4 10.4 %collective-permute-start.15 = (bf16[32,2048]{1,0:T(8,128)(2,1)S(1)}, bf16[32,2048]{1,0:T(8,128)(2,1)S(1)}, u32[]{:S(2)}, u32[]{:S(2)}) collective-permute-start(bf16[32,2048]{1,0:T(8,128)(2,1)S(1)} %get-tuple-element.67), channel_id=1, source_target_pairs={{0,2},{2,0},{1,3},{3,1},{4,6},{6,4},{5,7},{7,5},{8,10},{10,8},{9,1... | collective-permute-start | bytes 393224 | tf_op jit(solution)/shard_map/ppermute | solution.py:274
  106.6 9.2 %collective-permute-start.16 = (bf16[32,2048]{1,0:T(8,128)(2,1)S(1)}, bf16[32,2048]{1,0:T(8,128)(2,1)S(1)}, u32[]{:S(2)}, u32[]{:S(2)}) collective-permute-start(bf16[32,2048]{1,0:T(8,128)(2,1)S(1)} %collective-permute-done.12), channel_id=1, source_target_pairs={{0,2},{2,0},{1,3},{3,1},{4,6},{6,4},{5,7},{7,5},{8,10},{10,8},{9,1... | collective-permute-start | bytes 393224 | tf_op jit(solution)/shard_map/ppermute | solution.py:274
  114.2 3.8 %collective-permute-start.17 = (bf16[32,2048]{1,0:T(8,128)(2,1)S(1)}, bf16[32,2048]{1,0:T(8,128)(2,1)S(1)}, u32[]{:S(2)}, u32[]{:S(2)}) collective-permute-start(bf16[32,2048]{1,0:T(8,128)(2,1)S(1)} %collective-permute-done.13), channel_id=1, source_target_pairs={{0,2},{2,0},{1,3},{3,1},{4,6},{6,4},{5,7},{7,5},{8,10},{10,8},{9,1... | collective-permute-start | bytes 393224 | tf_op jit(solution)/shard_map/ppermute | solution.py:274
  115.5 4.4 %collective-permute-start.18 = (bf16[32,2048]{1,0:T(8,128)(2,1)S(1)}, bf16[32,2048]{1,0:T(8,128)(2,1)S(1)}, u32[]{:S(2)}, u32[]{:S(2)}) collective-permute-start(bf16[32,2048]{1,0:T(8,128)(2,1)S(1)} %collective-permute-done.14), channel_id=1, source_target_pairs={{0,2},{2,0},{1,3},{3,1},{4,6},{6,4},{5,7},{7,5},{8,10},{10,8},{9,1... | collective-permute-start | bytes 393224 | tf_op jit(solution)/shard_map/ppermute | solution.py:274
  126.0 13.8 %collective-permute-start.19 = (bf16[256,4096]{1,0:T(8,128)(2,1)S(1)}, bf16[256,4096]{1,0:T(8,128)(2,1)S(1)}, u32[]{:S(2)}, u32[]{:S(2)}) collective-permute-start(bf16[256,4096]{1,0:T(8,128)(2,1)S(1)} %back.1.refs_0_), channel_id=1, source_target_pairs={{0,1},{1,0},{2,3},{3,2},{4,5},{5,4},{6,7},{7,6},{8,9},{9,8},{10,11... | collective-permute-start | bytes 6291464 | tf_op jit(solution)/shard_map/ppermute | solution.py:287
  139.8 11.2 %copy-start.4 = (f32[256,4096]{1,0:T(8,128)S(1)}, f32[256,4096]{1,0:T(8,128)}, u32[]{:S(2)}) copy-start(f32[256,4096]{1,0:T(8,128)} %get-tuple-element.58.refs_2_) | copy-start | bytes 12582916

commit v4 on v3

--- a/solution.py
+++ b/solution.py
@@ -45,7 +45,7 @@
             copies.append(pltpu.make_async_copy(panel.at[:, span], tiles.at[:, span], sems.at[c]))
             copies[c].start()
         tiles[:, 2 * half_cap * PAIR :] = jnp.zeros((BLK, PAIR), tiles.dtype)
-        batch = largest((1, 2, 4, 5, 8), share)
+        batch = largest((1, 2, 4, 5, 8, 10, 16, 20, 40), share)
         for c in range(chunks):
             copies[c].wait()
 
@@ -91,7 +91,7 @@
             flops=0, bytes_accessed=4 * panel.size + 4 * n_rows * n_cols * BLK * BLK, transcendentals=0
         ),
         name="densify",
-    )(table, panel)
+    )(table, pltpu.with_memory_space_constraint(panel, pltpu.HBM))
 
 
 def gradient_kernel(n_steps, rows_per_step, n_cols, n_rhs, picks, lhs, *refs):
@@ -129,16 +129,23 @@
     def _():
         tiles[n_steps * rows_per_step * col_pairs] = jnp.zeros((BLK, PAIR), tiles.dtype)
 
-        def fetch(code):
-            tile = tiles[code // 2]
-            return jnp.where(code % 2 == 1, swap_halves(tile), tile)
-
-        def pick(k, carry):
-            out[:, lanes(k)] = join(fetch(picks[2 * k]), fetch(picks[2 * k + 1]))
+        def pair(first, second):
+            left, right = tiles[first >> 1], tiles[second >> 1]
+            turn_left, turn_right = (first & 1) == 1, (second & 1) == 1
+            turned = swap_halves(jnp.where(turn_left, jnp.where(turn_right, join(right, left), left), right))
+            return join(jnp.where(turn_left, turned, left), jnp.where(turn_right, turned, right))
+
+        pairs = out.shape[1] // PAIR
+        batch = largest((1, 2, 5, 8, 10, 16), pairs)
+
+        def pick(b, carry):
+            k = b * batch
+            kept = [pair(picks[2 * (k + u)], picks[2 * (k + u) + 1]) for u in range(batch)]
+            for u in range(batch):
+                out[:, lanes(k + u)] = kept[u]
             return carry
 
-        pairs = out.shape[1] // PAIR
-        lax.fori_loop(0, pairs, pick, 0, unroll=largest((1, 2, 5, 8), pairs))
+        lax.fori_loop(0, pairs // batch, pick, 0)
 
 
 def gradient(lhs, terms, picks):
@@ -176,13 +183,13 @@
     @pl.when(pl.program_id(0) == 0)
     def _():
         def act(j, carry):
-            span = pl.ds(pl.multiple_of(j * PAIR, PAIR), PAIR)
+            span = pl.ds(pl.multiple_of(j * 2 * PAIR, 2 * PAIR), 2 * PAIR)
             hidden[:, span] = activation(
                 whole(gate_mine[:, span], gate_theirs[:, span]), whole(up_mine[:, span], up_theirs[:, span])
             )
             return carry
 
-        lax.fori_loop(0, hidden.shape[1] // PAIR, act, 0)
+        lax.fori_loop(0, hidden.shape[1] // (2 * PAIR), act, 0)
 
     out[...] = jnp.dot(hidden[...], weights[...], preferred_element_type=jnp.float32).astype(out.dtype)
 
@@ -321,9 +328,8 @@
     tables, gate_panel = lax.optimization_barrier((tables, gate_panel))
     gate_table, up_table, down_table, gate_codes, up_codes, down_codes = tables
 
-    near = gather_near(tokens)
+    near, gate_table = lax.optimization_barrier((gather_near(tokens), gate_table))
     gate_w = densify(gate_panel[0, 0], gate_table, row_blocks, slab_blocks)
-    near, gate_w = lax.optimization_barrier((near, gate_w))
     inputs = jnp.concatenate(gather_far(near))
 
     gate_part = jnp.dot(inputs, gate_w, preferred_element_type=jnp.float32).astype(jnp.bfloat16)
@@ -339,18 +345,15 @@
     sent = [out_part[k * rows : (k + 1) * rows] for k in range(n_hid)]
     moved = [shift(sent[k], "hid", k) for k in range(n_hid)]
 
-    partials, own_hidden, out_part, down_table = lax.optimization_barrier(
-        (partials, own_hidden, out_part, down_table)
-    )
-    down_w = densify(down_panel[0, 0], down_table, slab_blocks, row_blocks)
+    partials, own_hidden, out_part = lax.optimization_barrier((partials, own_hidden, out_part))
     gate = whole(*partials[:2])
     up = whole(*partials[2:])
     sigmoid_gate = jax.nn.sigmoid(gate)
     silu_gate = gate * sigmoid_gate
     hidden = jnp.concatenate([own_hidden, activation(gate[own:], up[own:])])
     gate_factor = up * sigmoid_gate * (1.0 + gate * (1.0 - sigmoid_gate))
-    moved, down_w, silu_gate, hidden, gate_factor = lax.optimization_barrier(
-        (moved, down_w, silu_gate, hidden, gate_factor)
+    moved, silu_gate, hidden, gate_factor = lax.optimization_barrier(
+        (moved, silu_gate, hidden, gate_factor)
     )
 
     output = f32(moved[0])

time: 162 us -> 138 us (0.85)
  Pallas kernels: 89 us -> 70 us
  local copies, waits for them, and re-layouts: 7.13 us -> 3.11 us
  waiting for transfers between devices: 20.4 us -> 17.3 us
  other arithmetic: 10.9 us -> 13.7 us
    pallas_call x4 -> x3, Pallas kernels: 42.5 us -> 28.5 us  [densify(): pl.pallas_call(functools.partial(densify_kernel, half_cap, rows_per_step,...]
    pallas_call x3, Pallas kernels: 32.8 us -> 28.1 us  [gradient(): pl.pallas_call(functools.partial(gradient_kernel, n_steps, rows_per_step,...]
    unnamed x31 -> x19, local copies, waits for them, and re-layouts: 5.13 us -> 1.09 us
    ppermute x17, waiting for transfers between devices: 20.4 us -> 17.3 us  [shift(): lax.ppermute(values, axis, [(i, i ^ k) for i in range(n)])]
    convert_element_type x1, other arithmetic: 0.55 us -> 2.83 us  [activation(): return (gate * jax.nn.sigmoid(gate) * up).astype(jnp.bfloat16)]
  transfers between devices with their start and end apart: 20 -> 20, of which waited for: 7 -> 5; matrix products, arithmetic and copies ran while one was open for 7% -> 15% of each run, Pallas kernels for 26% -> 27%
where the time goes in v4:
time: 138 us
  Pallas kernels  70 us (51%)
  starting transfers between devices  23.5 us (17%)
  waiting for transfers between devices  17.3 us (13%)
  other arithmetic  13.7 us (10%)
  matrix products  9.49 us (7%)
  local copies, waits for them, and re-layouts  3.11 us (2%)
    pallas_call x3, Pallas kernels, densify(): pl.pallas_call(functools.partial(densify_kernel, half_cap, rows_per_step,...  28.5 us
    pallas_call x3, Pallas kernels, gradient(): pl.pallas_call(functools.partial(gradient_kernel, n_steps, rows_per_step,...  28.1 us
    ppermute x17, starting transfers between devices, shift(): lax.ppermute(values, axis, [(i, i ^ k) for i in range(n)])  19.3 us
    ppermute x17, waiting for transfers between devices, shift(): lax.ppermute(values, axis, [(i, i ^ k) for i in range(n)])  17.3 us
    pallas_call x1, Pallas kernels, hidden_and_output(): pl.pallas_call(output_kernel, grid=(width // part,), in_specs=[pl.BlockSp...  7.34 us
    mul x1, other arithmetic, local(): gate_factor = up * sigmoid_gate * (1.0 + gate * (1.0 - sigmoid_gate))  6.38 us
    pallas_call x1, Pallas kernels, back_product(): pl.pallas_call(back_kernel, grid=(width // part,), in_specs=[pl.BlockSpec...  6.06 us
    dot_general x1, matrix products, local(): jnp.dot(inputs, up_w, preferred_element_type=jnp.float32)  4.75 us
  transfers between devices with their start and end apart: 20, of which 5 were waited for; matrix products, arithmetic and copies ran while one was open for 15% of the time, Pallas kernels for 27%

profile of v4, /device:TPU:1, one launch (start us, length us, event | category | flops | bytes accessed | tf_op | source)
XLA Modules:
  0.0 138.1 jit_solution(10614136702813112812)
XLA Ops:
  0.6 3.2 %collective-permute-start.1 = (bf16[32,2048]{1,0:T(8,128)(2,1)}, bf16[32,2048]{1,0:T(8,128)(2,1)S(1)}, u32[]{:S(2)}, u32[]{:S(2)}) collective-permute-start(bf16[32,2048]{1,0:T(8,128)(2,1)} %param.8), channel_id=1, source_target_pairs={{0,8},{4,12},{8,0},{12,4},{1,9},{5,13},{9,1},{13,5},{2,10},{6,14},... | collective-permute-start | bytes 393224 | tf_op jit(solution)/shard_map/ppermute | solution.py:281
  3.8 1.3 collective-permute-start
  8.9 2.0 %select_reduce_fusion = (s32[2048]{0:T(1024)S(1)}, s32[2048]{0:T(1024)S(1)}, s32[2048]{0:T(1024)S(1)}) fusion(s32[640]{0:T(1024)S(1)} %reduce.2, s32[640]{0:T(1024)S(1)} %iota_add_fusion, s32[640]{0:T(1024)S(1)} %reduce.1, s32[640]{0:T(1024)S(1)} %reduce), kind=kLoop, calls=%fused_computation | loop fusion | flops 11790336 | bytes 34816 | tf_op jit(solution)/shard_map/reduce_sum | solution.py:256
  11.4 2.3 %collective-permute-done.2 = bf16[32,2048]{1,0:T(8,128)(2,1)S(1)} collective-permute-done((bf16[32,2048]{1,0:T(8,128)(2,1)}, bf16[32,2048]{1,0:T(8,128)(2,1)S(1)}, u32[]{:S(2)}, u32[]{:S(2)}) %collective-permute-start.2) | collective-permute-done | bytes 131104 | tf_op jit(solution)/shard_map/ppermute | solution.py:281
  13.7 1.2 collective-permute-start.3
  14.9 0.9 constant_dynamic-update-slice_fusion.7
  16.2 1.2 collective-permute-start.5
  17.7 9.6 %densify.3 = bf16[2048,4096]{1,0:T(8,128)(2,1)S(1)} custom-call(s32[2048]{0:T(1024)S(1)} %get-tuple-element.38.table, bf16[64,40960]{1,0:T(8,128)(2,1)} %bitcast.28), custom_call_target="tpu_custom_call" | custom-call | bytes 44040192 | tf_op jit(solution)/shard_map/densify/pallas_call | solution.py:76
  27.4 4.7 %convolution_convert_fusion.1.gate_mine = bf16[256,4096]{1,0:T(8,128)(2,1)S(1)} fusion(bf16[256,2048]{1,0:T(8,128)(2,1)S(1)} %constant_dynamic-update-slice_fusion.lhs, bf16[2048,4096]{1,0:T(8,128)(2,1)S(1)} %densify.3), kind=kOutput, calls=%fused_computation.7 | convolution fusion | flops 4296015872 | bytes 19922944 | tf_op jit(solution)/shard_map/dot_general | solution.py:335
  32.2 2.8 %collective-permute-start.7 = (bf16[256,4096]{1,0:T(8,128)(2,1)S(1)}, bf16[256,4096]{1,0:T(8,128)(2,1)S(1)}, u32[]{:S(2)}, u32[]{:S(2)}) collective-permute-start(bf16[256,4096]{1,0:T(8,128)(2,1)S(1)} %convolution_convert_fusion.1.gate_mine), channel_id=1, source_target_pairs={{0,1},{1,0},{2,3},{3,2},{4,5},{5,4},{6,7},{7,6},{8,9},{9,8},{10,11... | collective-permute-start | bytes 6291464 | tf_op jit(solution)/shard_map/ppermute | solution.py:294
  35.0 9.4 %densify.4 = bf16[2048,4096]{1,0:T(8,128)(2,1)S(1)} custom-call(s32[2048]{0:T(1024)S(1)} %get-tuple-element.41.table, bf16[64,40960]{1,0:T(8,128)(2,1)} %bitcast.29), custom_call_target="tpu_custom_call" | custom-call | bytes 44040192 | tf_op jit(solution)/shard_map/densify/pallas_call | solution.py:76
  44.4 4.7 %convolution_convert_fusion.up_mine = bf16[256,4096]{1,0:T(8,128)(2,1)S(1)} fusion(bf16[256,2048]{1,0:T(8,128)(2,1)S(1)} %constant_dynamic-update-slice_fusion.lhs, bf16[2048,4096]{1,0:T(8,128)(2,1)S(1)} %densify.4), kind=kOutput, calls=%fused_computation.6 | convolution fusion | flops 4296015872 | bytes 19922944 | tf_op jit(solution)/shard_map/dot_general | solution.py:339
  49.2 9.5 %densify.5.weights = bf16[4096,2048]{1,0:T(8,128)(2,1)S(1)} custom-call(s32[2048]{0:T(1024)S(1)} %reshape.60.table, bf16[64,40960]{1,0:T(8,128)(2,1)} %bitcast.30), custom_call_target="tpu_custom_call" | custom-call | bytes 44040192 | tf_op jit(solution)/shard_map/densify/pallas_call | solution.py:76
  58.8 7.3 %output.1 = (bf16[128,4096]{1,0:T(8,128)(2,1)S(1)}, bf16[128,2048]{1,0:T(8,128)(2,1)S(1)}) custom-call(bf16[256,4096]{1,0:T(8,128)(2,1)S(1)} %convolution_convert_fusion.1.gate_mine, bf16[256,4096]{1,0:T(8,128)(2,1)S(1)} %collective-permute-done.7.gate_theirs, bf16[256,4096]{1,0:T(8,128)(2,1)S(1)} %convolution_convert_fusion.up_mine, ...), custom_call_target="tpu_custom_call" | custom-call | flops 2147483648 | bytes 22544384 | tf_op jit(solution)/shard_map/output/pallas_call | solution.py:200
  66.2 2.2 %collective-permute-start.11 = (bf16[32,2048]{1,0:T(8,128)(2,1)S(1)}, bf16[32,2048]{1,0:T(8,128)(2,1)S(1)}, u32[]{:S(2)}, u32[]{:S(2)}) collective-permute-start(bf16[32,2048]{1,0:T(8,128)(2,1)S(1)} %get-tuple-element.68), channel_id=1, source_target_pairs={{0,12},{4,8},{8,4},{12,0},{1,13},{5,9},{9,5},{13,1},{2,14},{6,10},... | collective-permute-start | bytes 393224 | tf_op jit(solution)/shard_map/ppermute | solution.py:281
  68.4 1.9 %collective-permute-start.10 = (bf16[32,2048]{1,0:T(8,128)(2,1)S(1)}, bf16[32,2048]{1,0:T(8,128)(2,1)S(1)}, u32[]{:S(2)}, u32[]{:S(2)}) collective-permute-start(bf16[32,2048]{1,0:T(8,128)(2,1)S(1)} %get-tuple-element.69), channel_id=1, source_target_pairs={{0,8},{4,12},{8,0},{12,4},{1,9},{5,13},{9,1},{13,5},{2,10},{6,14},... | collective-permute-start | bytes 393224 | tf_op jit(solution)/shard_map/ppermute | solution.py:281
  70.5 6.4 %add_multiply_fusion = (f32[256,4096]{1,0:T(8,128)}, f32[256,4096]{1,0:T(8,128)}, f32[256,4096]{1,0:T(8,128)}, f32[256,4096]{1,0:T(8,128)}) fusion(bf16[256,4096]{1,0:T(8,128)(2,1)S(1)} %collective-permute-done.8.up_theirs, bf16[256,4096]{1,0:T(8,128)(2,1)S(1)} %convolution_convert_fusion.up_mine, ...), kind=kLoop, calls=%fused_computation.8 | loop fusion | flops 15728640 | bytes 25165824 | tf_op jit(solution)/shard_map/mul | solution.py:354
  76.9 2.8 %fusion.1 = bf16[128,4096]{1,0:T(8,128)(2,1)S(1)} fusion(f32[256,4096]{1,0:T(8,128)} %get-tuple-element.67, f32[256,4096]{1,0:T(8,128)} %get-tuple-element.66), kind=kLoop, calls=%fused_computation.14 | loop fusion | flops 3145728 | bytes 5242880 | tf_op jit(solution)/shard_map/convert_element_type | solution.py:306
  79.9 2.1 %collective-permute-done.10 = bf16[32,2048]{1,0:T(8,128)(2,1)S(1)} collective-permute-done((bf16[32,2048]{1,0:T(8,128)(2,1)S(1)}, bf16[32,2048]{1,0:T(8,128)(2,1)S(1)}, u32[]{:S(2)}, u32[]{:S(2)}) %collective-permute-start.10) | collective-permute-done | bytes 131104 | tf_op jit(solution)/shard_map/ppermute | solution.py:281
  82.0 2.2 %collective-permute-start.14 = (bf16[32,2048]{1,0:T(8,128)(2,1)S(1)}, bf16[32,2048]{1,0:T(8,128)(2,1)S(1)}, u32[]{:S(2)}, u32[]{:S(2)}) collective-permute-start(bf16[32,2048]{1,0:T(8,128)(2,1)S(1)} %get-tuple-element.63), channel_id=1, source_target_pairs={{0,12},{4,8},{8,4},{12,0},{1,13},{5,9},{9,5},{13,1},{2,14},{6,10},... | collective-permute-start | bytes 393224 | tf_op jit(solution)/shard_map/ppermute | solution.py:281
  84.2 1.4 %collective-permute-start.12 = (bf16[32,2048]{1,0:T(8,128)(2,1)S(1)}, bf16[32,2048]{1,0:T(8,128)(2,1)S(1)}, u32[]{:S(2)}, u32[]{:S(2)}) collective-permute-start(bf16[32,2048]{1,0:T(8,128)(2,1)S(1)} %get-tuple-element.63), channel_id=1, source_target_pairs={{0,4},{4,0},{8,12},{12,8},{1,5},{5,1},{9,13},{13,9},{2,6},{6,2},{1... | collective-permute-start | bytes 393224 | tf_op jit(solution)/shard_map/ppermute | solution.py:281
  85.6 1.2 collective-permute-start.15
  86.9 1.7 %collective-permute-done.14 = bf16[32,2048]{1,0:T(8,128)(2,1)S(1)} collective-permute-done((bf16[32,2048]{1,0:T(8,128)(2,1)S(1)}, bf16[32,2048]{1,0:T(8,128)(2,1)S(1)}, u32[]{:S(2)}, u32[]{:S(2)}) %collective-permute-start.14) | collective-permute-done | bytes 131104 | tf_op jit(solution)/shard_map/ppermute | solution.py:281
  88.5 1.2 collective-permute-start.18
  89.7 5.4 %collective-permute-done.13 = bf16[32,2048]{1,0:T(8,128)(2,1)S(1)} collective-permute-done((bf16[32,2048]{1,0:T(8,128)(2,1)S(1)}, bf16[32,2048]{1,0:T(8,128)(2,1)S(1)}, u32[]{:S(2)}, u32[]{:S(2)}) %collective-permute-start.13) | collective-permute-done | bytes 131104 | tf_op jit(solution)/shard_map/ppermute | solution.py:281
  95.1 1.2 collective-permute-start.17
  96.6 5.9 %collective-permute-done.16 = bf16[32,2048]{1,0:T(8,128)(2,1)S(1)} collective-permute-done((bf16[32,2048]{1,0:T(8,128)(2,1)S(1)}, bf16[32,2048]{1,0:T(8,128)(2,1)S(1)}, u32[]{:S(2)}, u32[]{:S(2)}) %collective-permute-start.16) | collective-permute-done | bytes 131104 | tf_op jit(solution)/shard_map/ppermute | solution.py:281
  102.6 6.1 %back.1.refs_0_ = bf16[256,4096]{1,0:T(8,128)(2,1)S(1)} custom-call(bf16[256,2048]{1,0:T(8,128)(2,1)S(1)} %constant_dynamic-update-slice_fusion.8.slope.refs_0_, bf16[4096,2048]{1,0:T(8,128)(2,1)S(1)} %densify.5.weights), custom_call_target="tpu_custom_call" | custom-call | flops 4294967296 | bytes 19922944 | tf_op jit(solution)/shard_map/back/pallas_call | solution.py:233
  108.7 1.3 collective-permute-start.19
  110.0 9.2 %gradient.5 = bf16[64,20480]{1,0:T(8,128)(2,1)} custom-call(s32[320]{0:T(512)S(1)} %fusion.34.picks, bf16[256,4096]{1,0:T(8,128)(2,1)S(1)} %pad_maximum_fusion.lhs, bf16[256,2048]{1,0:T(8,128)(2,1)S(1)} %constant_dynamic-update-slice_fusion.8.slope.refs_0_), custom_call_target="tpu_custom_call" | custom-call | flops 4294967296 | bytes 6815744 | tf_op jit(solution)/shard_map/gradient/pallas_call | solution.py:161
  119.3 9.4 %gradient.4 = bf16[64,20480]{1,0:T(8,128)(2,1)} custom-call(s32[320]{0:T(512)S(1)} %fusion.28.picks, bf16[256,2048]{1,0:T(8,128)(2,1)S(1)} %constant_dynamic-update-slice_fusion.lhs, bf16[256,4096]{1,0:T(8,128)(2,1)S(1)} %back.1.refs_0_, bf16[256,4096]{1,0:T(8,128)(2,1)S(1)} %collective-permute-done.19.refs_1_, f32[256,4096]{1,0:T(8,128)S(1)} %copy-done.1), custom_call_target="tpu_custom_call" | custom-call | flops 4294967296 | bytes 16252928 | tf_op jit(solution)/shard_map/gradient/pallas_call | solution.py:161
  128.7 9.4 %gradient.3 = bf16[64,20480]{1,0:T(8,128)(2,1)} custom-call(s32[320]{0:T(512)S(1)} %fusion.22.picks, bf16[256,2048]{1,0:T(8,128)(2,1)S(1)} %constant_dynamic-update-slice_fusion.lhs, bf16[256,4096]{1,0:T(8,128)(2,1)S(1)} %back.1.refs_0_, bf16[256,4096]{1,0:T(8,128)(2,1)S(1)} %collective-permute-done.19.refs_1_, f32[256,4096]{1,0:T(8,128)S(1)} %copy-done), custom_call_target="tpu_custom_call" | custom-call | flops 4294967296 | bytes 16252928 | tf_op jit(solution)/shard_map/gradient/pallas_call | solution.py:161
  (65 shorter events, 5.8 us)
Async XLA Ops:
  0.6 10.8 %collective-permute-start.1 = (bf16[32,2048]{1,0:T(8,128)(2,1)}, bf16[32,2048]{1,0:T(8,128)(2,1)S(1)}, u32[]{:S(2)}, u32[]{:S(2)}) collective-permute-start(bf16[32,2048]{1,0:T(8,128)(2,1)} %param.8), channel_id=1, source_target_pairs={{0,8},{4,12},{8,0},{12,4},{1,9},{5,13},{9,1},{13,5},{2,10},{6,14},... | collective-permute-start | bytes 393224 | tf_op jit(solution)/shard_map/ppermute | solution.py:281
  3.8 7.6 %collective-permute-start = (bf16[32,2048]{1,0:T(8,128)(2,1)}, bf16[32,2048]{1,0:T(8,128)(2,1)S(1)}, u32[]{:S(2)}, u32[]{:S(2)}) collective-permute-start(bf16[32,2048]{1,0:T(8,128)(2,1)} %param.8), channel_id=1, source_target_pairs={{0,4},{4,0},{8,12},{12,8},{1,5},{5,1},{9,13},{13,9},{2,6},{6,2},{1... | collective-permute-start | bytes 393224 | tf_op jit(solution)/shard_map/ppermute | solution.py:281
  5.1 8.6 %collective-permute-start.2 = (bf16[32,2048]{1,0:T(8,128)(2,1)}, bf16[32,2048]{1,0:T(8,128)(2,1)S(1)}, u32[]{:S(2)}, u32[]{:S(2)}) collective-permute-start(bf16[32,2048]{1,0:T(8,128)(2,1)} %param.8), channel_id=1, source_target_pairs={{0,12},{4,8},{8,4},{12,0},{1,13},{5,9},{9,5},{13,1},{2,14},{6,10},... | collective-permute-start | bytes 393224 | tf_op jit(solution)/shard_map/ppermute | solution.py:281
  13.7 13.6 %collective-permute-start.3 = (bf16[32,2048]{1,0:T(8,128)(2,1)}, bf16[32,2048]{1,0:T(8,128)(2,1)S(1)}, u32[]{:S(2)}, u32[]{:S(2)}) collective-permute-start(bf16[32,2048]{1,0:T(8,128)(2,1)} %param.8), channel_id=1, source_target_pairs={{0,2},{2,0},{1,3},{3,1},{4,6},{6,4},{5,7},{7,5},{8,10},{10,8},{9,1... | collective-permute-start | bytes 393224 | tf_op jit(solution)/shard_map/ppermute | solution.py:281
  15.9 11.5 %collective-permute-start.4 = (bf16[32,2048]{1,0:T(8,128)(2,1)S(1)}, bf16[32,2048]{1,0:T(8,128)(2,1)S(1)}, u32[]{:S(2)}, u32[]{:S(2)}) collective-permute-start(bf16[32,2048]{1,0:T(8,128)(2,1)S(1)} %collective-permute-done), channel_id=1, source_target_pairs={{0,2},{2,0},{1,3},{3,1},{4,6},{6,4},{5,7},{7,5},{8,10},{10,8},{9,1... | collective-permute-start | bytes 393224 | tf_op jit(solution)/shard_map/ppermute | solution.py:281
  16.2 11.2 %collective-permute-start.5 = (bf16[32,2048]{1,0:T(8,128)(2,1)S(1)}, bf16[32,2048]{1,0:T(8,128)(2,1)S(1)}, u32[]{:S(2)}, u32[]{:S(2)}) collective-permute-start(bf16[32,2048]{1,0:T(8,128)(2,1)S(1)} %collective-permute-done.1), channel_id=1, source_target_pairs={{0,2},{2,0},{1,3},{3,1},{4,6},{6,4},{5,7},{7,5},{8,10},{10,8},{9,1... | collective-permute-start | bytes 393224 | tf_op jit(solution)/shard_map/ppermute | solution.py:281
  17.4 10.0 %collective-permute-start.6 = (bf16[32,2048]{1,0:T(8,128)(2,1)S(1)}, bf16[32,2048]{1,0:T(8,128)(2,1)S(1)}, u32[]{:S(2)}, u32[]{:S(2)}) collective-permute-start(bf16[32,2048]{1,0:T(8,128)(2,1)S(1)} %collective-permute-done.2), channel_id=1, source_target_pairs={{0,2},{2,0},{1,3},{3,1},{4,6},{6,4},{5,7},{7,5},{8,10},{10,8},{9,1... | collective-permute-start | bytes 393224 | tf_op jit(solution)/shard_map/ppermute | solution.py:281
  32.2 26.6 %collective-permute-start.7 = (bf16[256,4096]{1,0:T(8,128)(2,1)S(1)}, bf16[256,4096]{1,0:T(8,128)(2,1)S(1)}, u32[]{:S(2)}, u32[]{:S(2)}) collective-permute-start(bf16[256,4096]{1,0:T(8,128)(2,1)S(1)} %convolution_convert_fusion.1.gate_mine), channel_id=1, source_target_pairs={{0,1},{1,0},{2,3},{3,2},{4,5},{5,4},{6,7},{7,6},{8,9},{9,8},{10,11... | collective-permute-start | bytes 6291464 | tf_op jit(solution)/shard_map/ppermute | solution.py:294
  49.2 9.6 %collective-permute-start.8 = (bf16[256,4096]{1,0:T(8,128)(2,1)S(1)}, bf16[256,4096]{1,0:T(8,128)(2,1)S(1)}, u32[]{:S(2)}, u32[]{:S(2)}) collective-permute-start(bf16[256,4096]{1,0:T(8,128)(2,1)S(1)} %convolution_convert_fusion.up_mine), channel_id=1, source_target_pairs={{0,1},{1,0},{2,3},{3,2},{4,5},{5,4},{6,7},{7,6},{8,9},{9,8},{10,11... | collective-permute-start | bytes 6291464 | tf_op jit(solution)/shard_map/ppermute | solution.py:294
  66.2 13.7 %collective-permute-start.11 = (bf16[32,2048]{1,0:T(8,128)(2,1)S(1)}, bf16[32,2048]{1,0:T(8,128)(2,1)S(1)}, u32[]{:S(2)}, u32[]{:S(2)}) collective-permute-start(bf16[32,2048]{1,0:T(8,128)(2,1)S(1)} %get-tuple-element.68), channel_id=1, source_target_pairs={{0,12},{4,8},{8,4},{12,0},{1,13},{5,9},{9,5},{13,1},{2,14},{6,10},... | collective-permute-start | bytes 393224 | tf_op jit(solution)/shard_map/ppermute | solution.py:281
  68.4 13.5 %collective-permute-start.10 = (bf16[32,2048]{1,0:T(8,128)(2,1)S(1)}, bf16[32,2048]{1,0:T(8,128)(2,1)S(1)}, u32[]{:S(2)}, u32[]{:S(2)}) collective-permute-start(bf16[32,2048]{1,0:T(8,128)(2,1)S(1)} %get-tuple-element.69), channel_id=1, source_target_pairs={{0,8},{4,12},{8,0},{12,4},{1,9},{5,13},{9,1},{13,5},{2,10},{6,14},... | collective-permute-start | bytes 393224 | tf_op jit(solution)/shard_map/ppermute | solution.py:281
  70.3 11.6 %collective-permute-start.9 = (bf16[32,2048]{1,0:T(8,128)(2,1)S(1)}, bf16[32,2048]{1,0:T(8,128)(2,1)S(1)}, u32[]{:S(2)}, u32[]{:S(2)}) collective-permute-start(bf16[32,2048]{1,0:T(8,128)(2,1)S(1)} %get-tuple-element.70), channel_id=1, source_target_pairs={{0,4},{4,0},{8,12},{12,8},{1,5},{5,1},{9,13},{13,9},{2,6},{6,2},{1... | collective-permute-start | bytes 393224 | tf_op jit(solution)/shard_map/ppermute | solution.py:281
  76.9 5.1 %copy-start.2 = (bf16[32,2048]{1,0:T(8,128)(2,1)S(1)}, bf16[32,2048]{1,0:T(8,128)(2,1)}, u32[]{:S(2)}) copy-start(bf16[32,2048]{1,0:T(8,128)(2,1)} %param.9) | copy-start | bytes 393220
  82.0 6.5 %collective-permute-start.14 = (bf16[32,2048]{1,0:T(8,128)(2,1)S(1)}, bf16[32,2048]{1,0:T(8,128)(2,1)S(1)}, u32[]{:S(2)}, u32[]{:S(2)}) collective-permute-start(bf16[32,2048]{1,0:T(8,128)(2,1)S(1)} %get-tuple-element.63), channel_id=1, source_target_pairs={{0,12},{4,8},{8,4},{12,0},{1,13},{5,9},{9,5},{13,1},{2,14},{6,10},... | collective-permute-start | bytes 393224 | tf_op jit(solution)/shard_map/ppermute | solution.py:281
  84.2 10.9 %collective-permute-start.13 = (bf16[32,2048]{1,0:T(8,128)(2,1)S(1)}, bf16[32,2048]{1,0:T(8,128)(2,1)S(1)}, u32[]{:S(2)}, u32[]{:S(2)}) collective-permute-start(bf16[32,2048]{1,0:T(8,128)(2,1)S(1)} %get-tuple-element.63), channel_id=1, source_target_pairs={{0,8},{4,12},{8,0},{12,4},{1,9},{5,13},{9,1},{13,5},{2,10},{6,14},... | collective-permute-start | bytes 393224 | tf_op jit(solution)/shard_map/ppermute | solution.py:281
  84.2 12.1 %collective-permute-start.12 = (bf16[32,2048]{1,0:T(8,128)(2,1)S(1)}, bf16[32,2048]{1,0:T(8,128)(2,1)S(1)}, u32[]{:S(2)}, u32[]{:S(2)}) collective-permute-start(bf16[32,2048]{1,0:T(8,128)(2,1)S(1)} %get-tuple-element.63), channel_id=1, source_target_pairs={{0,4},{4,0},{8,12},{12,8},{1,5},{5,1},{9,13},{13,9},{2,6},{6,2},{1... | collective-permute-start | bytes 393224 | tf_op jit(solution)/shard_map/ppermute | solution.py:281
  85.6 11.0 %collective-permute-start.15 = (bf16[32,2048]{1,0:T(8,128)(2,1)S(1)}, bf16[32,2048]{1,0:T(8,128)(2,1)S(1)}, u32[]{:S(2)}, u32[]{:S(2)}) collective-permute-start(bf16[32,2048]{1,0:T(8,128)(2,1)S(1)} %get-tuple-element.63), channel_id=1, source_target_pairs={{0,2},{2,0},{1,3},{3,1},{4,6},{6,4},{5,7},{7,5},{8,10},{10,8},{9,1... | collective-permute-start | bytes 393224 | tf_op jit(solution)/shard_map/ppermute | solution.py:281
  88.5 14.1 %collective-permute-start.18 = (bf16[32,2048]{1,0:T(8,128)(2,1)S(1)}, bf16[32,2048]{1,0:T(8,128)(2,1)S(1)}, u32[]{:S(2)}, u32[]{:S(2)}) collective-permute-start(bf16[32,2048]{1,0:T(8,128)(2,1)S(1)} %collective-permute-done.14), channel_id=1, source_target_pairs={{0,2},{2,0},{1,3},{3,1},{4,6},{6,4},{5,7},{7,5},{8,10},{10,8},{9,1... | collective-permute-start | bytes 393224 | tf_op jit(solution)/shard_map/ppermute | solution.py:281
  95.1 7.5 %collective-permute-start.17 = (bf16[32,2048]{1,0:T(8,128)(2,1)S(1)}, bf16[32,2048]{1,0:T(8,128)(2,1)S(1)}, u32[]{:S(2)}, u32[]{:S(2)}) collective-permute-start(bf16[32,2048]{1,0:T(8,128)(2,1)S(1)} %collective-permute-done.13), channel_id=1, source_target_pairs={{0,2},{2,0},{1,3},{3,1},{4,6},{6,4},{5,7},{7,5},{8,10},{10,8},{9,1... | collective-permute-start | bytes 393224 | tf_op jit(solution)/shard_map/ppermute | solution.py:281
  96.3 6.2 %collective-permute-start.16 = (bf16[32,2048]{1,0:T(8,128)(2,1)S(1)}, bf16[32,2048]{1,0:T(8,128)(2,1)S(1)}, u32[]{:S(2)}, u32[]{:S(2)}) collective-permute-start(bf16[32,2048]{1,0:T(8,128)(2,1)S(1)} %collective-permute-done.12), channel_id=1, source_target_pairs={{0,2},{2,0},{1,3},{3,1},{4,6},{6,4},{5,7},{7,5},{8,10},{10,8},{9,1... | collective-permute-start | bytes 393224 | tf_op jit(solution)/shard_map/ppermute | solution.py:281
  108.7 10.6 %copy-start.1 = (f32[256,4096]{1,0:T(8,128)S(1)}, f32[256,4096]{1,0:T(8,128)}, u32[]{:S(2)}) copy-start(f32[256,4096]{1,0:T(8,128)} %get-tuple-element.56.refs_2_) | copy-start | bytes 12582916
  108.7 10.6 %collective-permute-start.19 = (bf16[256,4096]{1,0:T(8,128)(2,1)S(1)}, bf16[256,4096]{1,0:T(8,128)(2,1)S(1)}, u32[]{:S(2)}, u32[]{:S(2)}) collective-permute-start(bf16[256,4096]{1,0:T(8,128)(2,1)S(1)} %back.1.refs_0_), channel_id=1, source_target_pairs={{0,1},{1,0},{2,3},{3,2},{4,5},{5,4},{6,7},{7,6},{8,9},{9,8},{10,11... | collective-permute-start | bytes 6291464 | tf_op jit(solution)/shard_map/ppermute | solution.py:294
  119.2 9.4 %copy-start = (f32[256,4096]{1,0:T(8,128)S(1)}, f32[256,4096]{1,0:T(8,128)}, u32[]{:S(2)}) copy-start(f32[256,4096]{1,0:T(8,128)} %get-tuple-element.54.refs_2_) | copy-start | bytes 12582916

commit v5 on v4

--- a/solution.py
+++ b/solution.py
@@ -14,6 +14,7 @@
 SLOPE_SCALE = 0.0625
 DENSIFY_VMEM = 14 * 2**20
 PRODUCT_VMEM = 14 * 2**20
+DEPTH_PART = 512
 GRADIENT_VMEM = 44 * 2**20
 
 
@@ -179,37 +180,41 @@
     )(picks, lhs, *terms)
 
 
-def output_kernel(gate_mine, gate_theirs, up_mine, up_theirs, weights, hidden, out):
-    @pl.when(pl.program_id(0) == 0)
-    def _():
-        def act(j, carry):
-            span = pl.ds(pl.multiple_of(j * 2 * PAIR, 2 * PAIR), 2 * PAIR)
-            hidden[:, span] = activation(
-                whole(gate_mine[:, span], gate_theirs[:, span]), whole(up_mine[:, span], up_theirs[:, span])
-            )
-            return carry
-
-        lax.fori_loop(0, hidden.shape[1] // (2 * PAIR), act, 0)
-
-    out[...] = jnp.dot(hidden[...], weights[...], preferred_element_type=jnp.float32).astype(out.dtype)
+def output_kernel(gate_mine, gate_theirs, up_mine, up_theirs, weights, hidden, out, total):
+    step = pl.program_id(0)
+    hidden[...] = activation(whole(gate_mine[...], gate_theirs[...]), whole(up_mine[...], up_theirs[...]))
+    term = jnp.dot(hidden[...], weights[...], preferred_element_type=jnp.float32)
+
+    @pl.when(step == 0)
+    def _():
+        total[...] = term
+
+    @pl.when(step > 0)
+    def _():
+        total[...] += term
+
+    @pl.when(step == pl.num_programs(0) - 1)
+    def _():
+        out[...] = total[...].astype(out.dtype)
 
 
 def hidden_and_output(own, partials, weights):
     depth, width = weights.shape
-    part = min(256, width)
+    part = min(DEPTH_PART, depth)
     return pl.pallas_call(
         output_kernel,
-        grid=(width // part,),
-        in_specs=[pl.BlockSpec((own, depth), lambda s: (0, 0), pipeline_mode=pl.Buffered(1))] * 4
-        + [pl.BlockSpec((depth, part), lambda s: (0, s))],
+        grid=(depth // part,),
+        in_specs=[pl.BlockSpec((own, part), lambda s: (0, s))] * 4
+        + [pl.BlockSpec((part, width), lambda s: (s, 0))],
         out_specs=[
-            pl.BlockSpec((own, depth), lambda s: (0, 0)),
             pl.BlockSpec((own, part), lambda s: (0, s)),
+            pl.BlockSpec((own, width), lambda s: (0, 0)),
         ],
         out_shape=[
             jax.ShapeDtypeStruct((own, depth), jnp.bfloat16),
             jax.ShapeDtypeStruct((own, width), jnp.bfloat16),
         ],
+        scratch_shapes=[pltpu.VMEM((own, width), jnp.float32)],
         compiler_params=pltpu.CompilerParams(vmem_limit_bytes=PRODUCT_VMEM),
         cost_estimate=pl.CostEstimate(
             flops=2 * own * depth * width,

time: 138 us -> 136 us (0.986)
  Pallas kernels: 70 us -> 67.9 us
    pallas_call x1, Pallas kernels: 7.34 us -> 5.25 us  [hidden_and_output(): pl.pallas_call(output_kernel, grid=(depth // part,), in_specs=[pl.BlockSp...]
  transfers between devices with their start and end apart: 20 -> 20, of which waited for: 5 -> 5; matrix products, arithmetic and copies ran while one was open for 15% -> 16% of each run, Pallas kernels for 27% -> 28%
where the time goes in v5:
time: 136 us
  Pallas kernels  67.9 us (50%)
  starting transfers between devices  23.5 us (17%)
  waiting for transfers between devices  17.3 us (13%)
  other arithmetic  13.7 us (10%)
  matrix products  9.49 us (7%)
  local copies, waits for them, and re-layouts  3.11 us (2%)
    pallas_call x3, Pallas kernels, densify(): pl.pallas_call(functools.partial(densify_kernel, half_cap, rows_per_step,...  28.5 us
    pallas_call x3, Pallas kernels, gradient(): pl.pallas_call(functools.partial(gradient_kernel, n_steps, rows_per_step,...  28.1 us
    ppermute x17, starting transfers between devices, shift(): lax.ppermute(values, axis, [(i, i ^ k) for i in range(n)])  19.3 us
    ppermute x17, waiting for transfers between devices, shift(): lax.ppermute(values, axis, [(i, i ^ k) for i in range(n)])  17.3 us
    mul x1, other arithmetic, local(): gate_factor = up * sigmoid_gate * (1.0 + gate * (1.0 - sigmoid_gate))  6.38 us
    pallas_call x1, Pallas kernels, back_product(): pl.pallas_call(back_kernel, grid=(width // part,), in_specs=[pl.BlockSpec...  6.06 us
    pallas_call x1, Pallas kernels, hidden_and_output(): pl.pallas_call(output_kernel, grid=(depth // part,), in_specs=[pl.BlockSp...  5.25 us
    dot_general x1, matrix products, local(): jnp.dot(inputs, up_w, preferred_element_type=jnp.float32)  4.75 us
  transfers between devices with their start and end apart: 20, of which 5 were waited for; matrix products, arithmetic and copies ran while one was open for 16% of the time, Pallas kernels for 28%

profile of v5, /device:TPU:1, one launch (start us, length us, event | category | flops | bytes accessed | tf_op | source)
XLA Modules:
  0.0 136.0 jit_solution(1448057460991719517)
XLA Ops:
  0.6 3.2 %collective-permute-start.1 = (bf16[32,2048]{1,0:T(8,128)(2,1)}, bf16[32,2048]{1,0:T(8,128)(2,1)S(1)}, u32[]{:S(2)}, u32[]{:S(2)}) collective-permute-start(bf16[32,2048]{1,0:T(8,128)(2,1)} %param.8), channel_id=1, source_target_pairs={{0,8},{4,12},{8,0},{12,4},{1,9},{5,13},{9,1},{13,5},{2,10},{6,14},... | collective-permute-start | bytes 393224 | tf_op jit(solution)/shard_map/ppermute | solution.py:286
  3.8 1.3 collective-permute-start
  8.9 2.0 %select_reduce_fusion = (s32[2048]{0:T(1024)S(1)}, s32[2048]{0:T(1024)S(1)}, s32[2048]{0:T(1024)S(1)}) fusion(s32[640]{0:T(1024)S(1)} %reduce.2, s32[640]{0:T(1024)S(1)} %iota_add_fusion, s32[640]{0:T(1024)S(1)} %reduce.1, s32[640]{0:T(1024)S(1)} %reduce), kind=kLoop, calls=%fused_computation | loop fusion | flops 11790336 | bytes 34816 | tf_op jit(solution)/shard_map/reduce_sum | solution.py:261
  11.4 2.3 %collective-permute-done.2 = bf16[32,2048]{1,0:T(8,128)(2,1)S(1)} collective-permute-done((bf16[32,2048]{1,0:T(8,128)(2,1)}, bf16[32,2048]{1,0:T(8,128)(2,1)S(1)}, u32[]{:S(2)}, u32[]{:S(2)}) %collective-permute-start.2) | collective-permute-done | bytes 131104 | tf_op jit(solution)/shard_map/ppermute | solution.py:286
  13.7 1.2 collective-permute-start.3
  14.9 0.9 constant_dynamic-update-slice_fusion.7
  16.2 1.2 collective-permute-start.5
  17.7 9.6 %densify.3 = bf16[2048,4096]{1,0:T(8,128)(2,1)S(1)} custom-call(s32[2048]{0:T(1024)S(1)} %get-tuple-element.38.table, bf16[64,40960]{1,0:T(8,128)(2,1)} %bitcast.28), custom_call_target="tpu_custom_call" | custom-call | bytes 44040192 | tf_op jit(solution)/shard_map/densify/pallas_call | solution.py:77
  27.4 4.7 %convolution_convert_fusion.1.gate_mine = bf16[256,4096]{1,0:T(8,128)(2,1)S(1)} fusion(bf16[256,2048]{1,0:T(8,128)(2,1)S(1)} %constant_dynamic-update-slice_fusion.lhs, bf16[2048,4096]{1,0:T(8,128)(2,1)S(1)} %densify.3), kind=kOutput, calls=%fused_computation.7 | convolution fusion | flops 4296015872 | bytes 19922944 | tf_op jit(solution)/shard_map/dot_general | solution.py:340
  32.2 2.8 %collective-permute-start.7 = (bf16[256,4096]{1,0:T(8,128)(2,1)S(1)}, bf16[256,4096]{1,0:T(8,128)(2,1)S(1)}, u32[]{:S(2)}, u32[]{:S(2)}) collective-permute-start(bf16[256,4096]{1,0:T(8,128)(2,1)S(1)} %convolution_convert_fusion.1.gate_mine), channel_id=1, source_target_pairs={{0,1},{1,0},{2,3},{3,2},{4,5},{5,4},{6,7},{7,6},{8,9},{9,8},{10,11... | collective-permute-start | bytes 6291464 | tf_op jit(solution)/shard_map/ppermute | solution.py:299
  35.0 9.4 %densify.4 = bf16[2048,4096]{1,0:T(8,128)(2,1)S(1)} custom-call(s32[2048]{0:T(1024)S(1)} %get-tuple-element.41.table, bf16[64,40960]{1,0:T(8,128)(2,1)} %bitcast.29), custom_call_target="tpu_custom_call" | custom-call | bytes 44040192 | tf_op jit(solution)/shard_map/densify/pallas_call | solution.py:77
  44.4 4.7 %convolution_convert_fusion.up_mine = bf16[256,4096]{1,0:T(8,128)(2,1)S(1)} fusion(bf16[256,2048]{1,0:T(8,128)(2,1)S(1)} %constant_dynamic-update-slice_fusion.lhs, bf16[2048,4096]{1,0:T(8,128)(2,1)S(1)} %densify.4), kind=kOutput, calls=%fused_computation.6 | convolution fusion | flops 4296015872 | bytes 19922944 | tf_op jit(solution)/shard_map/dot_general | solution.py:344
  49.2 9.5 %densify.5.weights = bf16[4096,2048]{1,0:T(8,128)(2,1)S(1)} custom-call(s32[2048]{0:T(1024)S(1)} %reshape.60.table, bf16[64,40960]{1,0:T(8,128)(2,1)} %bitcast.30), custom_call_target="tpu_custom_call" | custom-call | bytes 44040192 | tf_op jit(solution)/shard_map/densify/pallas_call | solution.py:77
  58.8 5.3 %output.1 = (bf16[128,4096]{1,0:T(8,128)(2,1)S(1)}, bf16[128,2048]{1,0:T(8,128)(2,1)S(1)}) custom-call(bf16[256,4096]{1,0:T(8,128)(2,1)S(1)} %convolution_convert_fusion.1.gate_mine, bf16[256,4096]{1,0:T(8,128)(2,1)S(1)} %collective-permute-done.7.gate_theirs, bf16[256,4096]{1,0:T(8,128)(2,1)S(1)} %convolution_convert_fusion.up_mine, ...), custom_call_target="tpu_custom_call" | custom-call | flops 2147483648 | bytes 22544384 | tf_op jit(solution)/shard_map/output/pallas_call | solution.py:204
  64.1 2.2 %collective-permute-start.11 = (bf16[32,2048]{1,0:T(8,128)(2,1)S(1)}, bf16[32,2048]{1,0:T(8,128)(2,1)S(1)}, u32[]{:S(2)}, u32[]{:S(2)}) collective-permute-start(bf16[32,2048]{1,0:T(8,128)(2,1)S(1)} %get-tuple-element.68), channel_id=1, source_target_pairs={{0,12},{4,8},{8,4},{12,0},{1,13},{5,9},{9,5},{13,1},{2,14},{6,10},... | collective-permute-start | bytes 393224 | tf_op jit(solution)/shard_map/ppermute | solution.py:286
  66.3 1.9 %collective-permute-start.10 = (bf16[32,2048]{1,0:T(8,128)(2,1)S(1)}, bf16[32,2048]{1,0:T(8,128)(2,1)S(1)}, u32[]{:S(2)}, u32[]{:S(2)}) collective-permute-start(bf16[32,2048]{1,0:T(8,128)(2,1)S(1)} %get-tuple-element.69), channel_id=1, source_target_pairs={{0,8},{4,12},{8,0},{12,4},{1,9},{5,13},{9,1},{13,5},{2,10},{6,14},... | collective-permute-start | bytes 393224 | tf_op jit(solution)/shard_map/ppermute | solution.py:286
  68.4 6.4 %add_multiply_fusion = (f32[256,4096]{1,0:T(8,128)}, f32[256,4096]{1,0:T(8,128)}, f32[256,4096]{1,0:T(8,128)}, f32[256,4096]{1,0:T(8,128)}) fusion(bf16[256,4096]{1,0:T(8,128)(2,1)S(1)} %collective-permute-done.8.up_theirs, bf16[256,4096]{1,0:T(8,128)(2,1)S(1)} %convolution_convert_fusion.up_mine, ...), kind=kLoop, calls=%fused_computation.8 | loop fusion | flops 15728640 | bytes 25165824 | tf_op jit(solution)/shard_map/mul | solution.py:359
  74.8 2.8 %fusion.1 = bf16[128,4096]{1,0:T(8,128)(2,1)S(1)} fusion(f32[256,4096]{1,0:T(8,128)} %get-tuple-element.67, f32[256,4096]{1,0:T(8,128)} %get-tuple-element.66), kind=kLoop, calls=%fused_computation.14 | loop fusion | flops 3145728 | bytes 5242880 | tf_op jit(solution)/shard_map/convert_element_type | solution.py:311
  77.8 2.1 %collective-permute-done.10 = bf16[32,2048]{1,0:T(8,128)(2,1)S(1)} collective-permute-done((bf16[32,2048]{1,0:T(8,128)(2,1)S(1)}, bf16[32,2048]{1,0:T(8,128)(2,1)S(1)}, u32[]{:S(2)}, u32[]{:S(2)}) %collective-permute-start.10) | collective-permute-done | bytes 131104 | tf_op jit(solution)/shard_map/ppermute | solution.py:286
  79.9 2.2 %collective-permute-start.14 = (bf16[32,2048]{1,0:T(8,128)(2,1)S(1)}, bf16[32,2048]{1,0:T(8,128)(2,1)S(1)}, u32[]{:S(2)}, u32[]{:S(2)}) collective-permute-start(bf16[32,2048]{1,0:T(8,128)(2,1)S(1)} %get-tuple-element.63), channel_id=1, source_target_pairs={{0,12},{4,8},{8,4},{12,0},{1,13},{5,9},{9,5},{13,1},{2,14},{6,10},... | collective-permute-start | bytes 393224 | tf_op jit(solution)/shard_map/ppermute | solution.py:286
  82.1 1.4 %collective-permute-start.12 = (bf16[32,2048]{1,0:T(8,128)(2,1)S(1)}, bf16[32,2048]{1,0:T(8,128)(2,1)S(1)}, u32[]{:S(2)}, u32[]{:S(2)}) collective-permute-start(bf16[32,2048]{1,0:T(8,128)(2,1)S(1)} %get-tuple-element.63), channel_id=1, source_target_pairs={{0,4},{4,0},{8,12},{12,8},{1,5},{5,1},{9,13},{13,9},{2,6},{6,2},{1... | collective-permute-start | bytes 393224 | tf_op jit(solution)/shard_map/ppermute | solution.py:286
  83.6 1.2 collective-permute-start.15
  84.8 1.7 %collective-permute-done.14 = bf16[32,2048]{1,0:T(8,128)(2,1)S(1)} collective-permute-done((bf16[32,2048]{1,0:T(8,128)(2,1)S(1)}, bf16[32,2048]{1,0:T(8,128)(2,1)S(1)}, u32[]{:S(2)}, u32[]{:S(2)}) %collective-permute-start.14) | collective-permute-done | bytes 131104 | tf_op jit(solution)/shard_map/ppermute | solution.py:286
  86.4 1.2 collective-permute-start.18
  87.6 5.4 %collective-permute-done.13 = bf16[32,2048]{1,0:T(8,128)(2,1)S(1)} collective-permute-done((bf16[32,2048]{1,0:T(8,128)(2,1)S(1)}, bf16[32,2048]{1,0:T(8,128)(2,1)S(1)}, u32[]{:S(2)}, u32[]{:S(2)}) %collective-permute-start.13) | collective-permute-done | bytes 131104 | tf_op jit(solution)/shard_map/ppermute | solution.py:286
  93.0 1.2 collective-permute-start.17
  94.5 5.9 %collective-permute-done.16 = bf16[32,2048]{1,0:T(8,128)(2,1)S(1)} collective-permute-done((bf16[32,2048]{1,0:T(8,128)(2,1)S(1)}, bf16[32,2048]{1,0:T(8,128)(2,1)S(1)}, u32[]{:S(2)}, u32[]{:S(2)}) %collective-permute-start.16) | collective-permute-done | bytes 131104 | tf_op jit(solution)/shard_map/ppermute | solution.py:286
  100.5 6.1 %back.1.refs_0_ = bf16[256,4096]{1,0:T(8,128)(2,1)S(1)} custom-call(bf16[256,2048]{1,0:T(8,128)(2,1)S(1)} %constant_dynamic-update-slice_fusion.8.slope.refs_0_, bf16[4096,2048]{1,0:T(8,128)(2,1)S(1)} %densify.5.weights), custom_call_target="tpu_custom_call" | custom-call | flops 4294967296 | bytes 19922944 | tf_op jit(solution)/shard_map/back/pallas_call | solution.py:238
  106.6 1.3 collective-permute-start.19
  107.9 9.2 %gradient.5 = bf16[64,20480]{1,0:T(8,128)(2,1)} custom-call(s32[320]{0:T(512)S(1)} %fusion.34.picks, bf16[256,4096]{1,0:T(8,128)(2,1)S(1)} %pad_maximum_fusion.lhs, bf16[256,2048]{1,0:T(8,128)(2,1)S(1)} %constant_dynamic-update-slice_fusion.8.slope.refs_0_), custom_call_target="tpu_custom_call" | custom-call | flops 4294967296 | bytes 6815744 | tf_op jit(solution)/shard_map/gradient/pallas_call | solution.py:162
  117.2 9.4 %gradient.4 = bf16[64,20480]{1,0:T(8,128)(2,1)} custom-call(s32[320]{0:T(512)S(1)} %fusion.28.picks, bf16[256,2048]{1,0:T(8,128)(2,1)S(1)} %constant_dynamic-update-slice_fusion.lhs, bf16[256,4096]{1,0:T(8,128)(2,1)S(1)} %back.1.refs_0_, bf16[256,4096]{1,0:T(8,128)(2,1)S(1)} %collective-permute-done.19.refs_1_, f32[256,4096]{1,0:T(8,128)S(1)} %copy-done.1), custom_call_target="tpu_custom_call" | custom-call | flops 4294967296 | bytes 16252928 | tf_op jit(solution)/shard_map/gradient/pallas_call | solution.py:162
  126.6 9.4 %gradient.3 = bf16[64,20480]{1,0:T(8,128)(2,1)} custom-call(s32[320]{0:T(512)S(1)} %fusion.22.picks, bf16[256,2048]{1,0:T(8,128)(2,1)S(1)} %constant_dynamic-update-slice_fusion.lhs, bf16[256,4096]{1,0:T(8,128)(2,1)S(1)} %back.1.refs_0_, bf16[256,4096]{1,0:T(8,128)(2,1)S(1)} %collective-permute-done.19.refs_1_, f32[256,4096]{1,0:T(8,128)S(1)} %copy-done), custom_call_target="tpu_custom_call" | custom-call | flops 4294967296 | bytes 16252928 | tf_op jit(solution)/shard_map/gradient/pallas_call | solution.py:162
  (65 shorter events, 5.9 us)
Async XLA Ops:
  0.6 10.8 %collective-permute-start.1 = (bf16[32,2048]{1,0:T(8,128)(2,1)}, bf16[32,2048]{1,0:T(8,128)(2,1)S(1)}, u32[]{:S(2)}, u32[]{:S(2)}) collective-permute-start(bf16[32,2048]{1,0:T(8,128)(2,1)} %param.8), channel_id=1, source_target_pairs={{0,8},{4,12},{8,0},{12,4},{1,9},{5,13},{9,1},{13,5},{2,10},{6,14},... | collective-permute-start | bytes 393224 | tf_op jit(solution)/shard_map/ppermute | solution.py:286
  3.8 7.6 %collective-permute-start = (bf16[32,2048]{1,0:T(8,128)(2,1)}, bf16[32,2048]{1,0:T(8,128)(2,1)S(1)}, u32[]{:S(2)}, u32[]{:S(2)}) collective-permute-start(bf16[32,2048]{1,0:T(8,128)(2,1)} %param.8), channel_id=1, source_target_pairs={{0,4},{4,0},{8,12},{12,8},{1,5},{5,1},{9,13},{13,9},{2,6},{6,2},{1... | collective-permute-start | bytes 393224 | tf_op jit(solution)/shard_map/ppermute | solution.py:286
  5.1 8.6 %collective-permute-start.2 = (bf16[32,2048]{1,0:T(8,128)(2,1)}, bf16[32,2048]{1,0:T(8,128)(2,1)S(1)}, u32[]{:S(2)}, u32[]{:S(2)}) collective-permute-start(bf16[32,2048]{1,0:T(8,128)(2,1)} %param.8), channel_id=1, source_target_pairs={{0,12},{4,8},{8,4},{12,0},{1,13},{5,9},{9,5},{13,1},{2,14},{6,10},... | collective-permute-start | bytes 393224 | tf_op jit(solution)/shard_map/ppermute | solution.py:286
  13.7 13.6 %collective-permute-start.3 = (bf16[32,2048]{1,0:T(8,128)(2,1)}, bf16[32,2048]{1,0:T(8,128)(2,1)S(1)}, u32[]{:S(2)}, u32[]{:S(2)}) collective-permute-start(bf16[32,2048]{1,0:T(8,128)(2,1)} %param.8), channel_id=1, source_target_pairs={{0,2},{2,0},{1,3},{3,1},{4,6},{6,4},{5,7},{7,5},{8,10},{10,8},{9,1... | collective-permute-start | bytes 393224 | tf_op jit(solution)/shard_map/ppermute | solution.py:286
  15.9 11.5 %collective-permute-start.4 = (bf16[32,2048]{1,0:T(8,128)(2,1)S(1)}, bf16[32,2048]{1,0:T(8,128)(2,1)S(1)}, u32[]{:S(2)}, u32[]{:S(2)}) collective-permute-start(bf16[32,2048]{1,0:T(8,128)(2,1)S(1)} %collective-permute-done), channel_id=1, source_target_pairs={{0,2},{2,0},{1,3},{3,1},{4,6},{6,4},{5,7},{7,5},{8,10},{10,8},{9,1... | collective-permute-start | bytes 393224 | tf_op jit(solution)/shard_map/ppermute | solution.py:286
  16.2 11.2 %collective-permute-start.5 = (bf16[32,2048]{1,0:T(8,128)(2,1)S(1)}, bf16[32,2048]{1,0:T(8,128)(2,1)S(1)}, u32[]{:S(2)}, u32[]{:S(2)}) collective-permute-start(bf16[32,2048]{1,0:T(8,128)(2,1)S(1)} %collective-permute-done.1), channel_id=1, source_target_pairs={{0,2},{2,0},{1,3},{3,1},{4,6},{6,4},{5,7},{7,5},{8,10},{10,8},{9,1... | collective-permute-start | bytes 393224 | tf_op jit(solution)/shard_map/ppermute | solution.py:286
  17.4 10.0 %collective-permute-start.6 = (bf16[32,2048]{1,0:T(8,128)(2,1)S(1)}, bf16[32,2048]{1,0:T(8,128)(2,1)S(1)}, u32[]{:S(2)}, u32[]{:S(2)}) collective-permute-start(bf16[32,2048]{1,0:T(8,128)(2,1)S(1)} %collective-permute-done.2), channel_id=1, source_target_pairs={{0,2},{2,0},{1,3},{3,1},{4,6},{6,4},{5,7},{7,5},{8,10},{10,8},{9,1... | collective-permute-start | bytes 393224 | tf_op jit(solution)/shard_map/ppermute | solution.py:286
  32.2 26.6 %collective-permute-start.7 = (bf16[256,4096]{1,0:T(8,128)(2,1)S(1)}, bf16[256,4096]{1,0:T(8,128)(2,1)S(1)}, u32[]{:S(2)}, u32[]{:S(2)}) collective-permute-start(bf16[256,4096]{1,0:T(8,128)(2,1)S(1)} %convolution_convert_fusion.1.gate_mine), channel_id=1, source_target_pairs={{0,1},{1,0},{2,3},{3,2},{4,5},{5,4},{6,7},{7,6},{8,9},{9,8},{10,11... | collective-permute-start | bytes 6291464 | tf_op jit(solution)/shard_map/ppermute | solution.py:299
  49.2 9.6 %collective-permute-start.8 = (bf16[256,4096]{1,0:T(8,128)(2,1)S(1)}, bf16[256,4096]{1,0:T(8,128)(2,1)S(1)}, u32[]{:S(2)}, u32[]{:S(2)}) collective-permute-start(bf16[256,4096]{1,0:T(8,128)(2,1)S(1)} %convolution_convert_fusion.up_mine), channel_id=1, source_target_pairs={{0,1},{1,0},{2,3},{3,2},{4,5},{5,4},{6,7},{7,6},{8,9},{9,8},{10,11... | collective-permute-start | bytes 6291464 | tf_op jit(solution)/shard_map/ppermute | solution.py:299
  64.1 13.7 %collective-permute-start.11 = (bf16[32,2048]{1,0:T(8,128)(2,1)S(1)}, bf16[32,2048]{1,0:T(8,128)(2,1)S(1)}, u32[]{:S(2)}, u32[]{:S(2)}) collective-permute-start(bf16[32,2048]{1,0:T(8,128)(2,1)S(1)} %get-tuple-element.68), channel_id=1, source_target_pairs={{0,12},{4,8},{8,4},{12,0},{1,13},{5,9},{9,5},{13,1},{2,14},{6,10},... | collective-permute-start | bytes 393224 | tf_op jit(solution)/shard_map/ppermute | solution.py:286
  66.3 13.5 %collective-permute-start.10 = (bf16[32,2048]{1,0:T(8,128)(2,1)S(1)}, bf16[32,2048]{1,0:T(8,128)(2,1)S(1)}, u32[]{:S(2)}, u32[]{:S(2)}) collective-permute-start(bf16[32,2048]{1,0:T(8,128)(2,1)S(1)} %get-tuple-element.69), channel_id=1, source_target_pairs={{0,8},{4,12},{8,0},{12,4},{1,9},{5,13},{9,1},{13,5},{2,10},{6,14},... | collective-permute-start | bytes 393224 | tf_op jit(solution)/shard_map/ppermute | solution.py:286
  68.2 11.6 %collective-permute-start.9 = (bf16[32,2048]{1,0:T(8,128)(2,1)S(1)}, bf16[32,2048]{1,0:T(8,128)(2,1)S(1)}, u32[]{:S(2)}, u32[]{:S(2)}) collective-permute-start(bf16[32,2048]{1,0:T(8,128)(2,1)S(1)} %get-tuple-element.70), channel_id=1, source_target_pairs={{0,4},{4,0},{8,12},{12,8},{1,5},{5,1},{9,13},{13,9},{2,6},{6,2},{1... | collective-permute-start | bytes 393224 | tf_op jit(solution)/shard_map/ppermute | solution.py:286
  74.8 5.1 %copy-start.2 = (bf16[32,2048]{1,0:T(8,128)(2,1)S(1)}, bf16[32,2048]{1,0:T(8,128)(2,1)}, u32[]{:S(2)}) copy-start(bf16[32,2048]{1,0:T(8,128)(2,1)} %param.9) | copy-start | bytes 393220
  79.9 6.5 %collective-permute-start.14 = (bf16[32,2048]{1,0:T(8,128)(2,1)S(1)}, bf16[32,2048]{1,0:T(8,128)(2,1)S(1)}, u32[]{:S(2)}, u32[]{:S(2)}) collective-permute-start(bf16[32,2048]{1,0:T(8,128)(2,1)S(1)} %get-tuple-element.63), channel_id=1, source_target_pairs={{0,12},{4,8},{8,4},{12,0},{1,13},{5,9},{9,5},{13,1},{2,14},{6,10},... | collective-permute-start | bytes 393224 | tf_op jit(solution)/shard_map/ppermute | solution.py:286
  82.1 10.9 %collective-permute-start.13 = (bf16[32,2048]{1,0:T(8,128)(2,1)S(1)}, bf16[32,2048]{1,0:T(8,128)(2,1)S(1)}, u32[]{:S(2)}, u32[]{:S(2)}) collective-permute-start(bf16[32,2048]{1,0:T(8,128)(2,1)S(1)} %get-tuple-element.63), channel_id=1, source_target_pairs={{0,8},{4,12},{8,0},{12,4},{1,9},{5,13},{9,1},{13,5},{2,10},{6,14},... | collective-permute-start | bytes 393224 | tf_op jit(solution)/shard_map/ppermute | solution.py:286
  82.1 12.1 %collective-permute-start.12 = (bf16[32,2048]{1,0:T(8,128)(2,1)S(1)}, bf16[32,2048]{1,0:T(8,128)(2,1)S(1)}, u32[]{:S(2)}, u32[]{:S(2)}) collective-permute-start(bf16[32,2048]{1,0:T(8,128)(2,1)S(1)} %get-tuple-element.63), channel_id=1, source_target_pairs={{0,4},{4,0},{8,12},{12,8},{1,5},{5,1},{9,13},{13,9},{2,6},{6,2},{1... | collective-permute-start | bytes 393224 | tf_op jit(solution)/shard_map/ppermute | solution.py:286
  83.6 11.0 %collective-permute-start.15 = (bf16[32,2048]{1,0:T(8,128)(2,1)S(1)}, bf16[32,2048]{1,0:T(8,128)(2,1)S(1)}, u32[]{:S(2)}, u32[]{:S(2)}) collective-permute-start(bf16[32,2048]{1,0:T(8,128)(2,1)S(1)} %get-tuple-element.63), channel_id=1, source_target_pairs={{0,2},{2,0},{1,3},{3,1},{4,6},{6,4},{5,7},{7,5},{8,10},{10,8},{9,1... | collective-permute-start | bytes 393224 | tf_op jit(solution)/shard_map/ppermute | solution.py:286
  86.4 14.1 %collective-permute-start.18 = (bf16[32,2048]{1,0:T(8,128)(2,1)S(1)}, bf16[32,2048]{1,0:T(8,128)(2,1)S(1)}, u32[]{:S(2)}, u32[]{:S(2)}) collective-permute-start(bf16[32,2048]{1,0:T(8,128)(2,1)S(1)} %collective-permute-done.14), channel_id=1, source_target_pairs={{0,2},{2,0},{1,3},{3,1},{4,6},{6,4},{5,7},{7,5},{8,10},{10,8},{9,1... | collective-permute-start | bytes 393224 | tf_op jit(solution)/shard_map/ppermute | solution.py:286
  93.0 7.5 %collective-permute-start.17 = (bf16[32,2048]{1,0:T(8,128)(2,1)S(1)}, bf16[32,2048]{1,0:T(8,128)(2,1)S(1)}, u32[]{:S(2)}, u32[]{:S(2)}) collective-permute-start(bf16[32,2048]{1,0:T(8,128)(2,1)S(1)} %collective-permute-done.13), channel_id=1, source_target_pairs={{0,2},{2,0},{1,3},{3,1},{4,6},{6,4},{5,7},{7,5},{8,10},{10,8},{9,1... | collective-permute-start | bytes 393224 | tf_op jit(solution)/shard_map/ppermute | solution.py:286
  94.2 6.3 %collective-permute-start.16 = (bf16[32,2048]{1,0:T(8,128)(2,1)S(1)}, bf16[32,2048]{1,0:T(8,128)(2,1)S(1)}, u32[]{:S(2)}, u32[]{:S(2)}) collective-permute-start(bf16[32,2048]{1,0:T(8,128)(2,1)S(1)} %collective-permute-done.12), channel_id=1, source_target_pairs={{0,2},{2,0},{1,3},{3,1},{4,6},{6,4},{5,7},{7,5},{8,10},{10,8},{9,1... | collective-permute-start | bytes 393224 | tf_op jit(solution)/shard_map/ppermute | solution.py:286
  106.6 10.6 %copy-start.1 = (f32[256,4096]{1,0:T(8,128)S(1)}, f32[256,4096]{1,0:T(8,128)}, u32[]{:S(2)}) copy-start(f32[256,4096]{1,0:T(8,128)} %get-tuple-element.56.refs_2_) | copy-start | bytes 12582916
  106.6 10.6 %collective-permute-start.19 = (bf16[256,4096]{1,0:T(8,128)(2,1)S(1)}, bf16[256,4096]{1,0:T(8,128)(2,1)S(1)}, u32[]{:S(2)}, u32[]{:S(2)}) collective-permute-start(bf16[256,4096]{1,0:T(8,128)(2,1)S(1)} %back.1.refs_0_), channel_id=1, source_target_pairs={{0,1},{1,0},{2,3},{3,2},{4,5},{5,4},{6,7},{7,6},{8,9},{9,8},{10,11... | collective-permute-start | bytes 6291464 | tf_op jit(solution)/shard_map/ppermute | solution.py:299
  117.2 9.4 %copy-start = (f32[256,4096]{1,0:T(8,128)S(1)}, f32[256,4096]{1,0:T(8,128)}, u32[]{:S(2)}) copy-start(f32[256,4096]{1,0:T(8,128)} %get-tuple-element.54.refs_2_) | copy-start | bytes 12582916

commit v6 on v5

--- a/solution.py
+++ b/solution.py
@@ -12,7 +12,7 @@
 BLK = 64
 PAIR = 2 * BLK
 SLOPE_SCALE = 0.0625
-DENSIFY_VMEM = 14 * 2**20
+STAGE_VMEM = 15 * 2**20
 PRODUCT_VMEM = 14 * 2**20
 DEPTH_PART = 512
 GRADIENT_VMEM = 44 * 2**20
@@ -34,30 +34,46 @@
     return max(n for n in options if total % n == 0)
 
 
-def densify_kernel(half_cap, rows_per_step, n_cols, chunks, table, panel, out, tiles, sems):
+def stage_kernel(half_cap, chunks, panel, tiles, sems):
+    share = half_cap // chunks
+    copies = []
+    for c in range(chunks):
+        span = pl.ds(c * share * PAIR, share * PAIR)
+        copies.append(pltpu.make_async_copy(panel.at[:, span], tiles.at[:, span], sems.at[c]))
+        copies[c].start()
+    tiles[:, 2 * half_cap * PAIR :] = jnp.zeros((BLK, PAIR), tiles.dtype)
+    batch = largest((1, 2, 4, 5, 8, 10, 16, 20, 40), share)
+    for c in range(chunks):
+        copies[c].wait()
+
+        def stage(b, carry):
+            t = c * share + b * batch
+            swapped = [swap_halves(tiles[:, lanes(t + u)]) for u in range(batch)]
+            for u in range(batch):
+                tiles[:, lanes(half_cap + t + u)] = swapped[u]
+            return carry
+
+        lax.fori_loop(0, share // batch, stage, 0)
+
+
+def staged(panel):
+    half_cap = panel.shape[1] // PAIR
+    chunks = largest((1, 2, 4), half_cap)
+    shape = (BLK, (2 * half_cap + 1) * PAIR)
+    return pl.pallas_call(
+        functools.partial(stage_kernel, half_cap, chunks),
+        in_specs=[pl.BlockSpec(memory_space=pltpu.HBM)],
+        out_specs=pl.BlockSpec(memory_space=pltpu.VMEM),
+        out_shape=jax.ShapeDtypeStruct(shape, panel.dtype),
+        scratch_shapes=[pltpu.SemaphoreType.DMA((chunks,))],
+        compiler_params=pltpu.CompilerParams(vmem_limit_bytes=STAGE_VMEM),
+        cost_estimate=pl.CostEstimate(flops=0, bytes_accessed=6 * panel.size, transcendentals=0),
+        name="stage",
+    )(pltpu.with_memory_space_constraint(panel, pltpu.HBM))
+
+
+def place_kernel(rows_per_step, n_cols, table, tiles, out):
     step = pl.program_id(0)
-    share = half_cap // chunks
-
-    @pl.when(step == 0)
-    def _():
-        copies = []
-        for c in range(chunks):
-            span = pl.ds(c * share * PAIR, share * PAIR)
-            copies.append(pltpu.make_async_copy(panel.at[:, span], tiles.at[:, span], sems.at[c]))
-            copies[c].start()
-        tiles[:, 2 * half_cap * PAIR :] = jnp.zeros((BLK, PAIR), tiles.dtype)
-        batch = largest((1, 2, 4, 5, 8, 10, 16, 20, 40), share)
-        for c in range(chunks):
-            copies[c].wait()
-
-            def stage(b, carry):
-                t = c * share + b * batch
-                swapped = [swap_halves(tiles[:, lanes(t + u)]) for u in range(batch)]
-                for u in range(batch):
-                    tiles[:, lanes(half_cap + t + u)] = swapped[u]
-                return carry
-
-            lax.fori_loop(0, share // batch, stage, 0)
 
     def row(i, carry):
         base = (step * rows_per_step + i) * n_cols
@@ -70,29 +86,23 @@
     lax.fori_loop(0, rows_per_step, row, 0)
 
 
-def densify(panel, table, n_rows, n_cols):
-    half_cap = panel.shape[1] // PAIR
+def place(tiles, table, n_rows, n_cols):
     rows_per_step = max(1, 128 // n_cols)
-    chunks = largest((1, 2, 4), half_cap)
-    return pl.pallas_call(
-        functools.partial(densify_kernel, half_cap, rows_per_step, n_cols, chunks),
+    return pl.pallas_call(
+        functools.partial(place_kernel, rows_per_step, n_cols),
         grid_spec=pltpu.PrefetchScalarGridSpec(
             num_scalar_prefetch=1,
             grid=(n_rows // rows_per_step,),
-            in_specs=[pl.BlockSpec(memory_space=pltpu.HBM)],
+            in_specs=[pl.BlockSpec(tiles.shape, lambda s, *_: (0, 0), pipeline_mode=pl.Buffered(1))],
             out_specs=pl.BlockSpec((rows_per_step * BLK, n_cols * BLK), lambda s, *_: (s, 0)),
-            scratch_shapes=[
-                pltpu.VMEM((BLK, (2 * half_cap + 1) * PAIR), panel.dtype),
-                pltpu.SemaphoreType.DMA((chunks,)),
-            ],
-        ),
-        out_shape=jax.ShapeDtypeStruct((n_rows * BLK, n_cols * BLK), panel.dtype),
-        compiler_params=pltpu.CompilerParams(vmem_limit_bytes=DENSIFY_VMEM),
+        ),
+        out_shape=jax.ShapeDtypeStruct((n_rows * BLK, n_cols * BLK), tiles.dtype),
+        compiler_params=pltpu.CompilerParams(vmem_limit_bytes=STAGE_VMEM),
         cost_estimate=pl.CostEstimate(
-            flops=0, bytes_accessed=4 * panel.size + 4 * n_rows * n_cols * BLK * BLK, transcendentals=0
-        ),
-        name="densify",
-    )(table, pltpu.with_memory_space_constraint(panel, pltpu.HBM))
+            flops=0, bytes_accessed=2 * tiles.size + 4 * n_rows * n_cols * BLK * BLK, transcendentals=0
+        ),
+        name="place",
+    )(table, tiles)
 
 
 def gradient_kernel(n_steps, rows_per_step, n_cols, n_rhs, picks, lhs, *refs):
@@ -225,6 +235,32 @@
     )(*partials, weights)
 
 
+def forward_kernel(rows, weights, out):
+    out[...] = jnp.dot(rows[...], weights[...], preferred_element_type=jnp.float32).astype(out.dtype)
+
+
+def forward_product(rows, weights):
+    depth, width = weights.shape
+    part = min(512, width)
+    return pl.pallas_call(
+        forward_kernel,
+        grid=(width // part,),
+        in_specs=[
+            pl.BlockSpec(rows.shape, lambda s: (0, 0)),
+            pl.BlockSpec((depth, part), lambda s: (0, s)),
+        ],
+        out_specs=pl.BlockSpec((rows.shape[0], part), lambda s: (0, s)),
+        out_shape=jax.ShapeDtypeStruct((rows.shape[0], width), jnp.bfloat16),
+        compiler_params=pltpu.CompilerParams(vmem_limit_bytes=PRODUCT_VMEM),
+        cost_estimate=pl.CostEstimate(
+            flops=2 * rows.size * width,
+            bytes_accessed=2 * (rows.size + weights.size + rows.shape[0] * width),
+            transcendentals=0,
+        ),
+        name="forward",
+    )(rows, weights)
+
+
 def back_kernel(slope, weights, out):
     out[...] = lax.dot_general(
         slope[...], weights[...], (((1,), (1,)), ((), ())), preferred_element_type=jnp.float32
@@ -333,17 +369,20 @@
     tables, gate_panel = lax.optimization_barrier((tables, gate_panel))
     gate_table, up_table, down_table, gate_codes, up_codes, down_codes = tables
 
-    near, gate_table = lax.optimization_barrier((gather_near(tokens), gate_table))
-    gate_w = densify(gate_panel[0, 0], gate_table, row_blocks, slab_blocks)
+    near, gate_tiles = lax.optimization_barrier((gather_near(tokens), staged(gate_panel[0, 0])))
     inputs = jnp.concatenate(gather_far(near))
-
-    gate_part = jnp.dot(inputs, gate_w, preferred_element_type=jnp.float32).astype(jnp.bfloat16)
+    gate_w = place(gate_tiles, gate_table, row_blocks, slab_blocks)
+    up_panel, gate_w = lax.optimization_barrier((up_panel, gate_w))
+    up_tiles = staged(up_panel[0, 0])
+    inputs, up_tiles = lax.optimization_barrier((inputs, up_tiles))
+    gate_part = forward_product(inputs, gate_w)
     gate_other = swap_cores(gate_part)
     up_table, gate_part = lax.optimization_barrier((up_table, gate_part))
-    up_w = densify(up_panel[0, 0], up_table, row_blocks, slab_blocks)
+    up_w = place(up_tiles, up_table, row_blocks, slab_blocks)
     up_part = jnp.dot(inputs, up_w, preferred_element_type=jnp.float32).astype(jnp.bfloat16)
     up_other = swap_cores(up_part)
-    down_w = densify(down_panel[0, 0], down_table, slab_blocks, row_blocks)
+    down_panel, up_part = lax.optimization_barrier((down_panel, up_part))
+    down_w = place(staged(down_panel[0, 0]), down_table, slab_blocks, row_blocks)
 
     partials = (gate_part, gate_other, up_part, up_other)
     own_hidden, out_part = hidden_and_output(own, partials, down_w)

time: 136 us -> 135 us (level)
  Pallas kernels: 67.9 us -> 75.2 us
  matrix products: 9.49 us -> 4.71 us
  waiting for transfers between devices: 17.3 us -> 15 us
    pallas_call x3 -> x7, Pallas kernels: 28.5 us -> 35.8 us  [the longest x3 18.5 us: place(): pl.pallas_call(functools.partial(place_kernel, rows_per_step, n_cols), gr...]
    dot_general x1 -> x0, matrix products: 4.74 us -> none  [local(): jnp.dot(inputs, gate_w, preferred_element_type=jnp.float32)]
    ppermute x17, waiting for transfers between devices: 17.3 us -> 15 us  [shift(): lax.ppermute(values, axis, [(i, i ^ k) for i in range(n)])]
  transfers between devices with their start and end apart: 20 -> 20, of which waited for: 5 -> 4; matrix products, arithmetic and copies ran while one was open for 16% -> 15% of each run, Pallas kernels for 28% -> 28%
where the time goes in v6:
time: 135 us
  Pallas kernels  75.2 us (56%)
  starting transfers between devices  22.8 us (17%)
  waiting for transfers between devices  15 us (11%)
  other arithmetic  13.7 us (10%)
  matrix products  4.71 us (3%)
  local copies, waits for them, and re-layouts  2.17 us (2%)
    pallas_call x3, Pallas kernels, gradient(): pl.pallas_call(functools.partial(gradient_kernel, n_steps, rows_per_step,...  28.1 us
    ppermute x17, starting transfers between devices, shift(): lax.ppermute(values, axis, [(i, i ^ k) for i in range(n)])  19 us
    pallas_call x3, Pallas kernels, place(): pl.pallas_call(functools.partial(place_kernel, rows_per_step, n_cols), gr...  18.5 us
    ppermute x17, waiting for transfers between devices, shift(): lax.ppermute(values, axis, [(i, i ^ k) for i in range(n)])  15 us
    pallas_call x3, Pallas kernels, staged(): pl.pallas_call(functools.partial(stage_kernel, half_cap, chunks), in_spec...  10.1 us
    pallas_call x1, Pallas kernels, forward_product(): pl.pallas_call(forward_kernel, grid=(width // part,), in_specs=[pl.BlockS...  7.12 us
    mul x1, other arithmetic, local(): gate_factor = up * sigmoid_gate * (1.0 + gate * (1.0 - sigmoid_gate))  6.39 us
    pallas_call x1, Pallas kernels, back_product(): pl.pallas_call(back_kernel, grid=(width // part,), in_specs=[pl.BlockSpec...  6.06 us
  transfers between devices with their start and end apart: 20, of which 4 were waited for; matrix products, arithmetic and copies ran while one was open for 15% of the time, Pallas kernels for 28%

profile of v6, /device:TPU:1, one launch (start us, length us, event | category | flops | bytes accessed | tf_op | source)
XLA Modules:
  0.0 134.6 jit_solution(9834807973836484871)
XLA Ops:
  0.6 3.2 %collective-permute-start.1 = (bf16[32,2048]{1,0:T(8,128)(2,1)}, bf16[32,2048]{1,0:T(8,128)(2,1)S(1)}, u32[]{:S(2)}, u32[]{:S(2)}) collective-permute-start(bf16[32,2048]{1,0:T(8,128)(2,1)} %param.8), channel_id=1, source_target_pairs={{0,8},{4,12},{8,0},{12,4},{1,9},{5,13},{9,1},{13,5},{2,10},{6,14},... | collective-permute-start | bytes 393224 | tf_op jit(solution)/shard_map/ppermute | solution.py:322
  3.8 1.3 collective-permute-start
  8.9 2.0 %select_reduce_fusion = (s32[2048]{0:T(1024)S(1)}, s32[2048]{0:T(1024)S(1)}, s32[2048]{0:T(1024)S(1)}) fusion(s32[640]{0:T(1024)S(1)} %reduce.2, s32[640]{0:T(1024)S(1)} %iota_add_fusion, s32[640]{0:T(1024)S(1)} %reduce.1, s32[640]{0:T(1024)S(1)} %reduce), kind=kLoop, calls=%fused_computation | loop fusion | flops 11790336 | bytes 34816 | tf_op jit(solution)/shard_map/reduce_sum | solution.py:297
  11.4 3.4 %stage.3.tiles = bf16[64,82048]{1,0:T(8,128)(2,1)S(1)} custom-call(bf16[64,40960]{1,0:T(8,128)(2,1)} %bitcast.26), custom_call_target="tpu_custom_call" | custom-call | bytes 15728640 | tf_op jit(solution)/shard_map/stage/pallas_call | solution.py:63
  14.9 1.3 collective-permute-start.3
  16.5 1.2 collective-permute-start.5
  18.0 6.1 %place.3.weights = bf16[2048,4096]{1,0:T(8,128)(2,1)S(1)} custom-call(s32[2048]{0:T(1024)S(1)} %get-tuple-element.43.table, bf16[64,82048]{1,0:T(8,128)(2,1)S(1)} %stage.3.tiles), custom_call_target="tpu_custom_call" | custom-call | bytes 44056576 | tf_op jit(solution)/shard_map/place/pallas_call | solution.py:91
  24.1 3.4 %stage.4.tiles = bf16[64,82048]{1,0:T(8,128)(2,1)S(1)} custom-call(bf16[64,40960]{1,0:T(8,128)(2,1)} %bitcast.27), custom_call_target="tpu_custom_call" | custom-call | bytes 15728640 | tf_op jit(solution)/shard_map/stage/pallas_call | solution.py:63
  27.6 7.1 %forward.1.gate_mine = bf16[256,4096]{1,0:T(8,128)(2,1)S(1)} custom-call(bf16[256,2048]{1,0:T(8,128)(2,1)S(1)} %constant_dynamic-update-slice_fusion.rows.lhs, bf16[2048,4096]{1,0:T(8,128)(2,1)S(1)} %place.3.weights), custom_call_target="tpu_custom_call" | custom-call | flops 4294967296 | bytes 19922944 | tf_op jit(solution)/shard_map/forward/pallas_call | solution.py:245
  34.7 2.4 %collective-permute-start.7 = (bf16[256,4096]{1,0:T(8,128)(2,1)S(1)}, bf16[256,4096]{1,0:T(8,128)(2,1)S(1)}, u32[]{:S(2)}, u32[]{:S(2)}) collective-permute-start(bf16[256,4096]{1,0:T(8,128)(2,1)S(1)} %forward.1.gate_mine), channel_id=1, source_target_pairs={{0,1},{1,0},{2,3},{3,2},{4,5},{5,4},{6,7},{7,6},{8,9},{9,8},{10,11... | collective-permute-start | bytes 6291464 | tf_op jit(solution)/shard_map/ppermute | solution.py:335
  37.1 6.1 %place.4 = bf16[2048,4096]{1,0:T(8,128)(2,1)S(1)} custom-call(s32[2048]{0:T(1024)S(1)} %get-tuple-element.50.table, bf16[64,82048]{1,0:T(8,128)(2,1)S(1)} %stage.4.tiles), custom_call_target="tpu_custom_call" | custom-call | bytes 44056576 | tf_op jit(solution)/shard_map/place/pallas_call | solution.py:91
  43.2 4.7 %convolution_convert_fusion.up_mine = bf16[256,4096]{1,0:T(8,128)(2,1)S(1)} fusion(bf16[256,2048]{1,0:T(8,128)(2,1)S(1)} %constant_dynamic-update-slice_fusion.rows.lhs, bf16[2048,4096]{1,0:T(8,128)(2,1)S(1)} %place.4), kind=kOutput, calls=%fused_computation.6 | convolution fusion | flops 4296015872 | bytes 19922944 | tf_op jit(solution)/shard_map/dot_general | solution.py:382
  48.0 3.4 %stage.5.tiles = bf16[64,82048]{1,0:T(8,128)(2,1)S(1)} custom-call(bf16[64,40960]{1,0:T(8,128)(2,1)} %bitcast.28), custom_call_target="tpu_custom_call" | custom-call | bytes 15728640 | tf_op jit(solution)/shard_map/stage/pallas_call | solution.py:63
  51.4 6.4 %place.5.weights = bf16[4096,2048]{1,0:T(8,128)(2,1)S(1)} custom-call(s32[2048]{0:T(1024)S(1)} %reshape.60.table, bf16[64,82048]{1,0:T(8,128)(2,1)S(1)} %stage.5.tiles), custom_call_target="tpu_custom_call" | custom-call | bytes 44056576 | tf_op jit(solution)/shard_map/place/pallas_call | solution.py:91
  57.8 5.3 %output.1 = (bf16[128,4096]{1,0:T(8,128)(2,1)S(1)}, bf16[128,2048]{1,0:T(8,128)(2,1)S(1)}) custom-call(bf16[256,4096]{1,0:T(8,128)(2,1)S(1)} %forward.1.gate_mine, bf16[256,4096]{1,0:T(8,128)(2,1)S(1)} %collective-permute-done.7.gate_theirs, bf16[256,4096]{1,0:T(8,128)(2,1)S(1)} %convolution_convert_fusion.up_mine, ...), custom_call_target="tpu_custom_call" | custom-call | flops 2147483648 | bytes 22544384 | tf_op jit(solution)/shard_map/output/pallas_call | solution.py:214
  63.1 3.6 %collective-permute-start.11 = (bf16[32,2048]{1,0:T(8,128)(2,1)S(1)}, bf16[32,2048]{1,0:T(8,128)(2,1)S(1)}, u32[]{:S(2)}, u32[]{:S(2)}) collective-permute-start(bf16[32,2048]{1,0:T(8,128)(2,1)S(1)} %get-tuple-element.80), channel_id=1, source_target_pairs={{0,12},{4,8},{8,4},{12,0},{1,13},{5,9},{9,5},{13,1},{2,14},{6,10},... | collective-permute-start | bytes 393224 | tf_op jit(solution)/shard_map/ppermute | solution.py:322
  67.1 6.4 %add_multiply_fusion = (f32[256,4096]{1,0:T(8,128)}, f32[256,4096]{1,0:T(8,128)}, f32[256,4096]{1,0:T(8,128)}, f32[256,4096]{1,0:T(8,128)}) fusion(bf16[256,4096]{1,0:T(8,128)(2,1)S(1)} %collective-permute-done.8.up_theirs, bf16[256,4096]{1,0:T(8,128)(2,1)S(1)} %convolution_convert_fusion.up_mine, ...), kind=kLoop, calls=%fused_computation.7 | loop fusion | flops 15728640 | bytes 25165824 | tf_op jit(solution)/shard_map/mul | solution.py:398
  73.5 2.8 %fusion.1 = bf16[128,4096]{1,0:T(8,128)(2,1)S(1)} fusion(f32[256,4096]{1,0:T(8,128)} %get-tuple-element.79, f32[256,4096]{1,0:T(8,128)} %get-tuple-element.78), kind=kLoop, calls=%fused_computation.13 | loop fusion | flops 3145728 | bytes 5242880 | tf_op jit(solution)/shard_map/convert_element_type | solution.py:347
  76.4 2.0 %collective-permute-done.10 = bf16[32,2048]{1,0:T(8,128)(2,1)S(1)} collective-permute-done((bf16[32,2048]{1,0:T(8,128)(2,1)S(1)}, bf16[32,2048]{1,0:T(8,128)(2,1)S(1)}, u32[]{:S(2)}, u32[]{:S(2)}) %collective-permute-start.10) | collective-permute-done | bytes 131104 | tf_op jit(solution)/shard_map/ppermute | solution.py:322
  78.6 1.9 %collective-permute-start.14 = (bf16[32,2048]{1,0:T(8,128)(2,1)S(1)}, bf16[32,2048]{1,0:T(8,128)(2,1)S(1)}, u32[]{:S(2)}, u32[]{:S(2)}) collective-permute-start(bf16[32,2048]{1,0:T(8,128)(2,1)S(1)} %get-tuple-element.75), channel_id=1, source_target_pairs={{0,12},{4,8},{8,4},{12,0},{1,13},{5,9},{9,5},{13,1},{2,14},{6,10},... | collective-permute-start | bytes 393224 | tf_op jit(solution)/shard_map/ppermute | solution.py:322
  80.4 1.7 %collective-permute-start.12 = (bf16[32,2048]{1,0:T(8,128)(2,1)S(1)}, bf16[32,2048]{1,0:T(8,128)(2,1)S(1)}, u32[]{:S(2)}, u32[]{:S(2)}) collective-permute-start(bf16[32,2048]{1,0:T(8,128)(2,1)S(1)} %get-tuple-element.75), channel_id=1, source_target_pairs={{0,4},{4,0},{8,12},{12,8},{1,5},{5,1},{9,13},{13,9},{2,6},{6,2},{1... | collective-permute-start | bytes 393224 | tf_op jit(solution)/shard_map/ppermute | solution.py:322
  82.2 1.2 collective-permute-start.15
  83.4 1.4 %collective-permute-done.14 = bf16[32,2048]{1,0:T(8,128)(2,1)S(1)} collective-permute-done((bf16[32,2048]{1,0:T(8,128)(2,1)S(1)}, bf16[32,2048]{1,0:T(8,128)(2,1)S(1)}, u32[]{:S(2)}, u32[]{:S(2)}) %collective-permute-start.14) | collective-permute-done | bytes 131104 | tf_op jit(solution)/shard_map/ppermute | solution.py:322
  84.8 1.2 collective-permute-start.18
  86.0 5.6 %collective-permute-done.13 = bf16[32,2048]{1,0:T(8,128)(2,1)S(1)} collective-permute-done((bf16[32,2048]{1,0:T(8,128)(2,1)S(1)}, bf16[32,2048]{1,0:T(8,128)(2,1)S(1)}, u32[]{:S(2)}, u32[]{:S(2)}) %collective-permute-start.13) | collective-permute-done | bytes 131104 | tf_op jit(solution)/shard_map/ppermute | solution.py:322
  91.6 1.3 collective-permute-start.17
  93.2 5.9 %collective-permute-done.16 = bf16[32,2048]{1,0:T(8,128)(2,1)S(1)} collective-permute-done((bf16[32,2048]{1,0:T(8,128)(2,1)S(1)}, bf16[32,2048]{1,0:T(8,128)(2,1)S(1)}, u32[]{:S(2)}, u32[]{:S(2)}) %collective-permute-start.16) | collective-permute-done | bytes 131104 | tf_op jit(solution)/shard_map/ppermute | solution.py:322
  99.2 6.1 %back.1.refs_0_ = bf16[256,4096]{1,0:T(8,128)(2,1)S(1)} custom-call(bf16[256,2048]{1,0:T(8,128)(2,1)S(1)} %constant_dynamic-update-slice_fusion.8.slope.refs_0_, bf16[4096,2048]{1,0:T(8,128)(2,1)S(1)} %place.5.weights), custom_call_target="tpu_custom_call" | custom-call | flops 4294967296 | bytes 19922944 | tf_op jit(solution)/shard_map/back/pallas_call | solution.py:274
  105.3 1.3 collective-permute-start.19
  106.5 9.0 %gradient.5 = bf16[64,20480]{1,0:T(8,128)(2,1)} custom-call(s32[320]{0:T(512)S(1)} %fusion.34.picks, bf16[256,4096]{1,0:T(8,128)(2,1)S(1)} %pad_maximum_fusion.lhs, bf16[256,2048]{1,0:T(8,128)(2,1)S(1)} %constant_dynamic-update-slice_fusion.8.slope.refs_0_), custom_call_target="tpu_custom_call" | custom-call | flops 4294967296 | bytes 6815744 | tf_op jit(solution)/shard_map/gradient/pallas_call | solution.py:172
  115.6 9.6 %gradient.4 = bf16[64,20480]{1,0:T(8,128)(2,1)} custom-call(s32[320]{0:T(512)S(1)} %fusion.28.picks, bf16[256,2048]{1,0:T(8,128)(2,1)S(1)} %constant_dynamic-update-slice_fusion.rows.lhs, bf16[256,4096]{1,0:T(8,128)(2,1)S(1)} %back.1.refs_0_, bf16[256,4096]{1,0:T(8,128)(2,1)S(1)} %collective-permute-done.19.refs_1_, f32[256,4096]{1,0:T(8,128)S(1)} %copy-done.1), custom_call_target="tpu_custom_call" | custom-call | flops 4294967296 | bytes 16252928 | tf_op jit(solution)/shard_map/gradient/pallas_call | solution.py:172
  125.2 9.4 %gradient.3 = bf16[64,20480]{1,0:T(8,128)(2,1)} custom-call(s32[320]{0:T(512)S(1)} %fusion.22.picks, bf16[256,2048]{1,0:T(8,128)(2,1)S(1)} %constant_dynamic-update-slice_fusion.rows.lhs, bf16[256,4096]{1,0:T(8,128)(2,1)S(1)} %back.1.refs_0_, bf16[256,4096]{1,0:T(8,128)(2,1)S(1)} %collective-permute-done.19.refs_1_, f32[256,4096]{1,0:T(8,128)S(1)} %copy-done), custom_call_target="tpu_custom_call" | custom-call | flops 4294967296 | bytes 16252928 | tf_op jit(solution)/shard_map/gradient/pallas_call | solution.py:172
  (70 shorter events, 6.0 us)
Async XLA Ops:
  0.6 14.2 %collective-permute-start.1 = (bf16[32,2048]{1,0:T(8,128)(2,1)}, bf16[32,2048]{1,0:T(8,128)(2,1)S(1)}, u32[]{:S(2)}, u32[]{:S(2)}) collective-permute-start(bf16[32,2048]{1,0:T(8,128)(2,1)} %param.8), channel_id=1, source_target_pairs={{0,8},{4,12},{8,0},{12,4},{1,9},{5,13},{9,1},{13,5},{2,10},{6,14},... | collective-permute-start | bytes 393224 | tf_op jit(solution)/shard_map/ppermute | solution.py:322
  3.8 11.0 %collective-permute-start = (bf16[32,2048]{1,0:T(8,128)(2,1)}, bf16[32,2048]{1,0:T(8,128)(2,1)S(1)}, u32[]{:S(2)}, u32[]{:S(2)}) collective-permute-start(bf16[32,2048]{1,0:T(8,128)(2,1)} %param.8), channel_id=1, source_target_pairs={{0,4},{4,0},{8,12},{12,8},{1,5},{5,1},{9,13},{13,9},{2,6},{6,2},{1... | collective-permute-start | bytes 393224 | tf_op jit(solution)/shard_map/ppermute | solution.py:322
  5.1 9.7 %collective-permute-start.2 = (bf16[32,2048]{1,0:T(8,128)(2,1)}, bf16[32,2048]{1,0:T(8,128)(2,1)S(1)}, u32[]{:S(2)}, u32[]{:S(2)}) collective-permute-start(bf16[32,2048]{1,0:T(8,128)(2,1)} %param.8), channel_id=1, source_target_pairs={{0,12},{4,8},{8,4},{12,0},{1,13},{5,9},{9,5},{13,1},{2,14},{6,10},... | collective-permute-start | bytes 393224 | tf_op jit(solution)/shard_map/ppermute | solution.py:322
  11.4 3.5 %copy-start.3 = (bf16[32,2048]{1,0:T(8,128)(2,1)S(1)}, bf16[32,2048]{1,0:T(8,128)(2,1)}, u32[]{:S(2)}) copy-start(bf16[32,2048]{1,0:T(8,128)(2,1)} %param.8) | copy-start | bytes 393220
  14.9 12.6 %collective-permute-start.3 = (bf16[32,2048]{1,0:T(8,128)(2,1)S(1)}, bf16[32,2048]{1,0:T(8,128)(2,1)S(1)}, u32[]{:S(2)}, u32[]{:S(2)}) collective-permute-start(bf16[32,2048]{1,0:T(8,128)(2,1)S(1)} %copy-done.3), channel_id=1, source_target_pairs={{0,2},{2,0},{1,3},{3,1},{4,6},{6,4},{5,7},{7,5},{8,10},{10,8},{9,1... | collective-permute-start | bytes 393224 | tf_op jit(solution)/shard_map/ppermute | solution.py:322
  16.1 11.4 %collective-permute-start.4 = (bf16[32,2048]{1,0:T(8,128)(2,1)S(1)}, bf16[32,2048]{1,0:T(8,128)(2,1)S(1)}, u32[]{:S(2)}, u32[]{:S(2)}) collective-permute-start(bf16[32,2048]{1,0:T(8,128)(2,1)S(1)} %collective-permute-done), channel_id=1, source_target_pairs={{0,2},{2,0},{1,3},{3,1},{4,6},{6,4},{5,7},{7,5},{8,10},{10,8},{9,1... | collective-permute-start | bytes 393224 | tf_op jit(solution)/shard_map/ppermute | solution.py:322
  16.5 11.1 %collective-permute-start.5 = (bf16[32,2048]{1,0:T(8,128)(2,1)S(1)}, bf16[32,2048]{1,0:T(8,128)(2,1)S(1)}, u32[]{:S(2)}, u32[]{:S(2)}) collective-permute-start(bf16[32,2048]{1,0:T(8,128)(2,1)S(1)} %collective-permute-done.1), channel_id=1, source_target_pairs={{0,2},{2,0},{1,3},{3,1},{4,6},{6,4},{5,7},{7,5},{8,10},{10,8},{9,1... | collective-permute-start | bytes 393224 | tf_op jit(solution)/shard_map/ppermute | solution.py:322
  17.7 9.9 %collective-permute-start.6 = (bf16[32,2048]{1,0:T(8,128)(2,1)S(1)}, bf16[32,2048]{1,0:T(8,128)(2,1)S(1)}, u32[]{:S(2)}, u32[]{:S(2)}) collective-permute-start(bf16[32,2048]{1,0:T(8,128)(2,1)S(1)} %collective-permute-done.2), channel_id=1, source_target_pairs={{0,2},{2,0},{1,3},{3,1},{4,6},{6,4},{5,7},{7,5},{8,10},{10,8},{9,1... | collective-permute-start | bytes 393224 | tf_op jit(solution)/shard_map/ppermute | solution.py:322
  34.7 23.1 %collective-permute-start.7 = (bf16[256,4096]{1,0:T(8,128)(2,1)S(1)}, bf16[256,4096]{1,0:T(8,128)(2,1)S(1)}, u32[]{:S(2)}, u32[]{:S(2)}) collective-permute-start(bf16[256,4096]{1,0:T(8,128)(2,1)S(1)} %forward.1.gate_mine), channel_id=1, source_target_pairs={{0,1},{1,0},{2,3},{3,2},{4,5},{5,4},{6,7},{7,6},{8,9},{9,8},{10,11... | collective-permute-start | bytes 6291464 | tf_op jit(solution)/shard_map/ppermute | solution.py:335
  48.0 9.8 %collective-permute-start.8 = (bf16[256,4096]{1,0:T(8,128)(2,1)S(1)}, bf16[256,4096]{1,0:T(8,128)(2,1)S(1)}, u32[]{:S(2)}, u32[]{:S(2)}) collective-permute-start(bf16[256,4096]{1,0:T(8,128)(2,1)S(1)} %convolution_convert_fusion.up_mine), channel_id=1, source_target_pairs={{0,1},{1,0},{2,3},{3,2},{4,5},{5,4},{6,7},{7,6},{8,9},{9,8},{10,11... | collective-permute-start | bytes 6291464 | tf_op jit(solution)/shard_map/ppermute | solution.py:335
  63.1 13.3 %collective-permute-start.11 = (bf16[32,2048]{1,0:T(8,128)(2,1)S(1)}, bf16[32,2048]{1,0:T(8,128)(2,1)S(1)}, u32[]{:S(2)}, u32[]{:S(2)}) collective-permute-start(bf16[32,2048]{1,0:T(8,128)(2,1)S(1)} %get-tuple-element.80), channel_id=1, source_target_pairs={{0,12},{4,8},{8,4},{12,0},{1,13},{5,9},{9,5},{13,1},{2,14},{6,10},... | collective-permute-start | bytes 393224 | tf_op jit(solution)/shard_map/ppermute | solution.py:322
  66.7 11.8 %collective-permute-start.10 = (bf16[32,2048]{1,0:T(8,128)(2,1)S(1)}, bf16[32,2048]{1,0:T(8,128)(2,1)S(1)}, u32[]{:S(2)}, u32[]{:S(2)}) collective-permute-start(bf16[32,2048]{1,0:T(8,128)(2,1)S(1)} %get-tuple-element.81), channel_id=1, source_target_pairs={{0,8},{4,12},{8,0},{12,4},{1,9},{5,13},{9,1},{13,5},{2,10},{6,14},... | collective-permute-start | bytes 393224 | tf_op jit(solution)/shard_map/ppermute | solution.py:322
  66.7 11.8 %collective-permute-start.9 = (bf16[32,2048]{1,0:T(8,128)(2,1)S(1)}, bf16[32,2048]{1,0:T(8,128)(2,1)S(1)}, u32[]{:S(2)}, u32[]{:S(2)}) collective-permute-start(bf16[32,2048]{1,0:T(8,128)(2,1)S(1)} %get-tuple-element.82), channel_id=1, source_target_pairs={{0,4},{4,0},{8,12},{12,8},{1,5},{5,1},{9,13},{13,9},{2,6},{6,2},{1... | collective-permute-start | bytes 393224 | tf_op jit(solution)/shard_map/ppermute | solution.py:322
  73.5 5.0 %copy-start.2 = (bf16[32,2048]{1,0:T(8,128)(2,1)S(1)}, bf16[32,2048]{1,0:T(8,128)(2,1)}, u32[]{:S(2)}) copy-start(bf16[32,2048]{1,0:T(8,128)(2,1)} %param.9) | copy-start | bytes 393220
  78.6 6.2 %collective-permute-start.14 = (bf16[32,2048]{1,0:T(8,128)(2,1)S(1)}, bf16[32,2048]{1,0:T(8,128)(2,1)S(1)}, u32[]{:S(2)}, u32[]{:S(2)}) collective-permute-start(bf16[32,2048]{1,0:T(8,128)(2,1)S(1)} %get-tuple-element.75), channel_id=1, source_target_pairs={{0,12},{4,8},{8,4},{12,0},{1,13},{5,9},{9,5},{13,1},{2,14},{6,10},... | collective-permute-start | bytes 393224 | tf_op jit(solution)/shard_map/ppermute | solution.py:322
  80.4 11.2 %collective-permute-start.13 = (bf16[32,2048]{1,0:T(8,128)(2,1)S(1)}, bf16[32,2048]{1,0:T(8,128)(2,1)S(1)}, u32[]{:S(2)}, u32[]{:S(2)}) collective-permute-start(bf16[32,2048]{1,0:T(8,128)(2,1)S(1)} %get-tuple-element.75), channel_id=1, source_target_pairs={{0,8},{4,12},{8,0},{12,4},{1,9},{5,13},{9,1},{13,5},{2,10},{6,14},... | collective-permute-start | bytes 393224 | tf_op jit(solution)/shard_map/ppermute | solution.py:322
  80.4 12.5 %collective-permute-start.12 = (bf16[32,2048]{1,0:T(8,128)(2,1)S(1)}, bf16[32,2048]{1,0:T(8,128)(2,1)S(1)}, u32[]{:S(2)}, u32[]{:S(2)}) collective-permute-start(bf16[32,2048]{1,0:T(8,128)(2,1)S(1)} %get-tuple-element.75), channel_id=1, source_target_pairs={{0,4},{4,0},{8,12},{12,8},{1,5},{5,1},{9,13},{13,9},{2,6},{6,2},{1... | collective-permute-start | bytes 393224 | tf_op jit(solution)/shard_map/ppermute | solution.py:322
  82.2 11.0 %collective-permute-start.15 = (bf16[32,2048]{1,0:T(8,128)(2,1)S(1)}, bf16[32,2048]{1,0:T(8,128)(2,1)S(1)}, u32[]{:S(2)}, u32[]{:S(2)}) collective-permute-start(bf16[32,2048]{1,0:T(8,128)(2,1)S(1)} %get-tuple-element.75), channel_id=1, source_target_pairs={{0,2},{2,0},{1,3},{3,1},{4,6},{6,4},{5,7},{7,5},{8,10},{10,8},{9,1... | collective-permute-start | bytes 393224 | tf_op jit(solution)/shard_map/ppermute | solution.py:322
  84.8 14.4 %collective-permute-start.18 = (bf16[32,2048]{1,0:T(8,128)(2,1)S(1)}, bf16[32,2048]{1,0:T(8,128)(2,1)S(1)}, u32[]{:S(2)}, u32[]{:S(2)}) collective-permute-start(bf16[32,2048]{1,0:T(8,128)(2,1)S(1)} %collective-permute-done.14), channel_id=1, source_target_pairs={{0,2},{2,0},{1,3},{3,1},{4,6},{6,4},{5,7},{7,5},{8,10},{10,8},{9,1... | collective-permute-start | bytes 393224 | tf_op jit(solution)/shard_map/ppermute | solution.py:322
  91.6 7.5 %collective-permute-start.17 = (bf16[32,2048]{1,0:T(8,128)(2,1)S(1)}, bf16[32,2048]{1,0:T(8,128)(2,1)S(1)}, u32[]{:S(2)}, u32[]{:S(2)}) collective-permute-start(bf16[32,2048]{1,0:T(8,128)(2,1)S(1)} %collective-permute-done.13), channel_id=1, source_target_pairs={{0,2},{2,0},{1,3},{3,1},{4,6},{6,4},{5,7},{7,5},{8,10},{10,8},{9,1... | collective-permute-start | bytes 393224 | tf_op jit(solution)/shard_map/ppermute | solution.py:322
  92.9 6.2 %collective-permute-start.16 = (bf16[32,2048]{1,0:T(8,128)(2,1)S(1)}, bf16[32,2048]{1,0:T(8,128)(2,1)S(1)}, u32[]{:S(2)}, u32[]{:S(2)}) collective-permute-start(bf16[32,2048]{1,0:T(8,128)(2,1)S(1)} %collective-permute-done.12), channel_id=1, source_target_pairs={{0,2},{2,0},{1,3},{3,1},{4,6},{6,4},{5,7},{7,5},{8,10},{10,8},{9,1... | collective-permute-start | bytes 393224 | tf_op jit(solution)/shard_map/ppermute | solution.py:322
  105.2 10.3 %copy-start.1 = (f32[256,4096]{1,0:T(8,128)S(1)}, f32[256,4096]{1,0:T(8,128)}, u32[]{:S(2)}) copy-start(f32[256,4096]{1,0:T(8,128)} %get-tuple-element.68.refs_2_) | copy-start | bytes 12582916
  105.3 10.3 %collective-permute-start.19 = (bf16[256,4096]{1,0:T(8,128)(2,1)S(1)}, bf16[256,4096]{1,0:T(8,128)(2,1)S(1)}, u32[]{:S(2)}, u32[]{:S(2)}) collective-permute-start(bf16[256,4096]{1,0:T(8,128)(2,1)S(1)} %back.1.refs_0_), channel_id=1, source_target_pairs={{0,1},{1,0},{2,3},{3,2},{4,5},{5,4},{6,7},{7,6},{8,9},{9,8},{10,11... | collective-permute-start | bytes 6291464 | tf_op jit(solution)/shard_map/ppermute | solution.py:335
  115.6 9.7 %copy-start = (f32[256,4096]{1,0:T(8,128)S(1)}, f32[256,4096]{1,0:T(8,128)}, u32[]{:S(2)}) copy-start(f32[256,4096]{1,0:T(8,128)} %get-tuple-element.66.refs_2_) | copy-start | bytes 12582916

commit v7 on v6

--- a/solution.py
+++ b/solution.py
@@ -241,7 +241,7 @@
 
 def forward_product(rows, weights):
     depth, width = weights.shape
-    part = min(512, width)
+    part = min(1024, width)
     return pl.pallas_call(
         forward_kernel,
         grid=(width // part,),
@@ -270,7 +270,7 @@
 def back_product(slope, weights):
     width, depth = weights.shape
     rows = slope.shape[0]
-    part = min(512, width)
+    part = min(1024, width)
     return pl.pallas_call(
         back_kernel,
         grid=(width // part,),

time: 135 us -> 133 us (0.985)
  Pallas kernels: 75.2 us -> 73.5 us
  transfers between devices with their start and end apart: 20 -> 20, of which waited for: 4 -> 4; matrix products, arithmetic and copies ran while one was open for 15% -> 15% of each run, Pallas kernels for 28% -> 29%
where the time goes in v7:
time: 133 us
  Pallas kernels  73.5 us (55%)
  starting transfers between devices  22.9 us (17%)
  waiting for transfers between devices  14.9 us (11%)
  other arithmetic  13.7 us (10%)
  matrix products  4.71 us (4%)
  local copies, waits for them, and re-layouts  2.17 us (2%)
    pallas_call x3, Pallas kernels, gradient(): pl.pallas_call(functools.partial(gradient_kernel, n_steps, rows_per_step,...  28.1 us
    ppermute x17, starting transfers between devices, shift(): lax.ppermute(values, axis, [(i, i ^ k) for i in range(n)])  19.1 us
    pallas_call x3, Pallas kernels, place(): pl.pallas_call(functools.partial(place_kernel, rows_per_step, n_cols), gr...  18.5 us
    ppermute x17, waiting for transfers between devices, shift(): lax.ppermute(values, axis, [(i, i ^ k) for i in range(n)])  14.9 us
    pallas_call x3, Pallas kernels, staged(): pl.pallas_call(functools.partial(stage_kernel, half_cap, chunks), in_spec...  10.1 us
    mul x1, other arithmetic, local(): gate_factor = up * sigmoid_gate * (1.0 + gate * (1.0 - sigmoid_gate))  6.39 us
    pallas_call x1, Pallas kernels, forward_product(): pl.pallas_call(forward_kernel, grid=(width // part,), in_specs=[pl.BlockS...  6.23 us
    pallas_call x1, Pallas kernels, hidden_and_output(): pl.pallas_call(output_kernel, grid=(depth // part,), in_specs=[pl.BlockSp...  5.28 us
  transfers between devices with their start and end apart: 20, of which 4 were waited for; matrix products, arithmetic and copies ran while one was open for 15% of the time, Pallas kernels for 29%

profile of v7, /device:TPU:1, one launch (start us, length us, event | category | flops | bytes accessed | tf_op | source)
XLA Modules:
  0.0 132.9 jit_solution(6554769819199055557)
XLA Ops:
  0.6 3.2 %collective-permute-start.1 = (bf16[32,2048]{1,0:T(8,128)(2,1)}, bf16[32,2048]{1,0:T(8,128)(2,1)S(1)}, u32[]{:S(2)}, u32[]{:S(2)}) collective-permute-start(bf16[32,2048]{1,0:T(8,128)(2,1)} %param.8), channel_id=1, source_target_pairs={{0,8},{4,12},{8,0},{12,4},{1,9},{5,13},{9,1},{13,5},{2,10},{6,14},... | collective-permute-start | bytes 393224 | tf_op jit(solution)/shard_map/ppermute | solution.py:322
  3.8 1.3 collective-permute-start
  8.9 2.0 %select_reduce_fusion = (s32[2048]{0:T(1024)S(1)}, s32[2048]{0:T(1024)S(1)}, s32[2048]{0:T(1024)S(1)}) fusion(s32[640]{0:T(1024)S(1)} %reduce.2, s32[640]{0:T(1024)S(1)} %iota_add_fusion, s32[640]{0:T(1024)S(1)} %reduce.1, s32[640]{0:T(1024)S(1)} %reduce), kind=kLoop, calls=%fused_computation | loop fusion | flops 11790336 | bytes 34816 | tf_op jit(solution)/shard_map/reduce_sum | solution.py:297
  11.4 3.4 %stage.3.tiles = bf16[64,82048]{1,0:T(8,128)(2,1)S(1)} custom-call(bf16[64,40960]{1,0:T(8,128)(2,1)} %bitcast.26), custom_call_target="tpu_custom_call" | custom-call | bytes 15728640 | tf_op jit(solution)/shard_map/stage/pallas_call | solution.py:63
  14.9 1.3 collective-permute-start.3
  16.5 1.2 collective-permute-start.5
  18.0 6.1 %place.3.weights = bf16[2048,4096]{1,0:T(8,128)(2,1)S(1)} custom-call(s32[2048]{0:T(1024)S(1)} %get-tuple-element.43.table, bf16[64,82048]{1,0:T(8,128)(2,1)S(1)} %stage.3.tiles), custom_call_target="tpu_custom_call" | custom-call | bytes 44056576 | tf_op jit(solution)/shard_map/place/pallas_call | solution.py:91
  24.1 3.4 %stage.4.tiles = bf16[64,82048]{1,0:T(8,128)(2,1)S(1)} custom-call(bf16[64,40960]{1,0:T(8,128)(2,1)} %bitcast.27), custom_call_target="tpu_custom_call" | custom-call | bytes 15728640 | tf_op jit(solution)/shard_map/stage/pallas_call | solution.py:63
  27.6 6.2 %forward.1.gate_mine = bf16[256,4096]{1,0:T(8,128)(2,1)S(1)} custom-call(bf16[256,2048]{1,0:T(8,128)(2,1)S(1)} %constant_dynamic-update-slice_fusion.rows.lhs, bf16[2048,4096]{1,0:T(8,128)(2,1)S(1)} %place.3.weights), custom_call_target="tpu_custom_call" | custom-call | flops 4294967296 | bytes 19922944 | tf_op jit(solution)/shard_map/forward/pallas_call | solution.py:245
  33.8 2.4 %collective-permute-start.7 = (bf16[256,4096]{1,0:T(8,128)(2,1)S(1)}, bf16[256,4096]{1,0:T(8,128)(2,1)S(1)}, u32[]{:S(2)}, u32[]{:S(2)}) collective-permute-start(bf16[256,4096]{1,0:T(8,128)(2,1)S(1)} %forward.1.gate_mine), channel_id=1, source_target_pairs={{0,1},{1,0},{2,3},{3,2},{4,5},{5,4},{6,7},{7,6},{8,9},{9,8},{10,11... | collective-permute-start | bytes 6291464 | tf_op jit(solution)/shard_map/ppermute | solution.py:335
  36.3 6.1 %place.4 = bf16[2048,4096]{1,0:T(8,128)(2,1)S(1)} custom-call(s32[2048]{0:T(1024)S(1)} %get-tuple-element.50.table, bf16[64,82048]{1,0:T(8,128)(2,1)S(1)} %stage.4.tiles), custom_call_target="tpu_custom_call" | custom-call | bytes 44056576 | tf_op jit(solution)/shard_map/place/pallas_call | solution.py:91
  42.4 4.7 %convolution_convert_fusion.up_mine = bf16[256,4096]{1,0:T(8,128)(2,1)S(1)} fusion(bf16[256,2048]{1,0:T(8,128)(2,1)S(1)} %constant_dynamic-update-slice_fusion.rows.lhs, bf16[2048,4096]{1,0:T(8,128)(2,1)S(1)} %place.4), kind=kOutput, calls=%fused_computation.6 | convolution fusion | flops 4296015872 | bytes 19922944 | tf_op jit(solution)/shard_map/dot_general | solution.py:382
  47.2 3.4 %stage.5.tiles = bf16[64,82048]{1,0:T(8,128)(2,1)S(1)} custom-call(bf16[64,40960]{1,0:T(8,128)(2,1)} %bitcast.28), custom_call_target="tpu_custom_call" | custom-call | bytes 15728640 | tf_op jit(solution)/shard_map/stage/pallas_call | solution.py:63
  50.5 6.4 %place.5.weights = bf16[4096,2048]{1,0:T(8,128)(2,1)S(1)} custom-call(s32[2048]{0:T(1024)S(1)} %reshape.60.table, bf16[64,82048]{1,0:T(8,128)(2,1)S(1)} %stage.5.tiles), custom_call_target="tpu_custom_call" | custom-call | bytes 44056576 | tf_op jit(solution)/shard_map/place/pallas_call | solution.py:91
  56.9 5.3 %output.1 = (bf16[128,4096]{1,0:T(8,128)(2,1)S(1)}, bf16[128,2048]{1,0:T(8,128)(2,1)S(1)}) custom-call(bf16[256,4096]{1,0:T(8,128)(2,1)S(1)} %forward.1.gate_mine, bf16[256,4096]{1,0:T(8,128)(2,1)S(1)} %collective-permute-done.7.gate_theirs, bf16[256,4096]{1,0:T(8,128)(2,1)S(1)} %convolution_convert_fusion.up_mine, ...), custom_call_target="tpu_custom_call" | custom-call | flops 2147483648 | bytes 22544384 | tf_op jit(solution)/shard_map/output/pallas_call | solution.py:214
  62.2 3.6 %collective-permute-start.11 = (bf16[32,2048]{1,0:T(8,128)(2,1)S(1)}, bf16[32,2048]{1,0:T(8,128)(2,1)S(1)}, u32[]{:S(2)}, u32[]{:S(2)}) collective-permute-start(bf16[32,2048]{1,0:T(8,128)(2,1)S(1)} %get-tuple-element.80), channel_id=1, source_target_pairs={{0,12},{4,8},{8,4},{12,0},{1,13},{5,9},{9,5},{13,1},{2,14},{6,10},... | collective-permute-start | bytes 393224 | tf_op jit(solution)/shard_map/ppermute | solution.py:322
  66.2 6.4 %add_multiply_fusion = (f32[256,4096]{1,0:T(8,128)}, f32[256,4096]{1,0:T(8,128)}, f32[256,4096]{1,0:T(8,128)}, f32[256,4096]{1,0:T(8,128)}) fusion(bf16[256,4096]{1,0:T(8,128)(2,1)S(1)} %collective-permute-done.8.up_theirs, bf16[256,4096]{1,0:T(8,128)(2,1)S(1)} %convolution_convert_fusion.up_mine, ...), kind=kLoop, calls=%fused_computation.7 | loop fusion | flops 15728640 | bytes 25165824 | tf_op jit(solution)/shard_map/mul | solution.py:398
  72.6 2.8 %fusion.1 = bf16[128,4096]{1,0:T(8,128)(2,1)S(1)} fusion(f32[256,4096]{1,0:T(8,128)} %get-tuple-element.79, f32[256,4096]{1,0:T(8,128)} %get-tuple-element.78), kind=kLoop, calls=%fused_computation.13 | loop fusion | flops 3145728 | bytes 5242880 | tf_op jit(solution)/shard_map/convert_element_type | solution.py:347
  75.6 2.0 %collective-permute-done.10 = bf16[32,2048]{1,0:T(8,128)(2,1)S(1)} collective-permute-done((bf16[32,2048]{1,0:T(8,128)(2,1)S(1)}, bf16[32,2048]{1,0:T(8,128)(2,1)S(1)}, u32[]{:S(2)}, u32[]{:S(2)}) %collective-permute-start.10) | collective-permute-done | bytes 131104 | tf_op jit(solution)/shard_map/ppermute | solution.py:322
  77.7 1.9 %collective-permute-start.14 = (bf16[32,2048]{1,0:T(8,128)(2,1)S(1)}, bf16[32,2048]{1,0:T(8,128)(2,1)S(1)}, u32[]{:S(2)}, u32[]{:S(2)}) collective-permute-start(bf16[32,2048]{1,0:T(8,128)(2,1)S(1)} %get-tuple-element.75), channel_id=1, source_target_pairs={{0,12},{4,8},{8,4},{12,0},{1,13},{5,9},{9,5},{13,1},{2,14},{6,10},... | collective-permute-start | bytes 393224 | tf_op jit(solution)/shard_map/ppermute | solution.py:322
  79.5 1.7 %collective-permute-start.12 = (bf16[32,2048]{1,0:T(8,128)(2,1)S(1)}, bf16[32,2048]{1,0:T(8,128)(2,1)S(1)}, u32[]{:S(2)}, u32[]{:S(2)}) collective-permute-start(bf16[32,2048]{1,0:T(8,128)(2,1)S(1)} %get-tuple-element.75), channel_id=1, source_target_pairs={{0,4},{4,0},{8,12},{12,8},{1,5},{5,1},{9,13},{13,9},{2,6},{6,2},{1... | collective-permute-start | bytes 393224 | tf_op jit(solution)/shard_map/ppermute | solution.py:322
  81.3 1.2 collective-permute-start.15
  82.5 1.3 %collective-permute-done.14 = bf16[32,2048]{1,0:T(8,128)(2,1)S(1)} collective-permute-done((bf16[32,2048]{1,0:T(8,128)(2,1)S(1)}, bf16[32,2048]{1,0:T(8,128)(2,1)S(1)}, u32[]{:S(2)}, u32[]{:S(2)}) %collective-permute-start.14) | collective-permute-done | bytes 131104 | tf_op jit(solution)/shard_map/ppermute | solution.py:322
  83.8 1.3 collective-permute-start.18
  85.1 5.6 %collective-permute-done.13 = bf16[32,2048]{1,0:T(8,128)(2,1)S(1)} collective-permute-done((bf16[32,2048]{1,0:T(8,128)(2,1)S(1)}, bf16[32,2048]{1,0:T(8,128)(2,1)S(1)}, u32[]{:S(2)}, u32[]{:S(2)}) %collective-permute-start.13) | collective-permute-done | bytes 131104 | tf_op jit(solution)/shard_map/ppermute | solution.py:322
  90.7 1.3 collective-permute-start.17
  92.3 5.9 %collective-permute-done.16 = bf16[32,2048]{1,0:T(8,128)(2,1)S(1)} collective-permute-done((bf16[32,2048]{1,0:T(8,128)(2,1)S(1)}, bf16[32,2048]{1,0:T(8,128)(2,1)S(1)}, u32[]{:S(2)}, u32[]{:S(2)}) %collective-permute-start.16) | collective-permute-done | bytes 131104 | tf_op jit(solution)/shard_map/ppermute | solution.py:322
  98.3 5.3 %back.1.refs_0_ = bf16[256,4096]{1,0:T(8,128)(2,1)S(1)} custom-call(bf16[256,2048]{1,0:T(8,128)(2,1)S(1)} %constant_dynamic-update-slice_fusion.8.slope.refs_0_, bf16[4096,2048]{1,0:T(8,128)(2,1)S(1)} %place.5.weights), custom_call_target="tpu_custom_call" | custom-call | flops 4294967296 | bytes 19922944 | tf_op jit(solution)/shard_map/back/pallas_call | solution.py:274
  103.6 1.3 collective-permute-start.19
  104.9 9.2 %gradient.5 = bf16[64,20480]{1,0:T(8,128)(2,1)} custom-call(s32[320]{0:T(512)S(1)} %fusion.34.picks, bf16[256,4096]{1,0:T(8,128)(2,1)S(1)} %pad_maximum_fusion.lhs, bf16[256,2048]{1,0:T(8,128)(2,1)S(1)} %constant_dynamic-update-slice_fusion.8.slope.refs_0_), custom_call_target="tpu_custom_call" | custom-call | flops 4294967296 | bytes 6815744 | tf_op jit(solution)/shard_map/gradient/pallas_call | solution.py:172
  114.1 9.4 %gradient.4 = bf16[64,20480]{1,0:T(8,128)(2,1)} custom-call(s32[320]{0:T(512)S(1)} %fusion.28.picks, bf16[256,2048]{1,0:T(8,128)(2,1)S(1)} %constant_dynamic-update-slice_fusion.rows.lhs, bf16[256,4096]{1,0:T(8,128)(2,1)S(1)} %back.1.refs_0_, bf16[256,4096]{1,0:T(8,128)(2,1)S(1)} %collective-permute-done.19.refs_1_, f32[256,4096]{1,0:T(8,128)S(1)} %copy-done.1), custom_call_target="tpu_custom_call" | custom-call | flops 4294967296 | bytes 16252928 | tf_op jit(solution)/shard_map/gradient/pallas_call | solution.py:172
  123.5 9.4 %gradient.3 = bf16[64,20480]{1,0:T(8,128)(2,1)} custom-call(s32[320]{0:T(512)S(1)} %fusion.22.picks, bf16[256,2048]{1,0:T(8,128)(2,1)S(1)} %constant_dynamic-update-slice_fusion.rows.lhs, bf16[256,4096]{1,0:T(8,128)(2,1)S(1)} %back.1.refs_0_, bf16[256,4096]{1,0:T(8,128)(2,1)S(1)} %collective-permute-done.19.refs_1_, f32[256,4096]{1,0:T(8,128)S(1)} %copy-done), custom_call_target="tpu_custom_call" | custom-call | flops 4294967296 | bytes 16252928 | tf_op jit(solution)/shard_map/gradient/pallas_call | solution.py:172
  (70 shorter events, 6.0 us)
Async XLA Ops:
  0.6 14.2 %collective-permute-start.1 = (bf16[32,2048]{1,0:T(8,128)(2,1)}, bf16[32,2048]{1,0:T(8,128)(2,1)S(1)}, u32[]{:S(2)}, u32[]{:S(2)}) collective-permute-start(bf16[32,2048]{1,0:T(8,128)(2,1)} %param.8), channel_id=1, source_target_pairs={{0,8},{4,12},{8,0},{12,4},{1,9},{5,13},{9,1},{13,5},{2,10},{6,14},... | collective-permute-start | bytes 393224 | tf_op jit(solution)/shard_map/ppermute | solution.py:322
  3.8 11.0 %collective-permute-start = (bf16[32,2048]{1,0:T(8,128)(2,1)}, bf16[32,2048]{1,0:T(8,128)(2,1)S(1)}, u32[]{:S(2)}, u32[]{:S(2)}) collective-permute-start(bf16[32,2048]{1,0:T(8,128)(2,1)} %param.8), channel_id=1, source_target_pairs={{0,4},{4,0},{8,12},{12,8},{1,5},{5,1},{9,13},{13,9},{2,6},{6,2},{1... | collective-permute-start | bytes 393224 | tf_op jit(solution)/shard_map/ppermute | solution.py:322
  5.1 9.7 %collective-permute-start.2 = (bf16[32,2048]{1,0:T(8,128)(2,1)}, bf16[32,2048]{1,0:T(8,128)(2,1)S(1)}, u32[]{:S(2)}, u32[]{:S(2)}) collective-permute-start(bf16[32,2048]{1,0:T(8,128)(2,1)} %param.8), channel_id=1, source_target_pairs={{0,12},{4,8},{8,4},{12,0},{1,13},{5,9},{9,5},{13,1},{2,14},{6,10},... | collective-permute-start | bytes 393224 | tf_op jit(solution)/shard_map/ppermute | solution.py:322
  11.4 3.5 %copy-start.3 = (bf16[32,2048]{1,0:T(8,128)(2,1)S(1)}, bf16[32,2048]{1,0:T(8,128)(2,1)}, u32[]{:S(2)}) copy-start(bf16[32,2048]{1,0:T(8,128)(2,1)} %param.8) | copy-start | bytes 393220
  14.9 12.6 %collective-permute-start.3 = (bf16[32,2048]{1,0:T(8,128)(2,1)S(1)}, bf16[32,2048]{1,0:T(8,128)(2,1)S(1)}, u32[]{:S(2)}, u32[]{:S(2)}) collective-permute-start(bf16[32,2048]{1,0:T(8,128)(2,1)S(1)} %copy-done.3), channel_id=1, source_target_pairs={{0,2},{2,0},{1,3},{3,1},{4,6},{6,4},{5,7},{7,5},{8,10},{10,8},{9,1... | collective-permute-start | bytes 393224 | tf_op jit(solution)/shard_map/ppermute | solution.py:322
  16.1 11.4 %collective-permute-start.4 = (bf16[32,2048]{1,0:T(8,128)(2,1)S(1)}, bf16[32,2048]{1,0:T(8,128)(2,1)S(1)}, u32[]{:S(2)}, u32[]{:S(2)}) collective-permute-start(bf16[32,2048]{1,0:T(8,128)(2,1)S(1)} %collective-permute-done), channel_id=1, source_target_pairs={{0,2},{2,0},{1,3},{3,1},{4,6},{6,4},{5,7},{7,5},{8,10},{10,8},{9,1... | collective-permute-start | bytes 393224 | tf_op jit(solution)/shard_map/ppermute | solution.py:322
  16.5 11.1 %collective-permute-start.5 = (bf16[32,2048]{1,0:T(8,128)(2,1)S(1)}, bf16[32,2048]{1,0:T(8,128)(2,1)S(1)}, u32[]{:S(2)}, u32[]{:S(2)}) collective-permute-start(bf16[32,2048]{1,0:T(8,128)(2,1)S(1)} %collective-permute-done.1), channel_id=1, source_target_pairs={{0,2},{2,0},{1,3},{3,1},{4,6},{6,4},{5,7},{7,5},{8,10},{10,8},{9,1... | collective-permute-start | bytes 393224 | tf_op jit(solution)/shard_map/ppermute | solution.py:322
  17.7 9.9 %collective-permute-start.6 = (bf16[32,2048]{1,0:T(8,128)(2,1)S(1)}, bf16[32,2048]{1,0:T(8,128)(2,1)S(1)}, u32[]{:S(2)}, u32[]{:S(2)}) collective-permute-start(bf16[32,2048]{1,0:T(8,128)(2,1)S(1)} %collective-permute-done.2), channel_id=1, source_target_pairs={{0,2},{2,0},{1,3},{3,1},{4,6},{6,4},{5,7},{7,5},{8,10},{10,8},{9,1... | collective-permute-start | bytes 393224 | tf_op jit(solution)/shard_map/ppermute | solution.py:322
  33.8 23.1 %collective-permute-start.7 = (bf16[256,4096]{1,0:T(8,128)(2,1)S(1)}, bf16[256,4096]{1,0:T(8,128)(2,1)S(1)}, u32[]{:S(2)}, u32[]{:S(2)}) collective-permute-start(bf16[256,4096]{1,0:T(8,128)(2,1)S(1)} %forward.1.gate_mine), channel_id=1, source_target_pairs={{0,1},{1,0},{2,3},{3,2},{4,5},{5,4},{6,7},{7,6},{8,9},{9,8},{10,11... | collective-permute-start | bytes 6291464 | tf_op jit(solution)/shard_map/ppermute | solution.py:335
  47.1 9.8 %collective-permute-start.8 = (bf16[256,4096]{1,0:T(8,128)(2,1)S(1)}, bf16[256,4096]{1,0:T(8,128)(2,1)S(1)}, u32[]{:S(2)}, u32[]{:S(2)}) collective-permute-start(bf16[256,4096]{1,0:T(8,128)(2,1)S(1)} %convolution_convert_fusion.up_mine), channel_id=1, source_target_pairs={{0,1},{1,0},{2,3},{3,2},{4,5},{5,4},{6,7},{7,6},{8,9},{9,8},{10,11... | collective-permute-start | bytes 6291464 | tf_op jit(solution)/shard_map/ppermute | solution.py:335
  62.2 13.3 %collective-permute-start.11 = (bf16[32,2048]{1,0:T(8,128)(2,1)S(1)}, bf16[32,2048]{1,0:T(8,128)(2,1)S(1)}, u32[]{:S(2)}, u32[]{:S(2)}) collective-permute-start(bf16[32,2048]{1,0:T(8,128)(2,1)S(1)} %get-tuple-element.80), channel_id=1, source_target_pairs={{0,12},{4,8},{8,4},{12,0},{1,13},{5,9},{9,5},{13,1},{2,14},{6,10},... | collective-permute-start | bytes 393224 | tf_op jit(solution)/shard_map/ppermute | solution.py:322
  65.8 11.7 %collective-permute-start.10 = (bf16[32,2048]{1,0:T(8,128)(2,1)S(1)}, bf16[32,2048]{1,0:T(8,128)(2,1)S(1)}, u32[]{:S(2)}, u32[]{:S(2)}) collective-permute-start(bf16[32,2048]{1,0:T(8,128)(2,1)S(1)} %get-tuple-element.81), channel_id=1, source_target_pairs={{0,8},{4,12},{8,0},{12,4},{1,9},{5,13},{9,1},{13,5},{2,10},{6,14},... | collective-permute-start | bytes 393224 | tf_op jit(solution)/shard_map/ppermute | solution.py:322
  65.8 11.7 %collective-permute-start.9 = (bf16[32,2048]{1,0:T(8,128)(2,1)S(1)}, bf16[32,2048]{1,0:T(8,128)(2,1)S(1)}, u32[]{:S(2)}, u32[]{:S(2)}) collective-permute-start(bf16[32,2048]{1,0:T(8,128)(2,1)S(1)} %get-tuple-element.82), channel_id=1, source_target_pairs={{0,4},{4,0},{8,12},{12,8},{1,5},{5,1},{9,13},{13,9},{2,6},{6,2},{1... | collective-permute-start | bytes 393224 | tf_op jit(solution)/shard_map/ppermute | solution.py:322
  72.6 5.0 %copy-start.2 = (bf16[32,2048]{1,0:T(8,128)(2,1)S(1)}, bf16[32,2048]{1,0:T(8,128)(2,1)}, u32[]{:S(2)}) copy-start(bf16[32,2048]{1,0:T(8,128)(2,1)} %param.9) | copy-start | bytes 393220
  77.7 6.2 %collective-permute-start.14 = (bf16[32,2048]{1,0:T(8,128)(2,1)S(1)}, bf16[32,2048]{1,0:T(8,128)(2,1)S(1)}, u32[]{:S(2)}, u32[]{:S(2)}) collective-permute-start(bf16[32,2048]{1,0:T(8,128)(2,1)S(1)} %get-tuple-element.75), channel_id=1, source_target_pairs={{0,12},{4,8},{8,4},{12,0},{1,13},{5,9},{9,5},{13,1},{2,14},{6,10},... | collective-permute-start | bytes 393224 | tf_op jit(solution)/shard_map/ppermute | solution.py:322
  79.5 11.2 %collective-permute-start.13 = (bf16[32,2048]{1,0:T(8,128)(2,1)S(1)}, bf16[32,2048]{1,0:T(8,128)(2,1)S(1)}, u32[]{:S(2)}, u32[]{:S(2)}) collective-permute-start(bf16[32,2048]{1,0:T(8,128)(2,1)S(1)} %get-tuple-element.75), channel_id=1, source_target_pairs={{0,8},{4,12},{8,0},{12,4},{1,9},{5,13},{9,1},{13,5},{2,10},{6,14},... | collective-permute-start | bytes 393224 | tf_op jit(solution)/shard_map/ppermute | solution.py:322
  79.5 12.5 %collective-permute-start.12 = (bf16[32,2048]{1,0:T(8,128)(2,1)S(1)}, bf16[32,2048]{1,0:T(8,128)(2,1)S(1)}, u32[]{:S(2)}, u32[]{:S(2)}) collective-permute-start(bf16[32,2048]{1,0:T(8,128)(2,1)S(1)} %get-tuple-element.75), channel_id=1, source_target_pairs={{0,4},{4,0},{8,12},{12,8},{1,5},{5,1},{9,13},{13,9},{2,6},{6,2},{1... | collective-permute-start | bytes 393224 | tf_op jit(solution)/shard_map/ppermute | solution.py:322
  81.3 11.0 %collective-permute-start.15 = (bf16[32,2048]{1,0:T(8,128)(2,1)S(1)}, bf16[32,2048]{1,0:T(8,128)(2,1)S(1)}, u32[]{:S(2)}, u32[]{:S(2)}) collective-permute-start(bf16[32,2048]{1,0:T(8,128)(2,1)S(1)} %get-tuple-element.75), channel_id=1, source_target_pairs={{0,2},{2,0},{1,3},{3,1},{4,6},{6,4},{5,7},{7,5},{8,10},{10,8},{9,1... | collective-permute-start | bytes 393224 | tf_op jit(solution)/shard_map/ppermute | solution.py:322
  83.8 14.4 %collective-permute-start.18 = (bf16[32,2048]{1,0:T(8,128)(2,1)S(1)}, bf16[32,2048]{1,0:T(8,128)(2,1)S(1)}, u32[]{:S(2)}, u32[]{:S(2)}) collective-permute-start(bf16[32,2048]{1,0:T(8,128)(2,1)S(1)} %collective-permute-done.14), channel_id=1, source_target_pairs={{0,2},{2,0},{1,3},{3,1},{4,6},{6,4},{5,7},{7,5},{8,10},{10,8},{9,1... | collective-permute-start | bytes 393224 | tf_op jit(solution)/shard_map/ppermute | solution.py:322
  90.7 7.5 %collective-permute-start.17 = (bf16[32,2048]{1,0:T(8,128)(2,1)S(1)}, bf16[32,2048]{1,0:T(8,128)(2,1)S(1)}, u32[]{:S(2)}, u32[]{:S(2)}) collective-permute-start(bf16[32,2048]{1,0:T(8,128)(2,1)S(1)} %collective-permute-done.13), channel_id=1, source_target_pairs={{0,2},{2,0},{1,3},{3,1},{4,6},{6,4},{5,7},{7,5},{8,10},{10,8},{9,1... | collective-permute-start | bytes 393224 | tf_op jit(solution)/shard_map/ppermute | solution.py:322
  92.0 6.2 %collective-permute-start.16 = (bf16[32,2048]{1,0:T(8,128)(2,1)S(1)}, bf16[32,2048]{1,0:T(8,128)(2,1)S(1)}, u32[]{:S(2)}, u32[]{:S(2)}) collective-permute-start(bf16[32,2048]{1,0:T(8,128)(2,1)S(1)} %collective-permute-done.12), channel_id=1, source_target_pairs={{0,2},{2,0},{1,3},{3,1},{4,6},{6,4},{5,7},{7,5},{8,10},{10,8},{9,1... | collective-permute-start | bytes 393224 | tf_op jit(solution)/shard_map/ppermute | solution.py:322
  103.6 10.5 %copy-start.1 = (f32[256,4096]{1,0:T(8,128)S(1)}, f32[256,4096]{1,0:T(8,128)}, u32[]{:S(2)}) copy-start(f32[256,4096]{1,0:T(8,128)} %get-tuple-element.68.refs_2_) | copy-start | bytes 12582916
  103.6 10.5 %collective-permute-start.19 = (bf16[256,4096]{1,0:T(8,128)(2,1)S(1)}, bf16[256,4096]{1,0:T(8,128)(2,1)S(1)}, u32[]{:S(2)}, u32[]{:S(2)}) collective-permute-start(bf16[256,4096]{1,0:T(8,128)(2,1)S(1)} %back.1.refs_0_), channel_id=1, source_target_pairs={{0,1},{1,0},{2,3},{3,2},{4,5},{5,4},{6,7},{7,6},{8,9},{9,8},{10,11... | collective-permute-start | bytes 6291464 | tf_op jit(solution)/shard_map/ppermute | solution.py:335
  114.1 9.4 %copy-start = (f32[256,4096]{1,0:T(8,128)S(1)}, f32[256,4096]{1,0:T(8,128)}, u32[]{:S(2)}) copy-start(f32[256,4096]{1,0:T(8,128)} %get-tuple-element.66.refs_2_) | copy-start | bytes 12582916

commit v8 on v7

--- a/solution.py
+++ b/solution.py
@@ -14,7 +14,7 @@
 SLOPE_SCALE = 0.0625
 STAGE_VMEM = 15 * 2**20
 PRODUCT_VMEM = 14 * 2**20
-DEPTH_PART = 512
+DEPTH_PART = 1024
 GRADIENT_VMEM = 44 * 2**20
 
 
@@ -161,7 +161,7 @@
 
 def gradient(lhs, terms, picks):
     n_rows, n_cols = lhs.shape[1] // BLK, terms[0].shape[1] // BLK
-    rows_per_step = min(16, n_rows)
+    rows_per_step = min(32, n_rows)
     n_steps = n_rows // rows_per_step
     scratch = [
         pltpu.VMEM((n_rows * n_cols // 2 + 1, BLK, PAIR), jnp.bfloat16),

time: 133 us -> 131 us (0.985)
  Pallas kernels: 73.5 us -> 71.2 us
  transfers between devices with their start and end apart: 20 -> 20, of which waited for: 4 -> 4; matrix products, arithmetic and copies ran while one was open for 15% -> 16% of each run, Pallas kernels for 29% -> 29%
where the time goes in v8:
time: 131 us
  Pallas kernels  71.2 us (54%)
  starting transfers between devices  22.8 us (17%)
  waiting for transfers between devices  15.1 us (12%)
  other arithmetic  13.7 us (10%)
  matrix products  4.71 us (4%)
  local copies, waits for them, and re-layouts  2.17 us (2%)
    pallas_call x3, Pallas kernels, gradient(): pl.pallas_call(functools.partial(gradient_kernel, n_steps, rows_per_step,...  26.9 us
    ppermute x17, starting transfers between devices, shift(): lax.ppermute(values, axis, [(i, i ^ k) for i in range(n)])  19 us
    pallas_call x3, Pallas kernels, place(): pl.pallas_call(functools.partial(place_kernel, rows_per_step, n_cols), gr...  18.5 us
    ppermute x17, waiting for transfers between devices, shift(): lax.ppermute(values, axis, [(i, i ^ k) for i in range(n)])  15.1 us
    pallas_call x3, Pallas kernels, staged(): pl.pallas_call(functools.partial(stage_kernel, half_cap, chunks), in_spec...  10.1 us
    mul x1, other arithmetic, local(): gate_factor = up * sigmoid_gate * (1.0 + gate * (1.0 - sigmoid_gate))  6.39 us
    pallas_call x1, Pallas kernels, forward_product(): pl.pallas_call(forward_kernel, grid=(width // part,), in_specs=[pl.BlockS...  6.23 us
    pallas_call x1, Pallas kernels, back_product(): pl.pallas_call(back_kernel, grid=(width // part,), in_specs=[pl.BlockSpec...  5.26 us
  transfers between devices with their start and end apart: 20, of which 4 were waited for; matrix products, arithmetic and copies ran while one was open for 16% of the time, Pallas kernels for 29%

profile of v8, /device:TPU:1, one launch (start us, length us, event | category | flops | bytes accessed | tf_op | source)
XLA Modules:
  0.0 130.7 jit_solution(10485067527797402843)
XLA Ops:
  0.6 3.2 %collective-permute-start.1 = (bf16[32,2048]{1,0:T(8,128)(2,1)}, bf16[32,2048]{1,0:T(8,128)(2,1)S(1)}, u32[]{:S(2)}, u32[]{:S(2)}) collective-permute-start(bf16[32,2048]{1,0:T(8,128)(2,1)} %param.8), channel_id=1, source_target_pairs={{0,8},{4,12},{8,0},{12,4},{1,9},{5,13},{9,1},{13,5},{2,10},{6,14},... | collective-permute-start | bytes 393224 | tf_op jit(solution)/shard_map/ppermute | solution.py:322
  3.8 1.3 collective-permute-start
  8.9 2.0 %select_reduce_fusion = (s32[2048]{0:T(1024)S(1)}, s32[2048]{0:T(1024)S(1)}, s32[2048]{0:T(1024)S(1)}) fusion(s32[640]{0:T(1024)S(1)} %reduce.2, s32[640]{0:T(1024)S(1)} %iota_add_fusion, s32[640]{0:T(1024)S(1)} %reduce.1, s32[640]{0:T(1024)S(1)} %reduce), kind=kLoop, calls=%fused_computation | loop fusion | flops 11790336 | bytes 34816 | tf_op jit(solution)/shard_map/reduce_sum | solution.py:297
  11.4 3.4 %stage.3.tiles = bf16[64,82048]{1,0:T(8,128)(2,1)S(1)} custom-call(bf16[64,40960]{1,0:T(8,128)(2,1)} %bitcast.26), custom_call_target="tpu_custom_call" | custom-call | bytes 15728640 | tf_op jit(solution)/shard_map/stage/pallas_call | solution.py:63
  14.9 1.3 collective-permute-start.3
  16.5 1.2 collective-permute-start.5
  18.0 6.1 %place.3.weights = bf16[2048,4096]{1,0:T(8,128)(2,1)S(1)} custom-call(s32[2048]{0:T(1024)S(1)} %get-tuple-element.43.table, bf16[64,82048]{1,0:T(8,128)(2,1)S(1)} %stage.3.tiles), custom_call_target="tpu_custom_call" | custom-call | bytes 44056576 | tf_op jit(solution)/shard_map/place/pallas_call | solution.py:91
  24.1 3.4 %stage.4.tiles = bf16[64,82048]{1,0:T(8,128)(2,1)S(1)} custom-call(bf16[64,40960]{1,0:T(8,128)(2,1)} %bitcast.27), custom_call_target="tpu_custom_call" | custom-call | bytes 15728640 | tf_op jit(solution)/shard_map/stage/pallas_call | solution.py:63
  27.6 6.2 %forward.1.gate_mine = bf16[256,4096]{1,0:T(8,128)(2,1)S(1)} custom-call(bf16[256,2048]{1,0:T(8,128)(2,1)S(1)} %constant_dynamic-update-slice_fusion.rows.lhs, bf16[2048,4096]{1,0:T(8,128)(2,1)S(1)} %place.3.weights), custom_call_target="tpu_custom_call" | custom-call | flops 4294967296 | bytes 19922944 | tf_op jit(solution)/shard_map/forward/pallas_call | solution.py:245
  33.8 2.4 %collective-permute-start.7 = (bf16[256,4096]{1,0:T(8,128)(2,1)S(1)}, bf16[256,4096]{1,0:T(8,128)(2,1)S(1)}, u32[]{:S(2)}, u32[]{:S(2)}) collective-permute-start(bf16[256,4096]{1,0:T(8,128)(2,1)S(1)} %forward.1.gate_mine), channel_id=1, source_target_pairs={{0,1},{1,0},{2,3},{3,2},{4,5},{5,4},{6,7},{7,6},{8,9},{9,8},{10,11... | collective-permute-start | bytes 6291464 | tf_op jit(solution)/shard_map/ppermute | solution.py:335
  36.3 6.1 %place.4 = bf16[2048,4096]{1,0:T(8,128)(2,1)S(1)} custom-call(s32[2048]{0:T(1024)S(1)} %get-tuple-element.50.table, bf16[64,82048]{1,0:T(8,128)(2,1)S(1)} %stage.4.tiles), custom_call_target="tpu_custom_call" | custom-call | bytes 44056576 | tf_op jit(solution)/shard_map/place/pallas_call | solution.py:91
  42.4 4.7 %convolution_convert_fusion.up_mine = bf16[256,4096]{1,0:T(8,128)(2,1)S(1)} fusion(bf16[256,2048]{1,0:T(8,128)(2,1)S(1)} %constant_dynamic-update-slice_fusion.rows.lhs, bf16[2048,4096]{1,0:T(8,128)(2,1)S(1)} %place.4), kind=kOutput, calls=%fused_computation.6 | convolution fusion | flops 4296015872 | bytes 19922944 | tf_op jit(solution)/shard_map/dot_general | solution.py:382
  47.2 3.4 %stage.5.tiles = bf16[64,82048]{1,0:T(8,128)(2,1)S(1)} custom-call(bf16[64,40960]{1,0:T(8,128)(2,1)} %bitcast.28), custom_call_target="tpu_custom_call" | custom-call | bytes 15728640 | tf_op jit(solution)/shard_map/stage/pallas_call | solution.py:63
  50.5 6.4 %place.5.weights = bf16[4096,2048]{1,0:T(8,128)(2,1)S(1)} custom-call(s32[2048]{0:T(1024)S(1)} %reshape.60.table, bf16[64,82048]{1,0:T(8,128)(2,1)S(1)} %stage.5.tiles), custom_call_target="tpu_custom_call" | custom-call | bytes 44056576 | tf_op jit(solution)/shard_map/place/pallas_call | solution.py:91
  56.9 4.1 %output.1 = (bf16[128,4096]{1,0:T(8,128)(2,1)S(1)}, bf16[128,2048]{1,0:T(8,128)(2,1)S(1)}) custom-call(bf16[256,4096]{1,0:T(8,128)(2,1)S(1)} %forward.1.gate_mine, bf16[256,4096]{1,0:T(8,128)(2,1)S(1)} %collective-permute-done.7.gate_theirs, bf16[256,4096]{1,0:T(8,128)(2,1)S(1)} %convolution_convert_fusion.up_mine, ...), custom_call_target="tpu_custom_call" | custom-call | flops 2147483648 | bytes 22544384 | tf_op jit(solution)/shard_map/output/pallas_call | solution.py:214
  61.0 3.6 %collective-permute-start.11 = (bf16[32,2048]{1,0:T(8,128)(2,1)S(1)}, bf16[32,2048]{1,0:T(8,128)(2,1)S(1)}, u32[]{:S(2)}, u32[]{:S(2)}) collective-permute-start(bf16[32,2048]{1,0:T(8,128)(2,1)S(1)} %get-tuple-element.80), channel_id=1, source_target_pairs={{0,12},{4,8},{8,4},{12,0},{1,13},{5,9},{9,5},{13,1},{2,14},{6,10},... | collective-permute-start | bytes 393224 | tf_op jit(solution)/shard_map/ppermute | solution.py:322
  65.0 6.4 %add_multiply_fusion = (f32[256,4096]{1,0:T(8,128)}, f32[256,4096]{1,0:T(8,128)}, f32[256,4096]{1,0:T(8,128)}, f32[256,4096]{1,0:T(8,128)}) fusion(bf16[256,4096]{1,0:T(8,128)(2,1)S(1)} %collective-permute-done.8.up_theirs, bf16[256,4096]{1,0:T(8,128)(2,1)S(1)} %convolution_convert_fusion.up_mine, ...), kind=kLoop, calls=%fused_computation.7 | loop fusion | flops 15728640 | bytes 25165824 | tf_op jit(solution)/shard_map/mul | solution.py:398
  71.4 2.8 %fusion.1 = bf16[128,4096]{1,0:T(8,128)(2,1)S(1)} fusion(f32[256,4096]{1,0:T(8,128)} %get-tuple-element.79, f32[256,4096]{1,0:T(8,128)} %get-tuple-element.78), kind=kLoop, calls=%fused_computation.13 | loop fusion | flops 3145728 | bytes 5242880 | tf_op jit(solution)/shard_map/convert_element_type | solution.py:347
  74.4 2.0 %collective-permute-done.10 = bf16[32,2048]{1,0:T(8,128)(2,1)S(1)} collective-permute-done((bf16[32,2048]{1,0:T(8,128)(2,1)S(1)}, bf16[32,2048]{1,0:T(8,128)(2,1)S(1)}, u32[]{:S(2)}, u32[]{:S(2)}) %collective-permute-start.10) | collective-permute-done | bytes 131104 | tf_op jit(solution)/shard_map/ppermute | solution.py:322
  76.5 1.9 %collective-permute-start.14 = (bf16[32,2048]{1,0:T(8,128)(2,1)S(1)}, bf16[32,2048]{1,0:T(8,128)(2,1)S(1)}, u32[]{:S(2)}, u32[]{:S(2)}) collective-permute-start(bf16[32,2048]{1,0:T(8,128)(2,1)S(1)} %get-tuple-element.75), channel_id=1, source_target_pairs={{0,12},{4,8},{8,4},{12,0},{1,13},{5,9},{9,5},{13,1},{2,14},{6,10},... | collective-permute-start | bytes 393224 | tf_op jit(solution)/shard_map/ppermute | solution.py:322
  78.4 1.7 %collective-permute-start.12 = (bf16[32,2048]{1,0:T(8,128)(2,1)S(1)}, bf16[32,2048]{1,0:T(8,128)(2,1)S(1)}, u32[]{:S(2)}, u32[]{:S(2)}) collective-permute-start(bf16[32,2048]{1,0:T(8,128)(2,1)S(1)} %get-tuple-element.75), channel_id=1, source_target_pairs={{0,4},{4,0},{8,12},{12,8},{1,5},{5,1},{9,13},{13,9},{2,6},{6,2},{1... | collective-permute-start | bytes 393224 | tf_op jit(solution)/shard_map/ppermute | solution.py:322
  80.1 1.2 collective-permute-start.15
  81.3 1.4 %collective-permute-done.14 = bf16[32,2048]{1,0:T(8,128)(2,1)S(1)} collective-permute-done((bf16[32,2048]{1,0:T(8,128)(2,1)S(1)}, bf16[32,2048]{1,0:T(8,128)(2,1)S(1)}, u32[]{:S(2)}, u32[]{:S(2)}) %collective-permute-start.14) | collective-permute-done | bytes 131104 | tf_op jit(solution)/shard_map/ppermute | solution.py:322
  82.7 1.2 collective-permute-start.18
  83.9 5.7 %collective-permute-done.13 = bf16[32,2048]{1,0:T(8,128)(2,1)S(1)} collective-permute-done((bf16[32,2048]{1,0:T(8,128)(2,1)S(1)}, bf16[32,2048]{1,0:T(8,128)(2,1)S(1)}, u32[]{:S(2)}, u32[]{:S(2)}) %collective-permute-start.13) | collective-permute-done | bytes 131104 | tf_op jit(solution)/shard_map/ppermute | solution.py:322
  89.6 1.2 collective-permute-start.17
  91.2 5.9 %collective-permute-done.16 = bf16[32,2048]{1,0:T(8,128)(2,1)S(1)} collective-permute-done((bf16[32,2048]{1,0:T(8,128)(2,1)S(1)}, bf16[32,2048]{1,0:T(8,128)(2,1)S(1)}, u32[]{:S(2)}, u32[]{:S(2)}) %collective-permute-start.16) | collective-permute-done | bytes 131104 | tf_op jit(solution)/shard_map/ppermute | solution.py:322
  97.2 5.3 %back.1.refs_0_ = bf16[256,4096]{1,0:T(8,128)(2,1)S(1)} custom-call(bf16[256,2048]{1,0:T(8,128)(2,1)S(1)} %constant_dynamic-update-slice_fusion.8.slope.refs_0_, bf16[4096,2048]{1,0:T(8,128)(2,1)S(1)} %place.5.weights), custom_call_target="tpu_custom_call" | custom-call | flops 4294967296 | bytes 19922944 | tf_op jit(solution)/shard_map/back/pallas_call | solution.py:274
  102.5 1.3 collective-permute-start.19
  103.7 8.8 %gradient.5 = bf16[64,20480]{1,0:T(8,128)(2,1)} custom-call(s32[320]{0:T(512)S(1)} %fusion.34.picks, bf16[256,4096]{1,0:T(8,128)(2,1)S(1)} %pad_maximum_fusion.lhs, bf16[256,2048]{1,0:T(8,128)(2,1)S(1)} %constant_dynamic-update-slice_fusion.8.slope.refs_0_), custom_call_target="tpu_custom_call" | custom-call | flops 4294967296 | bytes 6815744 | tf_op jit(solution)/shard_map/gradient/pallas_call | solution.py:172
  112.5 9.1 %gradient.4 = bf16[64,20480]{1,0:T(8,128)(2,1)} custom-call(s32[320]{0:T(512)S(1)} %fusion.28.picks, bf16[256,2048]{1,0:T(8,128)(2,1)S(1)} %constant_dynamic-update-slice_fusion.rows.lhs, bf16[256,4096]{1,0:T(8,128)(2,1)S(1)} %back.1.refs_0_, bf16[256,4096]{1,0:T(8,128)(2,1)S(1)} %collective-permute-done.19.refs_1_, f32[256,4096]{1,0:T(8,128)S(1)} %copy-done.1), custom_call_target="tpu_custom_call" | custom-call | flops 4294967296 | bytes 16252928 | tf_op jit(solution)/shard_map/gradient/pallas_call | solution.py:172
  121.6 9.1 %gradient.3 = bf16[64,20480]{1,0:T(8,128)(2,1)} custom-call(s32[320]{0:T(512)S(1)} %fusion.22.picks, bf16[256,2048]{1,0:T(8,128)(2,1)S(1)} %constant_dynamic-update-slice_fusion.rows.lhs, bf16[256,4096]{1,0:T(8,128)(2,1)S(1)} %back.1.refs_0_, bf16[256,4096]{1,0:T(8,128)(2,1)S(1)} %collective-permute-done.19.refs_1_, f32[256,4096]{1,0:T(8,128)S(1)} %copy-done), custom_call_target="tpu_custom_call" | custom-call | flops 4294967296 | bytes 16252928 | tf_op jit(solution)/shard_map/gradient/pallas_call | solution.py:172
  (70 shorter events, 6.0 us)
Async XLA Ops:
  0.6 14.2 %collective-permute-start.1 = (bf16[32,2048]{1,0:T(8,128)(2,1)}, bf16[32,2048]{1,0:T(8,128)(2,1)S(1)}, u32[]{:S(2)}, u32[]{:S(2)}) collective-permute-start(bf16[32,2048]{1,0:T(8,128)(2,1)} %param.8), channel_id=1, source_target_pairs={{0,8},{4,12},{8,0},{12,4},{1,9},{5,13},{9,1},{13,5},{2,10},{6,14},... | collective-permute-start | bytes 393224 | tf_op jit(solution)/shard_map/ppermute | solution.py:322
  3.8 11.0 %collective-permute-start = (bf16[32,2048]{1,0:T(8,128)(2,1)}, bf16[32,2048]{1,0:T(8,128)(2,1)S(1)}, u32[]{:S(2)}, u32[]{:S(2)}) collective-permute-start(bf16[32,2048]{1,0:T(8,128)(2,1)} %param.8), channel_id=1, source_target_pairs={{0,4},{4,0},{8,12},{12,8},{1,5},{5,1},{9,13},{13,9},{2,6},{6,2},{1... | collective-permute-start | bytes 393224 | tf_op jit(solution)/shard_map/ppermute | solution.py:322
  5.1 9.7 %collective-permute-start.2 = (bf16[32,2048]{1,0:T(8,128)(2,1)}, bf16[32,2048]{1,0:T(8,128)(2,1)S(1)}, u32[]{:S(2)}, u32[]{:S(2)}) collective-permute-start(bf16[32,2048]{1,0:T(8,128)(2,1)} %param.8), channel_id=1, source_target_pairs={{0,12},{4,8},{8,4},{12,0},{1,13},{5,9},{9,5},{13,1},{2,14},{6,10},... | collective-permute-start | bytes 393224 | tf_op jit(solution)/shard_map/ppermute | solution.py:322
  11.4 3.5 %copy-start.3 = (bf16[32,2048]{1,0:T(8,128)(2,1)S(1)}, bf16[32,2048]{1,0:T(8,128)(2,1)}, u32[]{:S(2)}) copy-start(bf16[32,2048]{1,0:T(8,128)(2,1)} %param.8) | copy-start | bytes 393220
  14.9 12.6 %collective-permute-start.3 = (bf16[32,2048]{1,0:T(8,128)(2,1)S(1)}, bf16[32,2048]{1,0:T(8,128)(2,1)S(1)}, u32[]{:S(2)}, u32[]{:S(2)}) collective-permute-start(bf16[32,2048]{1,0:T(8,128)(2,1)S(1)} %copy-done.3), channel_id=1, source_target_pairs={{0,2},{2,0},{1,3},{3,1},{4,6},{6,4},{5,7},{7,5},{8,10},{10,8},{9,1... | collective-permute-start | bytes 393224 | tf_op jit(solution)/shard_map/ppermute | solution.py:322
  16.1 11.4 %collective-permute-start.4 = (bf16[32,2048]{1,0:T(8,128)(2,1)S(1)}, bf16[32,2048]{1,0:T(8,128)(2,1)S(1)}, u32[]{:S(2)}, u32[]{:S(2)}) collective-permute-start(bf16[32,2048]{1,0:T(8,128)(2,1)S(1)} %collective-permute-done), channel_id=1, source_target_pairs={{0,2},{2,0},{1,3},{3,1},{4,6},{6,4},{5,7},{7,5},{8,10},{10,8},{9,1... | collective-permute-start | bytes 393224 | tf_op jit(solution)/shard_map/ppermute | solution.py:322
  16.5 11.1 %collective-permute-start.5 = (bf16[32,2048]{1,0:T(8,128)(2,1)S(1)}, bf16[32,2048]{1,0:T(8,128)(2,1)S(1)}, u32[]{:S(2)}, u32[]{:S(2)}) collective-permute-start(bf16[32,2048]{1,0:T(8,128)(2,1)S(1)} %collective-permute-done.1), channel_id=1, source_target_pairs={{0,2},{2,0},{1,3},{3,1},{4,6},{6,4},{5,7},{7,5},{8,10},{10,8},{9,1... | collective-permute-start | bytes 393224 | tf_op jit(solution)/shard_map/ppermute | solution.py:322
  17.7 9.9 %collective-permute-start.6 = (bf16[32,2048]{1,0:T(8,128)(2,1)S(1)}, bf16[32,2048]{1,0:T(8,128)(2,1)S(1)}, u32[]{:S(2)}, u32[]{:S(2)}) collective-permute-start(bf16[32,2048]{1,0:T(8,128)(2,1)S(1)} %collective-permute-done.2), channel_id=1, source_target_pairs={{0,2},{2,0},{1,3},{3,1},{4,6},{6,4},{5,7},{7,5},{8,10},{10,8},{9,1... | collective-permute-start | bytes 393224 | tf_op jit(solution)/shard_map/ppermute | solution.py:322
  33.8 23.1 %collective-permute-start.7 = (bf16[256,4096]{1,0:T(8,128)(2,1)S(1)}, bf16[256,4096]{1,0:T(8,128)(2,1)S(1)}, u32[]{:S(2)}, u32[]{:S(2)}) collective-permute-start(bf16[256,4096]{1,0:T(8,128)(2,1)S(1)} %forward.1.gate_mine), channel_id=1, source_target_pairs={{0,1},{1,0},{2,3},{3,2},{4,5},{5,4},{6,7},{7,6},{8,9},{9,8},{10,11... | collective-permute-start | bytes 6291464 | tf_op jit(solution)/shard_map/ppermute | solution.py:335
  47.1 9.8 %collective-permute-start.8 = (bf16[256,4096]{1,0:T(8,128)(2,1)S(1)}, bf16[256,4096]{1,0:T(8,128)(2,1)S(1)}, u32[]{:S(2)}, u32[]{:S(2)}) collective-permute-start(bf16[256,4096]{1,0:T(8,128)(2,1)S(1)} %convolution_convert_fusion.up_mine), channel_id=1, source_target_pairs={{0,1},{1,0},{2,3},{3,2},{4,5},{5,4},{6,7},{7,6},{8,9},{9,8},{10,11... | collective-permute-start | bytes 6291464 | tf_op jit(solution)/shard_map/ppermute | solution.py:335
  61.0 13.3 %collective-permute-start.11 = (bf16[32,2048]{1,0:T(8,128)(2,1)S(1)}, bf16[32,2048]{1,0:T(8,128)(2,1)S(1)}, u32[]{:S(2)}, u32[]{:S(2)}) collective-permute-start(bf16[32,2048]{1,0:T(8,128)(2,1)S(1)} %get-tuple-element.80), channel_id=1, source_target_pairs={{0,12},{4,8},{8,4},{12,0},{1,13},{5,9},{9,5},{13,1},{2,14},{6,10},... | collective-permute-start | bytes 393224 | tf_op jit(solution)/shard_map/ppermute | solution.py:322
  64.6 11.8 %collective-permute-start.10 = (bf16[32,2048]{1,0:T(8,128)(2,1)S(1)}, bf16[32,2048]{1,0:T(8,128)(2,1)S(1)}, u32[]{:S(2)}, u32[]{:S(2)}) collective-permute-start(bf16[32,2048]{1,0:T(8,128)(2,1)S(1)} %get-tuple-element.81), channel_id=1, source_target_pairs={{0,8},{4,12},{8,0},{12,4},{1,9},{5,13},{9,1},{13,5},{2,10},{6,14},... | collective-permute-start | bytes 393224 | tf_op jit(solution)/shard_map/ppermute | solution.py:322
  64.6 11.8 %collective-permute-start.9 = (bf16[32,2048]{1,0:T(8,128)(2,1)S(1)}, bf16[32,2048]{1,0:T(8,128)(2,1)S(1)}, u32[]{:S(2)}, u32[]{:S(2)}) collective-permute-start(bf16[32,2048]{1,0:T(8,128)(2,1)S(1)} %get-tuple-element.82), channel_id=1, source_target_pairs={{0,4},{4,0},{8,12},{12,8},{1,5},{5,1},{9,13},{13,9},{2,6},{6,2},{1... | collective-permute-start | bytes 393224 | tf_op jit(solution)/shard_map/ppermute | solution.py:322
  71.4 5.0 %copy-start.2 = (bf16[32,2048]{1,0:T(8,128)(2,1)S(1)}, bf16[32,2048]{1,0:T(8,128)(2,1)}, u32[]{:S(2)}) copy-start(bf16[32,2048]{1,0:T(8,128)(2,1)} %param.9) | copy-start | bytes 393220
  76.5 6.2 %collective-permute-start.14 = (bf16[32,2048]{1,0:T(8,128)(2,1)S(1)}, bf16[32,2048]{1,0:T(8,128)(2,1)S(1)}, u32[]{:S(2)}, u32[]{:S(2)}) collective-permute-start(bf16[32,2048]{1,0:T(8,128)(2,1)S(1)} %get-tuple-element.75), channel_id=1, source_target_pairs={{0,12},{4,8},{8,4},{12,0},{1,13},{5,9},{9,5},{13,1},{2,14},{6,10},... | collective-permute-start | bytes 393224 | tf_op jit(solution)/shard_map/ppermute | solution.py:322
  78.4 11.2 %collective-permute-start.13 = (bf16[32,2048]{1,0:T(8,128)(2,1)S(1)}, bf16[32,2048]{1,0:T(8,128)(2,1)S(1)}, u32[]{:S(2)}, u32[]{:S(2)}) collective-permute-start(bf16[32,2048]{1,0:T(8,128)(2,1)S(1)} %get-tuple-element.75), channel_id=1, source_target_pairs={{0,8},{4,12},{8,0},{12,4},{1,9},{5,13},{9,1},{13,5},{2,10},{6,14},... | collective-permute-start | bytes 393224 | tf_op jit(solution)/shard_map/ppermute | solution.py:322
  78.4 12.4 %collective-permute-start.12 = (bf16[32,2048]{1,0:T(8,128)(2,1)S(1)}, bf16[32,2048]{1,0:T(8,128)(2,1)S(1)}, u32[]{:S(2)}, u32[]{:S(2)}) collective-permute-start(bf16[32,2048]{1,0:T(8,128)(2,1)S(1)} %get-tuple-element.75), channel_id=1, source_target_pairs={{0,4},{4,0},{8,12},{12,8},{1,5},{5,1},{9,13},{13,9},{2,6},{6,2},{1... | collective-permute-start | bytes 393224 | tf_op jit(solution)/shard_map/ppermute | solution.py:322
  80.1 11.0 %collective-permute-start.15 = (bf16[32,2048]{1,0:T(8,128)(2,1)S(1)}, bf16[32,2048]{1,0:T(8,128)(2,1)S(1)}, u32[]{:S(2)}, u32[]{:S(2)}) collective-permute-start(bf16[32,2048]{1,0:T(8,128)(2,1)S(1)} %get-tuple-element.75), channel_id=1, source_target_pairs={{0,2},{2,0},{1,3},{3,1},{4,6},{6,4},{5,7},{7,5},{8,10},{10,8},{9,1... | collective-permute-start | bytes 393224 | tf_op jit(solution)/shard_map/ppermute | solution.py:322
  82.7 14.4 %collective-permute-start.18 = (bf16[32,2048]{1,0:T(8,128)(2,1)S(1)}, bf16[32,2048]{1,0:T(8,128)(2,1)S(1)}, u32[]{:S(2)}, u32[]{:S(2)}) collective-permute-start(bf16[32,2048]{1,0:T(8,128)(2,1)S(1)} %collective-permute-done.14), channel_id=1, source_target_pairs={{0,2},{2,0},{1,3},{3,1},{4,6},{6,4},{5,7},{7,5},{8,10},{10,8},{9,1... | collective-permute-start | bytes 393224 | tf_op jit(solution)/shard_map/ppermute | solution.py:322
  89.6 7.5 %collective-permute-start.17 = (bf16[32,2048]{1,0:T(8,128)(2,1)S(1)}, bf16[32,2048]{1,0:T(8,128)(2,1)S(1)}, u32[]{:S(2)}, u32[]{:S(2)}) collective-permute-start(bf16[32,2048]{1,0:T(8,128)(2,1)S(1)} %collective-permute-done.13), channel_id=1, source_target_pairs={{0,2},{2,0},{1,3},{3,1},{4,6},{6,4},{5,7},{7,5},{8,10},{10,8},{9,1... | collective-permute-start | bytes 393224 | tf_op jit(solution)/shard_map/ppermute | solution.py:322
  90.8 6.3 %collective-permute-start.16 = (bf16[32,2048]{1,0:T(8,128)(2,1)S(1)}, bf16[32,2048]{1,0:T(8,128)(2,1)S(1)}, u32[]{:S(2)}, u32[]{:S(2)}) collective-permute-start(bf16[32,2048]{1,0:T(8,128)(2,1)S(1)} %collective-permute-done.12), channel_id=1, source_target_pairs={{0,2},{2,0},{1,3},{3,1},{4,6},{6,4},{5,7},{7,5},{8,10},{10,8},{9,1... | collective-permute-start | bytes 393224 | tf_op jit(solution)/shard_map/ppermute | solution.py:322
  102.4 10.1 %copy-start.1 = (f32[256,4096]{1,0:T(8,128)S(1)}, f32[256,4096]{1,0:T(8,128)}, u32[]{:S(2)}) copy-start(f32[256,4096]{1,0:T(8,128)} %get-tuple-element.68.refs_2_) | copy-start | bytes 12582916
  102.5 10.1 %collective-permute-start.19 = (bf16[256,4096]{1,0:T(8,128)(2,1)S(1)}, bf16[256,4096]{1,0:T(8,128)(2,1)S(1)}, u32[]{:S(2)}, u32[]{:S(2)}) collective-permute-start(bf16[256,4096]{1,0:T(8,128)(2,1)S(1)} %back.1.refs_0_), channel_id=1, source_target_pairs={{0,1},{1,0},{2,3},{3,2},{4,5},{5,4},{6,7},{7,6},{8,9},{9,8},{10,11... | collective-permute-start | bytes 6291464 | tf_op jit(solution)/shard_map/ppermute | solution.py:335
  112.5 9.1 %copy-start = (f32[256,4096]{1,0:T(8,128)S(1)}, f32[256,4096]{1,0:T(8,128)}, u32[]{:S(2)}) copy-start(f32[256,4096]{1,0:T(8,128)} %get-tuple-element.66.refs_2_) | copy-start | bytes 12582916

commit v9 on v8

--- a/solution.py
+++ b/solution.py
@@ -87,7 +87,7 @@
 
 
 def place(tiles, table, n_rows, n_cols):
-    rows_per_step = max(1, 128 // n_cols)
+    rows_per_step = min(n_rows, max(1, 256 // n_cols))
     return pl.pallas_call(
         functools.partial(place_kernel, rows_per_step, n_cols),
         grid_spec=pltpu.PrefetchScalarGridSpec(

time: 131 us -> 131 us (level)
  no operation moved by 1% of the time
where the time goes in v9:
time: 131 us; the launch traced here: 130 us
  Pallas kernels  70.9 us (54%)
  starting transfers between devices  22.9 us (17%)
  waiting for transfers between devices  15 us (11%)
  other arithmetic  13.7 us (10%)
  matrix products  4.71 us (4%)
  local copies, waits for them, and re-layouts  2.17 us (2%)
    pallas_call x3, Pallas kernels, gradient(): pl.pallas_call(functools.partial(gradient_kernel, n_steps, rows_per_step,...  26.9 us
    ppermute x17, starting transfers between devices, shift(): lax.ppermute(values, axis, [(i, i ^ k) for i in range(n)])  19 us
    pallas_call x3, Pallas kernels, place(): pl.pallas_call(functools.partial(place_kernel, rows_per_step, n_cols), gr...  18.3 us
    ppermute x17, waiting for transfers between devices, shift(): lax.ppermute(values, axis, [(i, i ^ k) for i in range(n)])  15 us
    pallas_call x3, Pallas kernels, staged(): pl.pallas_call(functools.partial(stage_kernel, half_cap, chunks), in_spec...  10.1 us
    mul x1, other arithmetic, local(): gate_factor = up * sigmoid_gate * (1.0 + gate * (1.0 - sigmoid_gate))  6.39 us
    pallas_call x1, Pallas kernels, forward_product(): pl.pallas_call(forward_kernel, grid=(width // part,), in_specs=[pl.BlockS...  6.23 us
    pallas_call x1, Pallas kernels, back_product(): pl.pallas_call(back_kernel, grid=(width // part,), in_specs=[pl.BlockSpec...  5.26 us
  transfers between devices with their start and end apart: 20, of which 4 were waited for; matrix products, arithmetic and copies ran while one was open for 16% of the time, Pallas kernels for 29%

profile of v9, /device:TPU:1, one launch (start us, length us, event | category | flops | bytes accessed | tf_op | source)
XLA Modules:
  0.0 130.4 jit_solution(8149449526923890653)
XLA Ops:
  0.6 3.2 %collective-permute-start.1 = (bf16[32,2048]{1,0:T(8,128)(2,1)}, bf16[32,2048]{1,0:T(8,128)(2,1)S(1)}, u32[]{:S(2)}, u32[]{:S(2)}) collective-permute-start(bf16[32,2048]{1,0:T(8,128)(2,1)} %param.8), channel_id=1, source_target_pairs={{0,8},{4,12},{8,0},{12,4},{1,9},{5,13},{9,1},{13,5},{2,10},{6,14},... | collective-permute-start | bytes 393224 | tf_op jit(solution)/shard_map/ppermute | solution.py:322
  3.8 1.3 collective-permute-start
  8.9 2.0 %select_reduce_fusion = (s32[2048]{0:T(1024)S(1)}, s32[2048]{0:T(1024)S(1)}, s32[2048]{0:T(1024)S(1)}) fusion(s32[640]{0:T(1024)S(1)} %reduce.2, s32[640]{0:T(1024)S(1)} %iota_add_fusion, s32[640]{0:T(1024)S(1)} %reduce.1, s32[640]{0:T(1024)S(1)} %reduce), kind=kLoop, calls=%fused_computation | loop fusion | flops 11790336 | bytes 34816 | tf_op jit(solution)/shard_map/reduce_sum | solution.py:297
  11.4 3.4 %stage.3.tiles = bf16[64,82048]{1,0:T(8,128)(2,1)S(1)} custom-call(bf16[64,40960]{1,0:T(8,128)(2,1)} %bitcast.26), custom_call_target="tpu_custom_call" | custom-call | bytes 15728640 | tf_op jit(solution)/shard_map/stage/pallas_call | solution.py:63
  14.9 1.3 collective-permute-start.3
  16.5 1.2 collective-permute-start.5
  18.0 6.0 %place.3.weights = bf16[2048,4096]{1,0:T(8,128)(2,1)S(1)} custom-call(s32[2048]{0:T(1024)S(1)} %get-tuple-element.43.table, bf16[64,82048]{1,0:T(8,128)(2,1)S(1)} %stage.3.tiles), custom_call_target="tpu_custom_call" | custom-call | bytes 44056576 | tf_op jit(solution)/shard_map/place/pallas_call | solution.py:91
  24.0 3.4 %stage.4.tiles = bf16[64,82048]{1,0:T(8,128)(2,1)S(1)} custom-call(bf16[64,40960]{1,0:T(8,128)(2,1)} %bitcast.27), custom_call_target="tpu_custom_call" | custom-call | bytes 15728640 | tf_op jit(solution)/shard_map/stage/pallas_call | solution.py:63
  27.5 6.2 %forward.1.gate_mine = bf16[256,4096]{1,0:T(8,128)(2,1)S(1)} custom-call(bf16[256,2048]{1,0:T(8,128)(2,1)S(1)} %constant_dynamic-update-slice_fusion.rows.lhs, bf16[2048,4096]{1,0:T(8,128)(2,1)S(1)} %place.3.weights), custom_call_target="tpu_custom_call" | custom-call | flops 4294967296 | bytes 19922944 | tf_op jit(solution)/shard_map/forward/pallas_call | solution.py:245
  33.7 2.4 %collective-permute-start.7 = (bf16[256,4096]{1,0:T(8,128)(2,1)S(1)}, bf16[256,4096]{1,0:T(8,128)(2,1)S(1)}, u32[]{:S(2)}, u32[]{:S(2)}) collective-permute-start(bf16[256,4096]{1,0:T(8,128)(2,1)S(1)} %forward.1.gate_mine), channel_id=1, source_target_pairs={{0,1},{1,0},{2,3},{3,2},{4,5},{5,4},{6,7},{7,6},{8,9},{9,8},{10,11... | collective-permute-start | bytes 6291464 | tf_op jit(solution)/shard_map/ppermute | solution.py:335
  36.2 6.0 %place.4 = bf16[2048,4096]{1,0:T(8,128)(2,1)S(1)} custom-call(s32[2048]{0:T(1024)S(1)} %get-tuple-element.50.table, bf16[64,82048]{1,0:T(8,128)(2,1)S(1)} %stage.4.tiles), custom_call_target="tpu_custom_call" | custom-call | bytes 44056576 | tf_op jit(solution)/shard_map/place/pallas_call | solution.py:91
  42.2 4.7 %convolution_convert_fusion.up_mine = bf16[256,4096]{1,0:T(8,128)(2,1)S(1)} fusion(bf16[256,2048]{1,0:T(8,128)(2,1)S(1)} %constant_dynamic-update-slice_fusion.rows.lhs, bf16[2048,4096]{1,0:T(8,128)(2,1)S(1)} %place.4), kind=kOutput, calls=%fused_computation.6 | convolution fusion | flops 4296015872 | bytes 19922944 | tf_op jit(solution)/shard_map/dot_general | solution.py:382
  47.0 3.4 %stage.5.tiles = bf16[64,82048]{1,0:T(8,128)(2,1)S(1)} custom-call(bf16[64,40960]{1,0:T(8,128)(2,1)} %bitcast.28), custom_call_target="tpu_custom_call" | custom-call | bytes 15728640 | tf_op jit(solution)/shard_map/stage/pallas_call | solution.py:63
  50.4 6.3 %place.5.weights = bf16[4096,2048]{1,0:T(8,128)(2,1)S(1)} custom-call(s32[2048]{0:T(1024)S(1)} %reshape.60.table, bf16[64,82048]{1,0:T(8,128)(2,1)S(1)} %stage.5.tiles), custom_call_target="tpu_custom_call" | custom-call | bytes 44056576 | tf_op jit(solution)/shard_map/place/pallas_call | solution.py:91
  56.7 4.1 %output.1 = (bf16[128,4096]{1,0:T(8,128)(2,1)S(1)}, bf16[128,2048]{1,0:T(8,128)(2,1)S(1)}) custom-call(bf16[256,4096]{1,0:T(8,128)(2,1)S(1)} %forward.1.gate_mine, bf16[256,4096]{1,0:T(8,128)(2,1)S(1)} %collective-permute-done.7.gate_theirs, bf16[256,4096]{1,0:T(8,128)(2,1)S(1)} %convolution_convert_fusion.up_mine, ...), custom_call_target="tpu_custom_call" | custom-call | flops 2147483648 | bytes 22544384 | tf_op jit(solution)/shard_map/output/pallas_call | solution.py:214
  60.8 3.6 %collective-permute-start.11 = (bf16[32,2048]{1,0:T(8,128)(2,1)S(1)}, bf16[32,2048]{1,0:T(8,128)(2,1)S(1)}, u32[]{:S(2)}, u32[]{:S(2)}) collective-permute-start(bf16[32,2048]{1,0:T(8,128)(2,1)S(1)} %get-tuple-element.80), channel_id=1, source_target_pairs={{0,12},{4,8},{8,4},{12,0},{1,13},{5,9},{9,5},{13,1},{2,14},{6,10},... | collective-permute-start | bytes 393224 | tf_op jit(solution)/shard_map/ppermute | solution.py:322
  64.8 6.4 %add_multiply_fusion = (f32[256,4096]{1,0:T(8,128)}, f32[256,4096]{1,0:T(8,128)}, f32[256,4096]{1,0:T(8,128)}, f32[256,4096]{1,0:T(8,128)}) fusion(bf16[256,4096]{1,0:T(8,128)(2,1)S(1)} %collective-permute-done.8.up_theirs, bf16[256,4096]{1,0:T(8,128)(2,1)S(1)} %convolution_convert_fusion.up_mine, ...), kind=kLoop, calls=%fused_computation.7 | loop fusion | flops 15728640 | bytes 25165824 | tf_op jit(solution)/shard_map/mul | solution.py:398
  71.1 2.8 %fusion.1 = bf16[128,4096]{1,0:T(8,128)(2,1)S(1)} fusion(f32[256,4096]{1,0:T(8,128)} %get-tuple-element.79, f32[256,4096]{1,0:T(8,128)} %get-tuple-element.78), kind=kLoop, calls=%fused_computation.13 | loop fusion | flops 3145728 | bytes 5242880 | tf_op jit(solution)/shard_map/convert_element_type | solution.py:347
  74.1 2.2 %collective-permute-done.10 = bf16[32,2048]{1,0:T(8,128)(2,1)S(1)} collective-permute-done((bf16[32,2048]{1,0:T(8,128)(2,1)S(1)}, bf16[32,2048]{1,0:T(8,128)(2,1)S(1)}, u32[]{:S(2)}, u32[]{:S(2)}) %collective-permute-start.10) | collective-permute-done | bytes 131104 | tf_op jit(solution)/shard_map/ppermute | solution.py:322
  76.4 1.8 %collective-permute-start.14 = (bf16[32,2048]{1,0:T(8,128)(2,1)S(1)}, bf16[32,2048]{1,0:T(8,128)(2,1)S(1)}, u32[]{:S(2)}, u32[]{:S(2)}) collective-permute-start(bf16[32,2048]{1,0:T(8,128)(2,1)S(1)} %get-tuple-element.75), channel_id=1, source_target_pairs={{0,12},{4,8},{8,4},{12,0},{1,13},{5,9},{9,5},{13,1},{2,14},{6,10},... | collective-permute-start | bytes 393224 | tf_op jit(solution)/shard_map/ppermute | solution.py:322
  78.2 1.8 %collective-permute-start.12 = (bf16[32,2048]{1,0:T(8,128)(2,1)S(1)}, bf16[32,2048]{1,0:T(8,128)(2,1)S(1)}, u32[]{:S(2)}, u32[]{:S(2)}) collective-permute-start(bf16[32,2048]{1,0:T(8,128)(2,1)S(1)} %get-tuple-element.75), channel_id=1, source_target_pairs={{0,4},{4,0},{8,12},{12,8},{1,5},{5,1},{9,13},{13,9},{2,6},{6,2},{1... | collective-permute-start | bytes 393224 | tf_op jit(solution)/shard_map/ppermute | solution.py:322
  80.0 1.2 collective-permute-start.15
  81.3 1.4 %collective-permute-done.14 = bf16[32,2048]{1,0:T(8,128)(2,1)S(1)} collective-permute-done((bf16[32,2048]{1,0:T(8,128)(2,1)S(1)}, bf16[32,2048]{1,0:T(8,128)(2,1)S(1)}, u32[]{:S(2)}, u32[]{:S(2)}) %collective-permute-start.14) | collective-permute-done | bytes 131104 | tf_op jit(solution)/shard_map/ppermute | solution.py:322
  82.6 1.2 collective-permute-start.18
  83.8 5.5 %collective-permute-done.13 = bf16[32,2048]{1,0:T(8,128)(2,1)S(1)} collective-permute-done((bf16[32,2048]{1,0:T(8,128)(2,1)S(1)}, bf16[32,2048]{1,0:T(8,128)(2,1)S(1)}, u32[]{:S(2)}, u32[]{:S(2)}) %collective-permute-start.13) | collective-permute-done | bytes 131104 | tf_op jit(solution)/shard_map/ppermute | solution.py:322
  89.4 1.2 collective-permute-start.17
  90.9 5.8 %collective-permute-done.16 = bf16[32,2048]{1,0:T(8,128)(2,1)S(1)} collective-permute-done((bf16[32,2048]{1,0:T(8,128)(2,1)S(1)}, bf16[32,2048]{1,0:T(8,128)(2,1)S(1)}, u32[]{:S(2)}, u32[]{:S(2)}) %collective-permute-start.16) | collective-permute-done | bytes 131104 | tf_op jit(solution)/shard_map/ppermute | solution.py:322
  96.8 5.3 %back.1.refs_0_ = bf16[256,4096]{1,0:T(8,128)(2,1)S(1)} custom-call(bf16[256,2048]{1,0:T(8,128)(2,1)S(1)} %constant_dynamic-update-slice_fusion.8.slope.refs_0_, bf16[4096,2048]{1,0:T(8,128)(2,1)S(1)} %place.5.weights), custom_call_target="tpu_custom_call" | custom-call | flops 4294967296 | bytes 19922944 | tf_op jit(solution)/shard_map/back/pallas_call | solution.py:274
  102.1 1.4 %collective-permute-start.19 = (bf16[256,4096]{1,0:T(8,128)(2,1)S(1)}, bf16[256,4096]{1,0:T(8,128)(2,1)S(1)}, u32[]{:S(2)}, u32[]{:S(2)}) collective-permute-start(bf16[256,4096]{1,0:T(8,128)(2,1)S(1)} %back.1.refs_0_), channel_id=1, source_target_pairs={{0,1},{1,0},{2,3},{3,2},{4,5},{5,4},{6,7},{7,6},{8,9},{9,8},{10,11... | collective-permute-start | bytes 6291464 | tf_op jit(solution)/shard_map/ppermute | solution.py:335
  103.5 8.8 %gradient.5 = bf16[64,20480]{1,0:T(8,128)(2,1)} custom-call(s32[320]{0:T(512)S(1)} %fusion.34.picks, bf16[256,4096]{1,0:T(8,128)(2,1)S(1)} %pad_maximum_fusion.lhs, bf16[256,2048]{1,0:T(8,128)(2,1)S(1)} %constant_dynamic-update-slice_fusion.8.slope.refs_0_), custom_call_target="tpu_custom_call" | custom-call | flops 4294967296 | bytes 6815744 | tf_op jit(solution)/shard_map/gradient/pallas_call | solution.py:172
  112.3 9.1 %gradient.4 = bf16[64,20480]{1,0:T(8,128)(2,1)} custom-call(s32[320]{0:T(512)S(1)} %fusion.28.picks, bf16[256,2048]{1,0:T(8,128)(2,1)S(1)} %constant_dynamic-update-slice_fusion.rows.lhs, bf16[256,4096]{1,0:T(8,128)(2,1)S(1)} %back.1.refs_0_, bf16[256,4096]{1,0:T(8,128)(2,1)S(1)} %collective-permute-done.19.refs_1_, f32[256,4096]{1,0:T(8,128)S(1)} %copy-done.1), custom_call_target="tpu_custom_call" | custom-call | flops 4294967296 | bytes 16252928 | tf_op jit(solution)/shard_map/gradient/pallas_call | solution.py:172
  121.3 9.1 %gradient.3 = bf16[64,20480]{1,0:T(8,128)(2,1)} custom-call(s32[320]{0:T(512)S(1)} %fusion.22.picks, bf16[256,2048]{1,0:T(8,128)(2,1)S(1)} %constant_dynamic-update-slice_fusion.rows.lhs, bf16[256,4096]{1,0:T(8,128)(2,1)S(1)} %back.1.refs_0_, bf16[256,4096]{1,0:T(8,128)(2,1)S(1)} %collective-permute-done.19.refs_1_, f32[256,4096]{1,0:T(8,128)S(1)} %copy-done), custom_call_target="tpu_custom_call" | custom-call | flops 4294967296 | bytes 16252928 | tf_op jit(solution)/shard_map/gradient/pallas_call | solution.py:172
  (70 shorter events, 6.0 us)
Async XLA Ops:
  0.6 14.2 %collective-permute-start.1 = (bf16[32,2048]{1,0:T(8,128)(2,1)}, bf16[32,2048]{1,0:T(8,128)(2,1)S(1)}, u32[]{:S(2)}, u32[]{:S(2)}) collective-permute-start(bf16[32,2048]{1,0:T(8,128)(2,1)} %param.8), channel_id=1, source_target_pairs={{0,8},{4,12},{8,0},{12,4},{1,9},{5,13},{9,1},{13,5},{2,10},{6,14},... | collective-permute-start | bytes 393224 | tf_op jit(solution)/shard_map/ppermute | solution.py:322
  3.8 11.0 %collective-permute-start = (bf16[32,2048]{1,0:T(8,128)(2,1)}, bf16[32,2048]{1,0:T(8,128)(2,1)S(1)}, u32[]{:S(2)}, u32[]{:S(2)}) collective-permute-start(bf16[32,2048]{1,0:T(8,128)(2,1)} %param.8), channel_id=1, source_target_pairs={{0,4},{4,0},{8,12},{12,8},{1,5},{5,1},{9,13},{13,9},{2,6},{6,2},{1... | collective-permute-start | bytes 393224 | tf_op jit(solution)/shard_map/ppermute | solution.py:322
  5.1 9.7 %collective-permute-start.2 = (bf16[32,2048]{1,0:T(8,128)(2,1)}, bf16[32,2048]{1,0:T(8,128)(2,1)S(1)}, u32[]{:S(2)}, u32[]{:S(2)}) collective-permute-start(bf16[32,2048]{1,0:T(8,128)(2,1)} %param.8), channel_id=1, source_target_pairs={{0,12},{4,8},{8,4},{12,0},{1,13},{5,9},{9,5},{13,1},{2,14},{6,10},... | collective-permute-start | bytes 393224 | tf_op jit(solution)/shard_map/ppermute | solution.py:322
  11.4 3.5 %copy-start.3 = (bf16[32,2048]{1,0:T(8,128)(2,1)S(1)}, bf16[32,2048]{1,0:T(8,128)(2,1)}, u32[]{:S(2)}) copy-start(bf16[32,2048]{1,0:T(8,128)(2,1)} %param.8) | copy-start | bytes 393220
  14.9 12.5 %collective-permute-start.3 = (bf16[32,2048]{1,0:T(8,128)(2,1)S(1)}, bf16[32,2048]{1,0:T(8,128)(2,1)S(1)}, u32[]{:S(2)}, u32[]{:S(2)}) collective-permute-start(bf16[32,2048]{1,0:T(8,128)(2,1)S(1)} %copy-done.3), channel_id=1, source_target_pairs={{0,2},{2,0},{1,3},{3,1},{4,6},{6,4},{5,7},{7,5},{8,10},{10,8},{9,1... | collective-permute-start | bytes 393224 | tf_op jit(solution)/shard_map/ppermute | solution.py:322
  16.1 11.3 %collective-permute-start.4 = (bf16[32,2048]{1,0:T(8,128)(2,1)S(1)}, bf16[32,2048]{1,0:T(8,128)(2,1)S(1)}, u32[]{:S(2)}, u32[]{:S(2)}) collective-permute-start(bf16[32,2048]{1,0:T(8,128)(2,1)S(1)} %collective-permute-done), channel_id=1, source_target_pairs={{0,2},{2,0},{1,3},{3,1},{4,6},{6,4},{5,7},{7,5},{8,10},{10,8},{9,1... | collective-permute-start | bytes 393224 | tf_op jit(solution)/shard_map/ppermute | solution.py:322
  16.5 11.0 %collective-permute-start.5 = (bf16[32,2048]{1,0:T(8,128)(2,1)S(1)}, bf16[32,2048]{1,0:T(8,128)(2,1)S(1)}, u32[]{:S(2)}, u32[]{:S(2)}) collective-permute-start(bf16[32,2048]{1,0:T(8,128)(2,1)S(1)} %collective-permute-done.1), channel_id=1, source_target_pairs={{0,2},{2,0},{1,3},{3,1},{4,6},{6,4},{5,7},{7,5},{8,10},{10,8},{9,1... | collective-permute-start | bytes 393224 | tf_op jit(solution)/shard_map/ppermute | solution.py:322
  17.7 9.8 %collective-permute-start.6 = (bf16[32,2048]{1,0:T(8,128)(2,1)S(1)}, bf16[32,2048]{1,0:T(8,128)(2,1)S(1)}, u32[]{:S(2)}, u32[]{:S(2)}) collective-permute-start(bf16[32,2048]{1,0:T(8,128)(2,1)S(1)} %collective-permute-done.2), channel_id=1, source_target_pairs={{0,2},{2,0},{1,3},{3,1},{4,6},{6,4},{5,7},{7,5},{8,10},{10,8},{9,1... | collective-permute-start | bytes 393224 | tf_op jit(solution)/shard_map/ppermute | solution.py:322
  33.7 22.9 %collective-permute-start.7 = (bf16[256,4096]{1,0:T(8,128)(2,1)S(1)}, bf16[256,4096]{1,0:T(8,128)(2,1)S(1)}, u32[]{:S(2)}, u32[]{:S(2)}) collective-permute-start(bf16[256,4096]{1,0:T(8,128)(2,1)S(1)} %forward.1.gate_mine), channel_id=1, source_target_pairs={{0,1},{1,0},{2,3},{3,2},{4,5},{5,4},{6,7},{7,6},{8,9},{9,8},{10,11... | collective-permute-start | bytes 6291464 | tf_op jit(solution)/shard_map/ppermute | solution.py:335
  46.9 9.7 %collective-permute-start.8 = (bf16[256,4096]{1,0:T(8,128)(2,1)S(1)}, bf16[256,4096]{1,0:T(8,128)(2,1)S(1)}, u32[]{:S(2)}, u32[]{:S(2)}) collective-permute-start(bf16[256,4096]{1,0:T(8,128)(2,1)S(1)} %convolution_convert_fusion.up_mine), channel_id=1, source_target_pairs={{0,1},{1,0},{2,3},{3,2},{4,5},{5,4},{6,7},{7,6},{8,9},{9,8},{10,11... | collective-permute-start | bytes 6291464 | tf_op jit(solution)/shard_map/ppermute | solution.py:335
  60.8 13.3 %collective-permute-start.11 = (bf16[32,2048]{1,0:T(8,128)(2,1)S(1)}, bf16[32,2048]{1,0:T(8,128)(2,1)S(1)}, u32[]{:S(2)}, u32[]{:S(2)}) collective-permute-start(bf16[32,2048]{1,0:T(8,128)(2,1)S(1)} %get-tuple-element.80), channel_id=1, source_target_pairs={{0,12},{4,8},{8,4},{12,0},{1,13},{5,9},{9,5},{13,1},{2,14},{6,10},... | collective-permute-start | bytes 393224 | tf_op jit(solution)/shard_map/ppermute | solution.py:322
  64.4 11.9 %collective-permute-start.10 = (bf16[32,2048]{1,0:T(8,128)(2,1)S(1)}, bf16[32,2048]{1,0:T(8,128)(2,1)S(1)}, u32[]{:S(2)}, u32[]{:S(2)}) collective-permute-start(bf16[32,2048]{1,0:T(8,128)(2,1)S(1)} %get-tuple-element.81), channel_id=1, source_target_pairs={{0,8},{4,12},{8,0},{12,4},{1,9},{5,13},{9,1},{13,5},{2,10},{6,14},... | collective-permute-start | bytes 393224 | tf_op jit(solution)/shard_map/ppermute | solution.py:322
  64.4 11.9 %collective-permute-start.9 = (bf16[32,2048]{1,0:T(8,128)(2,1)S(1)}, bf16[32,2048]{1,0:T(8,128)(2,1)S(1)}, u32[]{:S(2)}, u32[]{:S(2)}) collective-permute-start(bf16[32,2048]{1,0:T(8,128)(2,1)S(1)} %get-tuple-element.82), channel_id=1, source_target_pairs={{0,4},{4,0},{8,12},{12,8},{1,5},{5,1},{9,13},{13,9},{2,6},{6,2},{1... | collective-permute-start | bytes 393224 | tf_op jit(solution)/shard_map/ppermute | solution.py:322
  71.1 5.2 %copy-start.2 = (bf16[32,2048]{1,0:T(8,128)(2,1)S(1)}, bf16[32,2048]{1,0:T(8,128)(2,1)}, u32[]{:S(2)}) copy-start(bf16[32,2048]{1,0:T(8,128)(2,1)} %param.9) | copy-start | bytes 393220
  76.4 6.2 %collective-permute-start.14 = (bf16[32,2048]{1,0:T(8,128)(2,1)S(1)}, bf16[32,2048]{1,0:T(8,128)(2,1)S(1)}, u32[]{:S(2)}, u32[]{:S(2)}) collective-permute-start(bf16[32,2048]{1,0:T(8,128)(2,1)S(1)} %get-tuple-element.75), channel_id=1, source_target_pairs={{0,12},{4,8},{8,4},{12,0},{1,13},{5,9},{9,5},{13,1},{2,14},{6,10},... | collective-permute-start | bytes 393224 | tf_op jit(solution)/shard_map/ppermute | solution.py:322
  78.2 11.1 %collective-permute-start.13 = (bf16[32,2048]{1,0:T(8,128)(2,1)S(1)}, bf16[32,2048]{1,0:T(8,128)(2,1)S(1)}, u32[]{:S(2)}, u32[]{:S(2)}) collective-permute-start(bf16[32,2048]{1,0:T(8,128)(2,1)S(1)} %get-tuple-element.75), channel_id=1, source_target_pairs={{0,8},{4,12},{8,0},{12,4},{1,9},{5,13},{9,1},{13,5},{2,10},{6,14},... | collective-permute-start | bytes 393224 | tf_op jit(solution)/shard_map/ppermute | solution.py:322
  78.2 12.4 %collective-permute-start.12 = (bf16[32,2048]{1,0:T(8,128)(2,1)S(1)}, bf16[32,2048]{1,0:T(8,128)(2,1)S(1)}, u32[]{:S(2)}, u32[]{:S(2)}) collective-permute-start(bf16[32,2048]{1,0:T(8,128)(2,1)S(1)} %get-tuple-element.75), channel_id=1, source_target_pairs={{0,4},{4,0},{8,12},{12,8},{1,5},{5,1},{9,13},{13,9},{2,6},{6,2},{1... | collective-permute-start | bytes 393224 | tf_op jit(solution)/shard_map/ppermute | solution.py:322
  80.0 10.8 %collective-permute-start.15 = (bf16[32,2048]{1,0:T(8,128)(2,1)S(1)}, bf16[32,2048]{1,0:T(8,128)(2,1)S(1)}, u32[]{:S(2)}, u32[]{:S(2)}) collective-permute-start(bf16[32,2048]{1,0:T(8,128)(2,1)S(1)} %get-tuple-element.75), channel_id=1, source_target_pairs={{0,2},{2,0},{1,3},{3,1},{4,6},{6,4},{5,7},{7,5},{8,10},{10,8},{9,1... | collective-permute-start | bytes 393224 | tf_op jit(solution)/shard_map/ppermute | solution.py:322
  82.6 14.2 %collective-permute-start.18 = (bf16[32,2048]{1,0:T(8,128)(2,1)S(1)}, bf16[32,2048]{1,0:T(8,128)(2,1)S(1)}, u32[]{:S(2)}, u32[]{:S(2)}) collective-permute-start(bf16[32,2048]{1,0:T(8,128)(2,1)S(1)} %collective-permute-done.14), channel_id=1, source_target_pairs={{0,2},{2,0},{1,3},{3,1},{4,6},{6,4},{5,7},{7,5},{8,10},{10,8},{9,1... | collective-permute-start | bytes 393224 | tf_op jit(solution)/shard_map/ppermute | solution.py:322
  89.4 7.4 %collective-permute-start.17 = (bf16[32,2048]{1,0:T(8,128)(2,1)S(1)}, bf16[32,2048]{1,0:T(8,128)(2,1)S(1)}, u32[]{:S(2)}, u32[]{:S(2)}) collective-permute-start(bf16[32,2048]{1,0:T(8,128)(2,1)S(1)} %collective-permute-done.13), channel_id=1, source_target_pairs={{0,2},{2,0},{1,3},{3,1},{4,6},{6,4},{5,7},{7,5},{8,10},{10,8},{9,1... | collective-permute-start | bytes 393224 | tf_op jit(solution)/shard_map/ppermute | solution.py:322
  90.6 6.2 %collective-permute-start.16 = (bf16[32,2048]{1,0:T(8,128)(2,1)S(1)}, bf16[32,2048]{1,0:T(8,128)(2,1)S(1)}, u32[]{:S(2)}, u32[]{:S(2)}) collective-permute-start(bf16[32,2048]{1,0:T(8,128)(2,1)S(1)} %collective-permute-done.12), channel_id=1, source_target_pairs={{0,2},{2,0},{1,3},{3,1},{4,6},{6,4},{5,7},{7,5},{8,10},{10,8},{9,1... | collective-permute-start | bytes 393224 | tf_op jit(solution)/shard_map/ppermute | solution.py:322
  102.1 10.2 %copy-start.1 = (f32[256,4096]{1,0:T(8,128)S(1)}, f32[256,4096]{1,0:T(8,128)}, u32[]{:S(2)}) copy-start(f32[256,4096]{1,0:T(8,128)} %get-tuple-element.68.refs_2_) | copy-start | bytes 12582916
  102.1 10.2 %collective-permute-start.19 = (bf16[256,4096]{1,0:T(8,128)(2,1)S(1)}, bf16[256,4096]{1,0:T(8,128)(2,1)S(1)}, u32[]{:S(2)}, u32[]{:S(2)}) collective-permute-start(bf16[256,4096]{1,0:T(8,128)(2,1)S(1)} %back.1.refs_0_), channel_id=1, source_target_pairs={{0,1},{1,0},{2,3},{3,2},{4,5},{5,4},{6,7},{7,6},{8,9},{9,8},{10,11... | collective-permute-start | bytes 6291464 | tf_op jit(solution)/shard_map/ppermute | solution.py:335
  112.3 9.1 %copy-start = (f32[256,4096]{1,0:T(8,128)S(1)}, f32[256,4096]{1,0:T(8,128)}, u32[]{:S(2)}) copy-start(f32[256,4096]{1,0:T(8,128)} %get-tuple-element.66.refs_2_) | copy-start | bytes 12582916
